TPU v7x, 256 devices: a whole 4x4x8 slice. The times are simulated.
256 devices in a mesh: rows: 64 (over z, y, core), section: 4 (over x).
Axes of the slice: x: 4, y: 4, z: 8, core: 2. Of those that a mesh axis runs over, the one named last changes fastest.
Arguments:
- block_out: bfloat16 [4, 64, 128, 512], P('section', 'rows'), may hold values from -6 to 6
- out_grad: bfloat16 [4, 64, 128, 512], P('section', 'rows'), may hold values from -6 to 6
- weights: bfloat16 [4, 2, 2304, 256], P('section'), may hold values from -0.125 to 0.125
Outputs:
- restored: bfloat16 [4, 64, 128, 512], P('section', 'rows')
- input_grad: bfloat16 [4, 64, 128, 512], P('section', 'rows')
- weight_grad: float32 [4, 2, 2304, 256], P('section', None, 'rows')
All inputs are finite; a program needn't handle non-finite values.
Results may differ from a plain program's by a relative error of at most 0.025.
Values may be sent and summed in bfloat16 or wider, within the bound.
No kernel may reach another device: no remote copies, remote signals or barrier semaphores. Data moves between devices by JAX's collectives and lax.ppermute only.
A program may use at most 128 MiB of HBM per device.

v0:
```python
import math

import jax
import jax.numpy as jnp
from jax import lax
from jax.sharding import PartitionSpec as P


def extended(value, sides, width):
    for axis, dim in sides:
        peers, length = (lax.axis_size(axis), value.shape[dim])
        up = [(i, (i + 1) % peers) for i in range(peers - 1)]
        down = [(j, i) for i, j in up]
        last = lax.slice_in_dim(value, length - width, length, axis=dim)
        initial = lax.slice_in_dim(value, 0, width, axis=dim)
        before = lax.ppermute(last, axis, up)
        after = lax.ppermute(initial, axis, down)
        value = jnp.concatenate([before, value, after], axis=dim)
    return value


def from_behind(value, axis, by):
    peers = lax.axis_size(axis)
    pairs = [(i, i + by) for i in range(peers) if 0 <= i + by < peers]
    return lax.ppermute(value, axis, pairs)


def broadcast(block, axis, holder):
    block = jnp.where(lax.axis_index(axis) == holder, block, jnp.zeros_like(block))
    return lax.psum(block, axis)


def column_pad(field):
    return jnp.pad(field, ((0, 0), (1, 1), (0, 0)))


def band_extend(field):
    return extended(field, (("rows", 0),), 1)


def stencil_taps(padded, height, across, flipped):
    pieces = []
    for row_off in range(3):
        for col_off in range(3):
            row_start = 2 - row_off if flipped else row_off
            col_start = 2 - col_off if flipped else col_off
            pieces.append(padded[row_start : row_start + height, col_start : col_start + across])
    return jnp.concatenate(pieces, axis=-1).reshape(height * across, -1)


def turned_weight(weight):
    channels = weight.shape[1]
    return weight.reshape(9, channels, channels).transpose(0, 2, 1).reshape(9 * channels, channels)


def silu_slope(pre_value, sig_value):
    return sig_value * (1.0 + pre_value * (1.0 - sig_value))


def block_backward(field, cotangent, weight_f, weight_g, extend):
    height, across, width = field.shape
    half = width // 2
    first = field[..., :half]
    second = field[..., half:]
    grad_first = cotangent[..., :half].reshape(-1, half).astype(jnp.float32)
    grad_second = cotangent[..., half:].reshape(-1, half).astype(jnp.float32)
    taps_first = stencil_taps(column_pad(extend(first)), height, across, False)
    pre_g = jnp.dot(taps_first, weight_g, preferred_element_type=jnp.float32)
    sig_g = jax.nn.sigmoid(pre_g)
    input_second = (second.reshape(-1, half).astype(jnp.float32) - pre_g * sig_g).astype(
        jnp.bfloat16
    )
    taps_second = stencil_taps(
        column_pad(extend(input_second.reshape(height, across, half))), height, across, False
    )
    pre_f = jnp.dot(taps_second, weight_f, preferred_element_type=jnp.float32)
    sig_f = jax.nn.sigmoid(pre_f)
    input_first = (first.reshape(-1, half).astype(jnp.float32) - pre_f * sig_f).astype(jnp.bfloat16)
    delta_g = (grad_second * silu_slope(pre_g, sig_g)).astype(jnp.bfloat16)
    grad_wg = lax.dot_general(
        taps_first, delta_g, (((0,), (0,)), ((), ())), preferred_element_type=jnp.float32
    )
    taps_back_g = stencil_taps(
        column_pad(extend(delta_g.reshape(height, across, half))), height, across, True
    )
    back_g = jnp.dot(taps_back_g, turned_weight(weight_g), preferred_element_type=jnp.float32)
    total_first = (grad_first + back_g).astype(jnp.bfloat16)
    delta_f = (total_first.astype(jnp.float32) * silu_slope(pre_f, sig_f)).astype(jnp.bfloat16)
    grad_wf = lax.dot_general(
        taps_second, delta_f, (((0,), (0,)), ((), ())), preferred_element_type=jnp.float32
    )
    taps_back_f = stencil_taps(
        column_pad(extend(delta_f.reshape(height, across, half))), height, across, True
    )
    back_f = jnp.dot(taps_back_f, turned_weight(weight_f), preferred_element_type=jnp.float32)
    total_second = (grad_second + back_f).astype(jnp.bfloat16)
    restored = jnp.concatenate([input_first, input_second], axis=-1).reshape(height, across, width)
    grads_in = jnp.concatenate([total_first, total_second], axis=-1).reshape(height, across, width)
    return (restored, grads_in, grad_wf, grad_wg)


def local(block_out, out_grad, weights):
    sections = lax.axis_size("section")
    place = lax.axis_index("section")
    own = weights[0]
    own_pair = jnp.stack([block_out[0], out_grad[0]])
    every_out, every_grad = (
        lax.all_gather(block_out, "section", axis=0, tiled=True),
        lax.all_gather(out_grad, "section", axis=0, tiled=True),
    )
    state = jnp.zeros_like(own_pair)
    grad_f = jnp.zeros(own.shape[1:], jnp.float32)
    grad_g = jnp.zeros(own.shape[1:], jnp.float32)
    finished = []
    for tick in range(2 * sections - 1):
        if tick > 0:
            state = from_behind(state, "section", -1)
        if tick < sections:
            fresh = jnp.stack([every_out[tick], every_grad[tick]])
            state = jnp.where(place == sections - 1, fresh, state)
        micro = tick - (sections - 1 - place)
        valid = jnp.logical_and(micro >= 0, micro < sections)
        field, cotangent, grad_wf, grad_wg = block_backward(
            state[0], state[1], own[0], own[1], band_extend
        )
        grad_f = grad_f + jnp.where(valid, grad_wf, 0.0)
        grad_g = grad_g + jnp.where(valid, grad_wg, 0.0)
        state = jnp.stack([field, cotangent])
        if tick >= sections - 1:
            finished.append(state)
    every_done = broadcast(jnp.stack(finished), "section", 0)
    kept = lax.dynamic_index_in_dim(every_done, place, 0, keepdims=False)
    height, across = (kept.shape[1], kept.shape[2])
    scale = 1.0 / math.sqrt(sections * lax.axis_size("rows") * height * across)
    terms = jnp.stack([grad_f, grad_g])[None]
    summed = lax.psum_scatter(terms, "rows", scatter_dimension=2, tiled=True)
    return (kept[0][None], kept[1][None], summed * scale)


def solution(mesh):
    return jax.shard_map(
        local,
        mesh=mesh,
        in_specs=(
            P("section", "rows", None, None),
            P("section", "rows", None, None),
            P("section", None, None, None),
        ),
        out_specs=(
            P("section", "rows", None, None),
            P("section", "rows", None, None),
            P("section", None, "rows", None),
        ),
        check_vma=False,
    )
```

profile of v0, /device:TPU:1, one launch (start us, length us, event | category | flops | bytes accessed | tf_op | source)
XLA Modules:
  0.0 665.0 jit_solution(6496967165204172016)
XLA Ops:
  7.2 12.5 %all_gather.7 = bf16[4,1,128,512]{3,2,1,0:T(8,128)(2,1)S(1)} all-gather(bf16[1,1,128,512]{3,2,1,0:T(8,128)(2,1)} %param.4), channel_id=1, replica_groups=mesh['rows'=64,'section'=4] {'section'}, dimensions={0}, use_global_device_ids=true | all-gather | bytes 655360 | tf_op jit(solution)/shard_map/all_gather | solution.py:109
  20.5 11.0 %all_gather.6 = bf16[4,1,128,512]{3,2,1,0:T(8,128)(2,1)S(1)} all-gather(bf16[1,1,128,512]{3,2,1,0:T(8,128)(2,1)} %param.3), channel_id=1, replica_groups=mesh['rows'=64,'section'=4] {'section'}, dimensions={0}, use_global_device_ids=true | all-gather | bytes 655360 | tf_op jit(solution)/shard_map/all_gather | solution.py:108
  32.4 9.2 %collective-permute-start.1 = (bf16[1,128,256]{2,1,0:T(8,128)(2,1)S(1)}, bf16[1,128,256]{2,1,0:T(8,128)(2,1)S(1)}, u32[]{:S(2)}, u32[]{:S(2)}) collective-permute-start(bf16[1,128,256]{2,1,0:T(8,128)(2,1)S(1)} %slice.1087), channel_id=1, source_target_pairs={{4,0},{8,4},{12,8},{16,12},{20,16},{24,20},{28,24},{32,28},{36,32}... | collective-permute-start | bytes 196616 | tf_op jit(solution)/shard_map/ppermute | solution.py:17
  74.4 7.4 %collective-permute-done.8 = bf16[2,1,128,512]{3,2,1,0:T(8,128)(2,1)S(1)} collective-permute-done((bf16[2,1,128,512]{3,2,1,0:T(8,128)(2,1)S(1)}, bf16[2,1,128,512]{3,2,1,0:T(8,128)(2,1)S(1)}, u32[]{:S(2)}, u32[]{:S(2)}) %collective-permute-start.8) | collective-permute-done | bytes 262176 | tf_op jit(solution)/shard_map/ppermute | solution.py:25
  91.8 4.3 collective-permute-start.13
  105.7 4.3 collective-permute-start.15
  113.2 6.8 %collective-permute-done.17 = bf16[2,1,128,512]{3,2,1,0:T(8,128)(2,1)S(1)} collective-permute-done((bf16[2,1,128,512]{3,2,1,0:T(8,128)(2,1)S(1)}, bf16[2,1,128,512]{3,2,1,0:T(8,128)(2,1)S(1)}, u32[]{:S(2)}, u32[]{:S(2)}) %collective-permute-start.17) | collective-permute-done | bytes 262176 | tf_op jit(solution)/shard_map/ppermute | solution.py:25
  122.1 5.6 collective-permute-start.18
  145.3 4.3 collective-permute-start.24
  153.6 7.1 %collective-permute-done.26 = bf16[2,1,128,512]{3,2,1,0:T(8,128)(2,1)} collective-permute-done((bf16[2,1,128,512]{3,2,1,0:T(8,128)(2,1)}, bf16[2,1,128,512]{3,2,1,0:T(8,128)(2,1)}, u32[]{:S(2)}, u32[]{:S(2)}) %collective-permute-start.26) | collective-permute-done | bytes 262176 | tf_op jit(solution)/shard_map/ppermute | solution.py:25
  163.9 4.9 collective-permute-start.27
  172.8 4.4 collective-permute-start.31
  181.1 8.8 %collective-permute-start.29 = (bf16[1,128,256]{2,1,0:T(8,128)(2,1)S(1)}, bf16[1,128,256]{2,1,0:T(8,128)(2,1)S(1)}, u32[]{:S(2)}, u32[]{:S(2)}) collective-permute-start(bf16[1,128,256]{2,1,0:T(8,128)(2,1)S(1)} %bitcast.561), channel_id=1, source_target_pairs={{0,4},{4,8},{8,12},{12,16},{16,20},{20,24},{24,28},{28,32},{32,36}... | collective-permute-start | bytes 196616 | tf_op jit(solution)/shard_map/ppermute | solution.py:16
  193.6 5.1 collective-permute-start.33
  202.6 5.5 collective-permute-done.35
  210.0 7.6 %collective-permute-start.36 = (bf16[1,128,256]{2,1,0:T(8,128)(2,1)S(1)}, bf16[1,128,256]{2,1,0:T(8,128)(2,1)S(1)}, u32[]{:S(2)}, u32[]{:S(2)}) collective-permute-start(bf16[1,128,256]{2,1,0:T(8,128)(2,1)S(1)} %slice.1207), channel_id=1, source_target_pairs={{0,4},{4,8},{8,12},{12,16},{16,20},{20,24},{24,28},{28,32},{32,36}... | collective-permute-start | bytes 196616 | tf_op jit(solution)/shard_map/ppermute | solution.py:16
  222.1 4.8 collective-permute-start.40
  229.4 8.4 %collective-permute-start.38 = (bf16[1,128,256]{2,1,0:T(8,128)(2,1)S(1)}, bf16[1,128,256]{2,1,0:T(8,128)(2,1)S(1)}, u32[]{:S(2)}, u32[]{:S(2)}) collective-permute-start(bf16[1,128,256]{2,1,0:T(8,128)(2,1)S(1)} %bitcast.564), channel_id=1, source_target_pairs={{0,4},{4,8},{8,12},{12,16},{16,20},{20,24},{24,28},{28,32},{32,36}... | collective-permute-start | bytes 196616 | tf_op jit(solution)/shard_map/ppermute | solution.py:16
  241.6 5.0 collective-permute-start.42
  257.9 7.5 %collective-permute-start.45 = (bf16[1,128,256]{2,1,0:T(8,128)(2,1)S(1)}, bf16[1,128,256]{2,1,0:T(8,128)(2,1)S(1)}, u32[]{:S(2)}, u32[]{:S(2)}) collective-permute-start(bf16[1,128,256]{2,1,0:T(8,128)(2,1)S(1)} %slice.1237), channel_id=1, source_target_pairs={{0,4},{4,8},{8,12},{12,16},{16,20},{20,24},{24,28},{28,32},{32,36}... | collective-permute-start | bytes 196616 | tf_op jit(solution)/shard_map/ppermute | solution.py:16
  269.3 4.4 collective-permute-start.49
  277.5 8.8 %collective-permute-start.47 = (bf16[1,128,256]{2,1,0:T(8,128)(2,1)S(1)}, bf16[1,128,256]{2,1,0:T(8,128)(2,1)S(1)}, u32[]{:S(2)}, u32[]{:S(2)}) collective-permute-start(bf16[1,128,256]{2,1,0:T(8,128)(2,1)S(1)} %bitcast.558), channel_id=1, source_target_pairs={{0,4},{4,8},{8,12},{12,16},{16,20},{20,24},{24,28},{28,32},{32,36}... | collective-permute-start | bytes 196616 | tf_op jit(solution)/shard_map/ppermute | solution.py:16
  290.2 4.3 collective-permute-start.51
  298.3 6.3 collective-permute-done.53
  306.5 7.1 %collective-permute-start.54 = (bf16[1,128,256]{2,1,0:T(8,128)(2,1)S(1)}, bf16[1,128,256]{2,1,0:T(8,128)(2,1)S(1)}, u32[]{:S(2)}, u32[]{:S(2)}) collective-permute-start(bf16[1,128,256]{2,1,0:T(8,128)(2,1)S(1)} %slice.1267), channel_id=1, source_target_pairs={{0,4},{4,8},{8,12},{12,16},{16,20},{20,24},{24,28},{28,32},{32,36}... | collective-permute-start | bytes 196616 | tf_op jit(solution)/shard_map/ppermute | solution.py:16
  318.2 4.4 collective-permute-start.58
  324.5 8.9 %collective-permute-start.56 = (bf16[1,128,256]{2,1,0:T(8,128)(2,1)S(1)}, bf16[1,128,256]{2,1,0:T(8,128)(2,1)S(1)}, u32[]{:S(2)}, u32[]{:S(2)}) collective-permute-start(bf16[1,128,256]{2,1,0:T(8,128)(2,1)S(1)} %bitcast.552), channel_id=1, source_target_pairs={{0,4},{4,8},{8,12},{12,16},{16,20},{20,24},{24,28},{28,32},{32,36}... | collective-permute-start | bytes 196616 | tf_op jit(solution)/shard_map/ppermute | solution.py:16
  340.3 5.5 collective-permute-start.60
  350.3 5.5 fusion.13
  356.1 14.2 %copy.13 = f32[1,2,2304,256]{3,1,0,2:T(2,128)} copy(f32[1,2,2304,256]{3,2,1,0:T(8,128)S(1)} %maximum_bitcast_fusion) | data formatting | bytes 9437184 | tf_op jit(solution)/shard_map/broadcast_in_dim | solution.py:135
  372.3 83.0 %all-reduce.32.cloned.1.call-done = bf16[4,2,1,128,512]{4,3,1,2,0:T(8,128)(2,1)} async-done(((bf16[4,2,1,128,512]{4,3,1,2,0:T(8,128)(2,1)}), bf16[4,2,1,128,512]{4,3,1,2,0:T(8,128)(2,1)}) %all-reduce.32.cloned.1.call-update) | async-done | bytes 1048592 | tf_op jit(solution)/shard_map/psum | solution.py:30
  456.9 199.7 %all-reduce.34.cloned.1.call-done = f32[1,2,2304,256]{3,1,0,2:T(2,128)} async-done(((f32[1,2,2304,256]{3,1,0,2:T(2,128)}), f32[1,2,2304,256]{3,1,0,2:T(2,128)}) %all-reduce.34.cloned.1.call-update) | async-done | bytes 4718608
  (538 shorter events, 159.9 us)
Async XLA Ops:
  7.2 448.1 %all-reduce.32.cloned.1.call-start = ((), (), s32[]{:S(2)}) async-start(), calls=%async_computation | async-start | bytes 2097152 | tf_op jit(solution)/shard_map/psum | solution.py:30
  32.4 11.2 %collective-permute-start.1 = (bf16[1,128,256]{2,1,0:T(8,128)(2,1)S(1)}, bf16[1,128,256]{2,1,0:T(8,128)(2,1)S(1)}, u32[]{:S(2)}, u32[]{:S(2)}) collective-permute-start(bf16[1,128,256]{2,1,0:T(8,128)(2,1)S(1)} %slice.1087), channel_id=1, source_target_pairs={{4,0},{8,4},{12,8},{16,12},{20,16},{24,20},{28,24},{32,28},{36,32}... | collective-permute-start | bytes 196616 | tf_op jit(solution)/shard_map/ppermute | solution.py:17
  46.1 13.6 %collective-permute-start.5 = (bf16[1,128,256]{2,1,0:T(8,128)(2,1)}, bf16[1,128,256]{2,1,0:T(8,128)(2,1)}, u32[]{:S(2)}, u32[]{:S(2)}) collective-permute-start(bf16[1,128,256]{2,1,0:T(8,128)(2,1)} %bitcast.12), channel_id=1, source_target_pairs={{4,0},{8,4},{12,8},{16,12},{20,16},{24,20},{28,24},{32,28},{36,32}... | collective-permute-start | bytes 196616 | tf_op jit(solution)/shard_map/ppermute | solution.py:17
  48.2 11.6 %collective-permute-start.4 = (bf16[1,128,256]{2,1,0:T(8,128)(2,1)}, bf16[1,128,256]{2,1,0:T(8,128)(2,1)}, u32[]{:S(2)}, u32[]{:S(2)}) collective-permute-start(bf16[1,128,256]{2,1,0:T(8,128)(2,1)} %bitcast.12), channel_id=1, source_target_pairs={{0,4},{4,8},{8,12},{12,16},{16,20},{20,24},{24,28},{28,32},{32,36}... | collective-permute-start | bytes 196616 | tf_op jit(solution)/shard_map/ppermute | solution.py:16
  54.0 9.5 %collective-permute-start.3 = (bf16[1,128,256]{2,1,0:T(8,128)(2,1)}, bf16[1,128,256]{2,1,0:T(8,128)(2,1)S(1)}, u32[]{:S(2)}, u32[]{:S(2)}) collective-permute-start(bf16[1,128,256]{2,1,0:T(8,128)(2,1)} %bitcast.554), channel_id=1, source_target_pairs={{4,0},{8,4},{12,8},{16,12},{20,16},{24,20},{28,24},{32,28},{36,32}... | collective-permute-start | bytes 196616 | tf_op jit(solution)/shard_map/ppermute | solution.py:17
  89.9 11.8 %collective-permute-start.14 = (bf16[1,128,256]{2,1,0:T(8,128)(2,1)S(1)}, bf16[1,128,256]{2,1,0:T(8,128)(2,1)S(1)}, u32[]{:S(2)}, u32[]{:S(2)}) collective-permute-start(bf16[1,128,256]{2,1,0:T(8,128)(2,1)S(1)} %bitcast.515), channel_id=1, source_target_pairs={{4,0},{8,4},{12,8},{16,12},{20,16},{24,20},{28,24},{32,28},{36,32}... | collective-permute-start | bytes 196616 | tf_op jit(solution)/shard_map/ppermute | solution.py:17
  91.8 9.9 %collective-permute-start.13 = (bf16[1,128,256]{2,1,0:T(8,128)(2,1)S(1)}, bf16[1,128,256]{2,1,0:T(8,128)(2,1)S(1)}, u32[]{:S(2)}, u32[]{:S(2)}) collective-permute-start(bf16[1,128,256]{2,1,0:T(8,128)(2,1)S(1)} %bitcast.516), channel_id=1, source_target_pairs={{0,4},{4,8},{8,12},{12,16},{16,20},{20,24},{24,28},{28,32},{32,36}... | collective-permute-start | bytes 196616 | tf_op jit(solution)/shard_map/ppermute | solution.py:16
  129.7 11.8 %collective-permute-start.23 = (bf16[1,128,256]{2,1,0:T(8,128)(2,1)S(1)}, bf16[1,128,256]{2,1,0:T(8,128)(2,1)S(1)}, u32[]{:S(2)}, u32[]{:S(2)}) collective-permute-start(bf16[1,128,256]{2,1,0:T(8,128)(2,1)S(1)} %bitcast.518), channel_id=1, source_target_pairs={{4,0},{8,4},{12,8},{16,12},{20,16},{24,20},{28,24},{32,28},{36,32}... | collective-permute-start | bytes 196616 | tf_op jit(solution)/shard_map/ppermute | solution.py:17
  131.6 9.9 %collective-permute-start.22 = (bf16[1,128,256]{2,1,0:T(8,128)(2,1)S(1)}, bf16[1,128,256]{2,1,0:T(8,128)(2,1)S(1)}, u32[]{:S(2)}, u32[]{:S(2)}) collective-permute-start(bf16[1,128,256]{2,1,0:T(8,128)(2,1)S(1)} %bitcast.519), channel_id=1, source_target_pairs={{0,4},{4,8},{8,12},{12,16},{16,20},{20,24},{24,28},{28,32},{32,36}... | collective-permute-start | bytes 196616 | tf_op jit(solution)/shard_map/ppermute | solution.py:16
  170.9 19.0 %collective-permute-start.32 = (bf16[1,128,256]{2,1,0:T(8,128)(2,1)S(1)}, bf16[1,128,256]{2,1,0:T(8,128)(2,1)S(1)}, u32[]{:S(2)}, u32[]{:S(2)}) collective-permute-start(bf16[1,128,256]{2,1,0:T(8,128)(2,1)S(1)} %bitcast.530), channel_id=1, source_target_pairs={{4,0},{8,4},{12,8},{16,12},{20,16},{24,20},{28,24},{32,28},{36,32}... | collective-permute-start | bytes 196616 | tf_op jit(solution)/shard_map/ppermute | solution.py:17
  172.8 17.1 %collective-permute-start.31 = (bf16[1,128,256]{2,1,0:T(8,128)(2,1)S(1)}, bf16[1,128,256]{2,1,0:T(8,128)(2,1)S(1)}, u32[]{:S(2)}, u32[]{:S(2)}) collective-permute-start(bf16[1,128,256]{2,1,0:T(8,128)(2,1)S(1)} %bitcast.531), channel_id=1, source_target_pairs={{0,4},{4,8},{8,12},{12,16},{16,20},{20,24},{24,28},{28,32},{32,36}... | collective-permute-start | bytes 196616 | tf_op jit(solution)/shard_map/ppermute | solution.py:16
  179.2 11.3 %collective-permute-start.30 = (bf16[1,128,256]{2,1,0:T(8,128)(2,1)S(1)}, bf16[1,128,256]{2,1,0:T(8,128)(2,1)S(1)}, u32[]{:S(2)}, u32[]{:S(2)}) collective-permute-start(bf16[1,128,256]{2,1,0:T(8,128)(2,1)S(1)} %bitcast.560), channel_id=1, source_target_pairs={{4,0},{8,4},{12,8},{16,12},{20,16},{24,20},{28,24},{32,28},{36,32}... | collective-permute-start | bytes 196616 | tf_op jit(solution)/shard_map/ppermute | solution.py:17
  181.1 10.0 %collective-permute-start.29 = (bf16[1,128,256]{2,1,0:T(8,128)(2,1)S(1)}, bf16[1,128,256]{2,1,0:T(8,128)(2,1)S(1)}, u32[]{:S(2)}, u32[]{:S(2)}) collective-permute-start(bf16[1,128,256]{2,1,0:T(8,128)(2,1)S(1)} %bitcast.561), channel_id=1, source_target_pairs={{0,4},{4,8},{8,12},{12,16},{16,20},{20,24},{24,28},{28,32},{32,36}... | collective-permute-start | bytes 196616 | tf_op jit(solution)/shard_map/ppermute | solution.py:16
  208.1 11.5 %collective-permute-start.37 = (bf16[1,128,256]{2,1,0:T(8,128)(2,1)S(1)}, bf16[1,128,256]{2,1,0:T(8,128)(2,1)S(1)}, u32[]{:S(2)}, u32[]{:S(2)}) collective-permute-start(bf16[1,128,256]{2,1,0:T(8,128)(2,1)S(1)} %slice.1207), channel_id=1, source_target_pairs={{4,0},{8,4},{12,8},{16,12},{20,16},{24,20},{28,24},{32,28},{36,32}... | collective-permute-start | bytes 196616 | tf_op jit(solution)/shard_map/ppermute | solution.py:17
  210.0 9.5 %collective-permute-start.36 = (bf16[1,128,256]{2,1,0:T(8,128)(2,1)S(1)}, bf16[1,128,256]{2,1,0:T(8,128)(2,1)S(1)}, u32[]{:S(2)}, u32[]{:S(2)}) collective-permute-start(bf16[1,128,256]{2,1,0:T(8,128)(2,1)S(1)} %slice.1207), channel_id=1, source_target_pairs={{0,4},{4,8},{8,12},{12,16},{16,20},{20,24},{24,28},{28,32},{32,36}... | collective-permute-start | bytes 196616 | tf_op jit(solution)/shard_map/ppermute | solution.py:16
  220.2 17.6 %collective-permute-start.41 = (bf16[1,128,256]{2,1,0:T(8,128)(2,1)S(1)}, bf16[1,128,256]{2,1,0:T(8,128)(2,1)S(1)}, u32[]{:S(2)}, u32[]{:S(2)}) collective-permute-start(bf16[1,128,256]{2,1,0:T(8,128)(2,1)S(1)} %bitcast.533), channel_id=1, source_target_pairs={{4,0},{8,4},{12,8},{16,12},{20,16},{24,20},{28,24},{32,28},{36,32}... | collective-permute-start | bytes 196616 | tf_op jit(solution)/shard_map/ppermute | solution.py:17
  222.1 15.6 %collective-permute-start.40 = (bf16[1,128,256]{2,1,0:T(8,128)(2,1)S(1)}, bf16[1,128,256]{2,1,0:T(8,128)(2,1)S(1)}, u32[]{:S(2)}, u32[]{:S(2)}) collective-permute-start(bf16[1,128,256]{2,1,0:T(8,128)(2,1)S(1)} %bitcast.534), channel_id=1, source_target_pairs={{0,4},{4,8},{8,12},{12,16},{16,20},{20,24},{24,28},{28,32},{32,36}... | collective-permute-start | bytes 196616 | tf_op jit(solution)/shard_map/ppermute | solution.py:16
  227.4 10.9 %collective-permute-start.39 = (bf16[1,128,256]{2,1,0:T(8,128)(2,1)S(1)}, bf16[1,128,256]{2,1,0:T(8,128)(2,1)S(1)}, u32[]{:S(2)}, u32[]{:S(2)}) collective-permute-start(bf16[1,128,256]{2,1,0:T(8,128)(2,1)S(1)} %bitcast.563), channel_id=1, source_target_pairs={{4,0},{8,4},{12,8},{16,12},{20,16},{24,20},{28,24},{32,28},{36,32}... | collective-permute-start | bytes 196616 | tf_op jit(solution)/shard_map/ppermute | solution.py:17
  229.4 9.7 %collective-permute-start.38 = (bf16[1,128,256]{2,1,0:T(8,128)(2,1)S(1)}, bf16[1,128,256]{2,1,0:T(8,128)(2,1)S(1)}, u32[]{:S(2)}, u32[]{:S(2)}) collective-permute-start(bf16[1,128,256]{2,1,0:T(8,128)(2,1)S(1)} %bitcast.564), channel_id=1, source_target_pairs={{0,4},{4,8},{8,12},{12,16},{16,20},{20,24},{24,28},{28,32},{32,36}... | collective-permute-start | bytes 196616 | tf_op jit(solution)/shard_map/ppermute | solution.py:16
  256.0 9.9 %collective-permute-start.46 = (bf16[1,128,256]{2,1,0:T(8,128)(2,1)S(1)}, bf16[1,128,256]{2,1,0:T(8,128)(2,1)S(1)}, u32[]{:S(2)}, u32[]{:S(2)}) collective-permute-start(bf16[1,128,256]{2,1,0:T(8,128)(2,1)S(1)} %slice.1237), channel_id=1, source_target_pairs={{4,0},{8,4},{12,8},{16,12},{20,16},{24,20},{28,24},{32,28},{36,32}... | collective-permute-start | bytes 196616 | tf_op jit(solution)/shard_map/ppermute | solution.py:17
  267.4 19.0 %collective-permute-start.50 = (bf16[1,128,256]{2,1,0:T(8,128)(2,1)S(1)}, bf16[1,128,256]{2,1,0:T(8,128)(2,1)S(1)}, u32[]{:S(2)}, u32[]{:S(2)}) collective-permute-start(bf16[1,128,256]{2,1,0:T(8,128)(2,1)S(1)} %bitcast.536), channel_id=1, source_target_pairs={{4,0},{8,4},{12,8},{16,12},{20,16},{24,20},{28,24},{32,28},{36,32}... | collective-permute-start | bytes 196616 | tf_op jit(solution)/shard_map/ppermute | solution.py:17
  269.3 17.1 %collective-permute-start.49 = (bf16[1,128,256]{2,1,0:T(8,128)(2,1)S(1)}, bf16[1,128,256]{2,1,0:T(8,128)(2,1)S(1)}, u32[]{:S(2)}, u32[]{:S(2)}) collective-permute-start(bf16[1,128,256]{2,1,0:T(8,128)(2,1)S(1)} %bitcast.537), channel_id=1, source_target_pairs={{0,4},{4,8},{8,12},{12,16},{16,20},{20,24},{24,28},{28,32},{32,36}... | collective-permute-start | bytes 196616 | tf_op jit(solution)/shard_map/ppermute | solution.py:16
  275.6 11.3 %collective-permute-start.48 = (bf16[1,128,256]{2,1,0:T(8,128)(2,1)S(1)}, bf16[1,128,256]{2,1,0:T(8,128)(2,1)S(1)}, u32[]{:S(2)}, u32[]{:S(2)}) collective-permute-start(bf16[1,128,256]{2,1,0:T(8,128)(2,1)S(1)} %bitcast.557), channel_id=1, source_target_pairs={{4,0},{8,4},{12,8},{16,12},{20,16},{24,20},{28,24},{32,28},{36,32}... | collective-permute-start | bytes 196616 | tf_op jit(solution)/shard_map/ppermute | solution.py:17
  277.5 10.1 %collective-permute-start.47 = (bf16[1,128,256]{2,1,0:T(8,128)(2,1)S(1)}, bf16[1,128,256]{2,1,0:T(8,128)(2,1)S(1)}, u32[]{:S(2)}, u32[]{:S(2)}) collective-permute-start(bf16[1,128,256]{2,1,0:T(8,128)(2,1)S(1)} %bitcast.558), channel_id=1, source_target_pairs={{0,4},{4,8},{8,12},{12,16},{16,20},{20,24},{24,28},{28,32},{32,36}... | collective-permute-start | bytes 196616 | tf_op jit(solution)/shard_map/ppermute | solution.py:16
  304.6 11.0 %collective-permute-start.55 = (bf16[1,128,256]{2,1,0:T(8,128)(2,1)S(1)}, bf16[1,128,256]{2,1,0:T(8,128)(2,1)S(1)}, u32[]{:S(2)}, u32[]{:S(2)}) collective-permute-start(bf16[1,128,256]{2,1,0:T(8,128)(2,1)S(1)} %slice.1267), channel_id=1, source_target_pairs={{4,0},{8,4},{12,8},{16,12},{20,16},{24,20},{28,24},{32,28},{36,32}... | collective-permute-start | bytes 196616 | tf_op jit(solution)/shard_map/ppermute | solution.py:17
  306.5 9.1 %collective-permute-start.54 = (bf16[1,128,256]{2,1,0:T(8,128)(2,1)S(1)}, bf16[1,128,256]{2,1,0:T(8,128)(2,1)S(1)}, u32[]{:S(2)}, u32[]{:S(2)}) collective-permute-start(bf16[1,128,256]{2,1,0:T(8,128)(2,1)S(1)} %slice.1267), channel_id=1, source_target_pairs={{0,4},{4,8},{8,12},{12,16},{16,20},{20,24},{24,28},{28,32},{32,36}... | collective-permute-start | bytes 196616 | tf_op jit(solution)/shard_map/ppermute | solution.py:16
  316.2 20.9 %collective-permute-start.59 = (bf16[1,128,256]{2,1,0:T(8,128)(2,1)S(1)}, bf16[1,128,256]{2,1,0:T(8,128)(2,1)S(1)}, u32[]{:S(2)}, u32[]{:S(2)}) collective-permute-start(bf16[1,128,256]{2,1,0:T(8,128)(2,1)S(1)} %bitcast.545), channel_id=1, source_target_pairs={{4,0},{8,4},{12,8},{16,12},{20,16},{24,20},{28,24},{32,28},{36,32}... | collective-permute-start | bytes 196616 | tf_op jit(solution)/shard_map/ppermute | solution.py:17
  318.2 18.9 %collective-permute-start.58 = (bf16[1,128,256]{2,1,0:T(8,128)(2,1)S(1)}, bf16[1,128,256]{2,1,0:T(8,128)(2,1)S(1)}, u32[]{:S(2)}, u32[]{:S(2)}) collective-permute-start(bf16[1,128,256]{2,1,0:T(8,128)(2,1)S(1)} %bitcast.546), channel_id=1, source_target_pairs={{0,4},{4,8},{8,12},{12,16},{16,20},{20,24},{24,28},{28,32},{32,36}... | collective-permute-start | bytes 196616 | tf_op jit(solution)/shard_map/ppermute | solution.py:16
  322.6 15.1 %collective-permute-start.57 = (bf16[1,128,256]{2,1,0:T(8,128)(2,1)S(1)}, bf16[1,128,256]{2,1,0:T(8,128)(2,1)S(1)}, u32[]{:S(2)}, u32[]{:S(2)}) collective-permute-start(bf16[1,128,256]{2,1,0:T(8,128)(2,1)S(1)} %bitcast.551), channel_id=1, source_target_pairs={{4,0},{8,4},{12,8},{16,12},{20,16},{24,20},{28,24},{32,28},{36,32}... | collective-permute-start | bytes 196616 | tf_op jit(solution)/shard_map/ppermute | solution.py:17
  324.5 13.1 %collective-permute-start.56 = (bf16[1,128,256]{2,1,0:T(8,128)(2,1)S(1)}, bf16[1,128,256]{2,1,0:T(8,128)(2,1)S(1)}, u32[]{:S(2)}, u32[]{:S(2)}) collective-permute-start(bf16[1,128,256]{2,1,0:T(8,128)(2,1)S(1)} %bitcast.552), channel_id=1, source_target_pairs={{0,4},{4,8},{8,12},{12,16},{16,20},{20,24},{24,28},{28,32},{32,36}... | collective-permute-start | bytes 196616 | tf_op jit(solution)/shard_map/ppermute | solution.py:16
  338.3 9.4 %collective-permute-start.61 = (bf16[1,128,256]{2,1,0:T(8,128)(2,1)S(1)}, bf16[1,128,256]{2,1,0:T(8,128)(2,1)S(1)}, u32[]{:S(2)}, u32[]{:S(2)}) collective-permute-start(bf16[1,128,256]{2,1,0:T(8,128)(2,1)S(1)} %bitcast.548), channel_id=1, source_target_pairs={{4,0},{8,4},{12,8},{16,12},{20,16},{24,20},{28,24},{32,28},{36,32}... | collective-permute-start | bytes 196616 | tf_op jit(solution)/shard_map/ppermute | solution.py:17
  349.5 307.1 %all-reduce.34.cloned.1.call-start = ((), (), s32[]{:S(2)}) async-start(), calls=%async_computation.1 | async-start | bytes 9437184
  (65 other events, 574.3 us)
Sparse Core Ops, SparseCore 0:
  349.7 105.5 all-reduce.31
  459.2 197.3 all-reduce.33
where the time goes:
time: 668 us; the launch traced here: 665 us
  waiting for transfers between devices  336 us (50%)
  starting transfers between devices  217 us (32%)
  matrix products  34.9 us (5%)
  local copies, waits for them, and re-layouts  26.8 us (4%)
  blocking collectives  23.5 us (4%)
  between operations  18.6 us (3%)
  other arithmetic  8.63 us (1%)
    unnamed x3, waiting for transfers between devices  200 us
    ppermute x28, starting transfers between devices, extended(): before = lax.ppermute(last, axis, up)  147 us
    psum x1, waiting for transfers between devices, broadcast(): return lax.psum(block, axis)  83 us
    ppermute x28, starting transfers between devices, extended(): after = lax.ppermute(initial, axis, down)  61.6 us
    ppermute x6, waiting for transfers between devices, from_behind(): return lax.ppermute(value, axis, pairs)  37.2 us
    dot_general x7, matrix products, block_backward(): lax.dot_general(taps_second, delta_f, (((0,), (0,)), ((), ())), preferred...  17.1 us
    ppermute x28, waiting for transfers between devices, extended(): before = lax.ppermute(last, axis, up)  15.7 us
    broadcast_in_dim x1, local copies, waits for them, and re-layouts, local(): terms = jnp.stack([grad_f, grad_g])[None]  14.2 us
  transfers between devices with their start and end apart: 64, of which 23 were waited for; matrix products, arithmetic and copies ran while one was open for 7% of the time, Pallas kernels for 0%

commit v1 on v0

v1 whole, which is shorter than its diff:
```python
import functools
import math

import jax
import jax.numpy as jnp
from jax import lax
from jax.experimental import pallas as pl
from jax.experimental.pallas import tpu as pltpu
from jax.sharding import PartitionSpec as P

HALF=256; TR=8; TC=16

def row_chunks(rows, most):
    n = -(-rows // most)
    base, extra = divmod(rows, n)
    out=[]; a=0
    for i in range(n):
        b = base + (1 if i < extra else 0)
        out.append((a, b)); a += b
    return out

def block_kernel(p, W, WN, most, meta, y1, y2, g1, g2, wa, wb, x1o, x2o, t1o, n2o, ay, ax, dgo, dfo, w, s1, s2, s3, s4, sems):
    C = HALF
    core, rowbase, colbase = meta[0], meta[1], meta[2]
    ca = pltpu.make_async_copy(wa, w.at[core], sems.at[0])
    cb = pltpu.make_async_copy(wb, w.at[1 - core], sems.at[1])
    ca.start(); cb.start()
    first = 8 + 2 * (p + 1)
    own = (W - TC) // 2
    cut = (W - WN) // 2

    def spread(buf, at, value):
        n = value.shape[0]
        flat = value.reshape(n * W, C)
        buf[at * W:(at + n) * W, 0:C] = pltpu.roll(flat, 1, 0).astype(jnp.bfloat16)
        buf[at * W:(at + n) * W, C:2 * C] = flat.astype(jnp.bfloat16)
        buf[at * W:(at + n) * W, 2 * C:3 * C] = pltpu.roll(flat, n * W - 1, 0).astype(jnp.bfloat16)

    def mask(a, n, halo):
        r = lax.broadcasted_iota(jnp.int32, (n, W, 1), 0) + (rowbase - halo + a)
        c = lax.broadcasted_iota(jnp.int32, (n, W, 1), 1) + (colbase - own)
        return (r >= 0) & (r < 64) & (c >= 0) & (c < 128)

    def conv(buf, a, n, branch):
        acc = None
        for dr in range(3):
            d = jnp.dot(buf[(a + dr) * W:(a + dr + n) * W, :], w[branch, 768 * dr:768 * (dr + 1), :],
                        preferred_element_type=jnp.float32)
            acc = d if acc is None else acc + d
        return acc.reshape(n, W, C)

    def conv_t(buf, a, n, branch):
        acc = None
        for dr in range(3):
            for dc in range(3):
                tap = 3 * dr + dc
                d = lax.dot_general(buf[(a + 2 - dr) * W:(a + 2 - dr + n) * W, (2 - dc) * C:(3 - dc) * C],
                                    w[branch, 256 * tap:256 * (tap + 1), :],
                                    (((1,), (1,)), ((), ())), preferred_element_type=jnp.float32)
                acc = d if acc is None else acc + d
        return acc.reshape(n, W, C)

    for a, n in row_chunks(first, most):
        spread(s1, a, y1[a:a + n].astype(jnp.float32))
    ca.wait(); cb.wait()
    for a, n in row_chunks(8 + 2 * p, most):
        pre = conv(s1, a, n, 1)
        sig = jax.nn.sigmoid(pre)
        x2 = jnp.where(mask(a, n, p), y2[a:a + n].astype(jnp.float32) - pre * sig, 0.0)
        x2 = x2.astype(jnp.bfloat16).astype(jnp.float32)
        spread(s2, a, x2)
        dg = g2[a:a + n].astype(jnp.float32) * (sig * (1.0 + pre * (1.0 - sig)))
        spread(s3, a, dg.astype(jnp.bfloat16).astype(jnp.float32))
    for a, n in row_chunks(8 + 2 * (p - 1), most):
        pre = conv(s2, a, n, 0)
        sig = jax.nn.sigmoid(pre)
        m = mask(a, n, p - 1)
        x1 = jnp.where(m, y1[a + 2:a + 2 + n].astype(jnp.float32) - pre * sig, 0.0)
        t1 = jnp.where(m, g1[a:a + n].astype(jnp.float32) + conv_t(s3, a, n, 1), 0.0)
        t1 = t1.astype(jnp.bfloat16).astype(jnp.float32)
        df = t1 * (sig * (1.0 + pre * (1.0 - sig)))
        spread(s4, a, df.astype(jnp.bfloat16).astype(jnp.float32))
        store(x1o, x1, a, n, p - 1, cut, WN)
        store(t1o, t1, a, n, p - 1, cut, WN)
    for a, n in row_chunks(8 + 2 * (p - 2), most):
        n2 = jnp.where(mask(a, n, p - 2), g2[a + 2:a + 2 + n].astype(jnp.float32) + conv_t(s4, a, n, 0), 0.0)
        store(n2o, n2, a, n, p - 2, cut, WN)
    rows2 = x2o.shape[0]; off = (8 + 2 * p - rows2) // 2
    x2 = s2[off * W:(off + rows2) * W, C:2 * C].astype(jnp.float32).reshape(rows2, W, C)
    x2o[...] = x2[:, cut:cut + WN].astype(jnp.bfloat16)
    e = own - 8
    for dst, src, h in ((ay, s1, p + 1), (ax, s2, p)):
        v = src[(h - 1) * W:(h + 9) * W, C:2 * C].astype(jnp.float32).reshape(10, W, C)
        dst[...] = v[:, e:e + 32].astype(jnp.bfloat16)
    for dst, src, h in ((dgo, s3, p), (dfo, s4, p - 1)):
        v = src[h * W:(h + 8) * W, C:2 * C].astype(jnp.float32).reshape(8, W, C)
        dst[...] = v[:, own:own + TC].astype(jnp.bfloat16)

def store(ref, value, a, n, halo, cut, WN):
    rows = ref.shape[0]; off = (8 + 2 * halo - rows) // 2
    lo, hi = max(a, off), min(a + n, off + rows)
    if lo < hi:
        ref[lo - off:hi - off] = value[lo - a:hi - a, cut:cut + WN].astype(jnp.bfloat16)

def block(p, W, WN, meta, y1, y2, g1, g2, wa, wb, most=8):
    C = HALF; b = jnp.bfloat16
    q = max(p - 2, 0)
    rows_x1 = 8 + 2 * (p - 1) if p > 2 else 8
    outs = [(rows_x1, WN), (8 + 2 * q, WN), (8 + 2 * max(p - 3, 0), WN), (8 + 2 * q, WN), (10, 32), (10, 32), (8, TC), (8, TC)]
    V = pl.BlockSpec(memory_space=pltpu.VMEM)
    flops = 2 * 2304 * 256 * W * 2 * (4 * (8 + 2 * p) - 8)
    return pl.pallas_call(
        functools.partial(block_kernel, p, W, WN, most),
        out_shape=[jax.ShapeDtypeStruct((r, w_, C), b) for r, w_ in outs],
        in_specs=[pl.BlockSpec(memory_space=pltpu.SMEM), V, V, V, V, pl.BlockSpec(memory_space=pl.ANY), pl.BlockSpec(memory_space=pl.ANY)],
        out_specs=[V] * 8,
        scratch_shapes=[pltpu.VMEM((2, 2304, C), b)] + [pltpu.VMEM(((8 + 2 * (p + 1 - i)) * W, 3 * C), b) for i in (0, 1, 1, 2)] + [pltpu.SemaphoreType.DMA((2,))],
        compiler_params=pltpu.CompilerParams(vmem_limit_bytes=40 * 1024 * 1024),
        cost_estimate=pl.CostEstimate(flops=flops, bytes_accessed=6 * 1024 * 1024, transcendentals=0),
        name="block_p%d" % p,
    )(meta, y1, y2, g1, g2, wa, wb)


def grad_kernel(meta, acts, send, mine, lhs):
    C = HALF
    core = meta[0]
    for branch, out in ((1 - core, send), (core, mine)):
        for m in range(4):
            v = acts[m, branch, 0:320, :].astype(jnp.float32)
            for dc, shifted in enumerate((pltpu.roll(v, 1, 0), v, pltpu.roll(v, 319, 0))):
                s = shifted.reshape(10, 32, C)[:, 8:24].astype(jnp.bfloat16)
                for dr in range(3):
                    t = 3 * dr + dc
                    lhs[m * 128:(m + 1) * 128, t * C:(t + 1) * C] = s[dr:dr + 8].reshape(128, C)
        d = jnp.concatenate([acts[m, branch, 320:448, :] for m in range(4)], axis=0)
        for t in range(9):
            g = lax.dot_general(lhs[:, t * C:(t + 1) * C], d, (((0,), (0,)), ((), ())),
                                preferred_element_type=jnp.float32)
            out[t * C:(t + 1) * C, :] = g.astype(out.dtype)


def kernel_grads(meta, acts):
    V = pl.BlockSpec(memory_space=pltpu.VMEM)
    return pl.pallas_call(
        grad_kernel,
        out_shape=[jax.ShapeDtypeStruct((2304, HALF), jnp.bfloat16), jax.ShapeDtypeStruct((2304, HALF), jnp.float32)],
        in_specs=[pl.BlockSpec(memory_space=pltpu.SMEM), V],
        out_specs=[V, V],
        scratch_shapes=[pltpu.VMEM((512, 2304), jnp.bfloat16)],
        compiler_params=pltpu.CompilerParams(vmem_limit_bytes=40 * 1024 * 1024),
        cost_estimate=pl.CostEstimate(flops=4 * 512 * 2304 * 256, bytes_accessed=8 * 1024 * 1024, transcendentals=0),
        name="kernel_grads",
    )(meta, acts)


def device(z, y, c):
    return (z * 4 + y) * 2 + c


PLANE = [[device(z, y, c) for y in range(4) for c in range(2)] for z in range(8)]
YLINE = [[device(z, y, c) for y in range(4)] for z in range(8) for c in range(2)]
ZLINE = [[device(z, y, c) for z in range(8)] for y in range(4) for c in range(2)]
CORES = [(i, i ^ 1) for i in range(64)]


def along_z(value, by):
    pairs = [(i, i + 8 * by) for i in range(64) if 0 <= i + 8 * by < 64]
    return lax.ppermute(value, "rows", pairs)


def exchange(value, groups):
    return lax.all_to_all(value, "rows", 0, 0, axis_index_groups=groups)


def local(block_out, out_grad, weights):
    C = HALF
    place = lax.axis_index("rows")
    z, j = place // 8, place % 8
    y, core = j // 2, place % 2
    meta = jnp.stack([core, 8 * z, 16 * j]).astype(jnp.int32)

    own = weights[0].reshape(4608, C)
    part = lax.dynamic_slice_in_dim(own, core * 2304 + y * 576, 576, 0)
    parts = lax.all_to_all(jnp.broadcast_to(part[None], (4, 576, C)), "section", 0, 0)

    pair = jnp.concatenate([block_out[0, 0], out_grad[0, 0]], axis=-1)
    padded = jnp.pad(pair, ((16, 16), (0, 0)))
    pieces = jnp.stack([padded[16 * i + 4:16 * i + 44] for i in range(8)])
    tile = exchange(pieces, PLANE)
    above = along_z(tile, 1)
    below = along_z(tile, -1)
    far_above = along_z(tile[7, :, :C], 2)
    far_below = along_z(tile[0, :, :C], -2)
    wide = lambda v: jnp.pad(v, ((0, 0), (4, 4), (0, 0)))
    y1 = wide(jnp.concatenate([far_above[None], above[..., :C], tile[..., :C], below[..., :C], far_below[None]], axis=0))
    y2, g1, g2 = (wide(jnp.concatenate([above[..., i * C:(i + 1) * C], tile[..., i * C:(i + 1) * C], below[..., i * C:(i + 1) * C]], axis=0)) for i in (1, 2, 3))
    g1 = g1[1:-1]

    acts = [None] * 4
    for k, p, W, WN in ((3, 8, 48, 32), (2, 6, 32, 32), (1, 4, 32, 32), (0, 2, 32, 16)):
        mine = exchange(jnp.broadcast_to(parts[k][None], (4, 576, C)), YLINE).reshape(2304, C)
        other = lax.ppermute(mine, "rows", CORES)
        y1, y2, g1, g2, ay, ax, dg, df = block(p, W, WN, meta, y1, y2, g1, g2, mine, other)
        acts[k] = jnp.concatenate([v.reshape(-1, C) for v in (ax, df, ay, dg)], axis=0)

    done = exchange(jnp.concatenate([y1, y2, g1, g2], axis=-1), PLANE).reshape(128, 4 * C)
    restored = done[:, :2 * C][None, None]
    input_grad = done[:, 2 * C:][None, None]

    gathered = lax.all_to_all(jnp.stack(acts), "section", 0, 0).reshape(4, 2, 448, C)
    away, kept = kernel_grads(meta, gathered)
    kept = kept + lax.ppermute(away, "rows", CORES).astype(jnp.float32)
    kept = kept.astype(jnp.bfloat16).reshape(8, 4, 72, C).transpose(1, 0, 2, 3).reshape(4, 576, C)
    kept = jnp.sum(exchange(kept, YLINE).astype(jnp.float32), axis=0)
    kept = kept.astype(jnp.bfloat16).reshape(8, 72, C)
    kept = jnp.sum(exchange(kept, ZLINE).astype(jnp.float32), axis=0)
    here = lax.dynamic_slice_in_dim(kept, 36 * core, 36, 0)
    there = lax.ppermute(lax.dynamic_slice_in_dim(kept, 36 * (1 - core), 36, 0), "rows", CORES)
    grad = jnp.where(core == 0, jnp.stack([here, there]), jnp.stack([there, here]))
    return restored, input_grad, (grad * (1.0 / math.sqrt(32768)))[None]


def solution(mesh):
    spec = P("section", "rows", None, None)
    return jax.shard_map(
        local,
        mesh=mesh,
        in_specs=(spec, spec, P("section", None, None, None)),
        out_specs=(spec, spec, P("section", None, "rows", None)),
        check_vma=False,
    )
```

time: 668 us -> 244 us (0.37)
  waiting for transfers between devices: 336 us -> 47.7 us
  starting transfers between devices: 217 us -> 65.4 us
  blocking collectives: 23.5 us -> 64 us
  matrix products: 34.9 us -> 0 us
  Pallas kernels: 0 us -> 25.2 us
  between operations: 18.6 us -> 0.93 us
    unnamed x3 -> x0, waiting for transfers between devices: 200 us -> none
    ppermute x62 -> x10, starting transfers between devices: 217 us -> 22.9 us  [the longest x4 11.9 us: along_z(): return lax.ppermute(value, 'rows', pairs)]
    psum x1 -> x0, waiting for transfers between devices: 83 us -> none  [broadcast(): return lax.psum(block, axis)]
    all_to_all x0 -> x3, blocking collectives: none -> 64 us  [the longest x2 38.2 us: exchange(): return lax.all_to_all(value, 'rows', 0, 0, axis_index_groups=groups)]
    ppermute x62 -> x10, waiting for transfers between devices: 53 us -> 3.44 us  [the longest x1 2.47 us: local(): kept = kept + lax.ppermute(away, 'rows', CORES).astype(jnp.float32)]
    all_to_all x0 -> x7, waiting for transfers between devices: none -> 44.3 us  [the longest x6 35.4 us: exchange(): return lax.all_to_all(value, 'rows', 0, 0, axis_index_groups=groups)]
    all_to_all x0 -> x7, starting transfers between devices: none -> 42.5 us  [the longest x6 37.5 us: exchange(): return lax.all_to_all(value, 'rows', 0, 0, axis_index_groups=groups)]
    dot_general x42 -> x0, matrix products: 34.9 us -> none  [the longest x7 17.1 us: block_backward(): lax.dot_general(taps_second, delta_f, (((0,), (0,)), ((), ())), preferred...]
  transfers between devices with their start and end apart: 64 -> 17, of which waited for: 23 -> 7; matrix products, arithmetic and copies ran while one was open for 7% -> 11% of each run, Pallas kernels for 0% -> 8%
where the time goes in v1:
time: 244 us; the launch traced here: 242 us
  starting transfers between devices  65.4 us (27%)
  blocking collectives  64 us (26%)
  waiting for transfers between devices  47.7 us (20%)
  local copies, waits for them, and re-layouts  28.8 us (12%)
  Pallas kernels  25.2 us (10%)
  other arithmetic  10.2 us (4%)
    all_to_all x2, blocking collectives, exchange(): return lax.all_to_all(value, 'rows', 0, 0, axis_index_groups=groups)  38.2 us
    all_to_all x6, starting transfers between devices, exchange(): return lax.all_to_all(value, 'rows', 0, 0, axis_index_groups=groups)  37.5 us
    all_to_all x6, waiting for transfers between devices, exchange(): return lax.all_to_all(value, 'rows', 0, 0, axis_index_groups=groups)  35.4 us
    all_to_all x1, blocking collectives, local(): lax.all_to_all(jnp.stack(acts), 'section', 0, 0).reshape(4, 2, 448, C)  25.9 us
    pallas_call x4, Pallas kernels, block(): pl.pallas_call(functools.partial(block_kernel, p, W, WN, most), out_shape...  23.2 us
    ppermute x4, starting transfers between devices, along_z(): return lax.ppermute(value, 'rows', pairs)  11.9 us
    ppermute x4, starting transfers between devices, local(): other = lax.ppermute(mine, 'rows', CORES)  9.7 us
    unnamed x25, local copies, waits for them, and re-layouts  9.09 us
  transfers between devices with their start and end apart: 17, of which 7 were waited for; matrix products, arithmetic and copies ran while one was open for 11% of the time, Pallas kernels for 8%

profile of v1, /device:TPU:1, one launch (start us, length us, event | category | flops | bytes accessed | tf_op | source)
XLA Modules:
  0.0 242.3 jit_solution(17049742865519836372)
XLA Ops:
  3.4 5.0 %all-to-all-start.1 = ((bf16[4,576,256]{2,1,0:T(8,128)(2,1)}), bf16[4,576,256]{2,1,0:T(8,128)(2,1)}, u32[]{:S(2)}, u32[]{:S(2)}) async-start(bf16[4,576,256]{2,1,0:T(8,128)(2,1)} %broadcast_in_dim.49), calls=%async_computation.1 | async-start | bytes 2359296 | tf_op jit(solution)/shard_map/all_to_all | solution.py:184
  13.6 8.8 %all-to-all-done.1 = bf16[4,576,256]{2,1,0:T(8,128)(2,1)} async-done(((bf16[4,576,256]{2,1,0:T(8,128)(2,1)}), bf16[4,576,256]{2,1,0:T(8,128)(2,1)}, u32[]{:S(2)}, u32[]{:S(2)}) %all-to-all-start.1) | async-done | bytes 1179680 | tf_op jit(solution)/shard_map/all_to_all | solution.py:184
  22.5 8.2 %all-to-all-start = ((bf16[8,40,1024]{2,1,0:T(8,128)(2,1)}), bf16[8,40,1024]{2,1,0:T(8,128)(2,1)}, u32[]{:S(2)}, u32[]{:S(2)}) async-start(bf16[8,40,1024]{2,1,0:T(8,128)(2,1)} %fusion.11), calls=%async_computation | async-start | bytes 1310720 | tf_op jit(solution)/shard_map/all_to_all | solution.py:172
  30.6 2.0 slice_bitcast_fusion
  32.7 8.9 %all-to-all-done = bf16[8,40,1024]{2,1,0:T(8,128)(2,1)} async-done(((bf16[8,40,1024]{2,1,0:T(8,128)(2,1)}), bf16[8,40,1024]{2,1,0:T(8,128)(2,1)}, u32[]{:S(2)}, u32[]{:S(2)}) %all-to-all-start) | async-done | bytes 655392 | tf_op jit(solution)/shard_map/all_to_all | solution.py:172
  41.7 18.8 %all_to_all.50 = bf16[4,576,256]{2,1,0:T(8,128)(2,1)} all-to-all(bf16[4,576,256]{2,1,0:T(8,128)(2,1)S(1)} %broadcast_in_dim.51), channel_id=1, replica_groups={{0,8,16,24},{4,12,20,28},{32,40,48,56},{36,44,52,60},{64,72,80,88},{68,..., dimensions={0} | all-to-all | bytes 2359296 | tf_op jit(solution)/shard_map/all_to_all | solution.py:172
  61.6 4.3 %all-to-all-start.3 = ((bf16[4,576,256]{2,1,0:T(8,128)(2,1)}), bf16[4,576,256]{2,1,0:T(8,128)(2,1)}, u32[]{:S(2)}, u32[]{:S(2)}) async-start(bf16[4,576,256]{2,1,0:T(8,128)(2,1)} %broadcast_in_dim.53), calls=%async_computation.3 | async-start | bytes 2359296 | tf_op jit(solution)/shard_map/all_to_all | solution.py:172
  65.9 4.4 %collective-permute-start.1 = (bf16[8,40,1024]{2,1,0:T(8,128)(2,1)}, bf16[8,40,1024]{2,1,0:T(8,128)(2,1)}, u32[]{:S(2)}, u32[]{:S(2)}) collective-permute-start(bf16[8,40,1024]{2,1,0:T(8,128)(2,1)} %all-to-all-done), channel_id=1, source_target_pairs={{0,32},{4,36},{8,40},{12,44},{16,48},{20,52},{24,56},{28,60},{32,6... | collective-permute-start | bytes 1966088 | tf_op jit(solution)/shard_map/ppermute | solution.py:168
  70.3 10.3 %all-to-all-done.3 = bf16[4,576,256]{2,1,0:T(8,128)(2,1)} async-done(((bf16[4,576,256]{2,1,0:T(8,128)(2,1)}), bf16[4,576,256]{2,1,0:T(8,128)(2,1)}, u32[]{:S(2)}, u32[]{:S(2)}) %all-to-all-start.3) | async-done | bytes 1179680 | tf_op jit(solution)/shard_map/all_to_all | solution.py:172
  81.7 3.5 %all-to-all-start.4 = ((bf16[4,576,256]{2,1,0:T(8,128)(2,1)}), bf16[4,576,256]{2,1,0:T(8,128)(2,1)S(1)}, u32[]{:S(2)}, u32[]{:S(2)}) async-start(bf16[4,576,256]{2,1,0:T(8,128)(2,1)} %broadcast_in_dim.55), calls=%async_computation.4 | async-start | bytes 2359296 | tf_op jit(solution)/shard_map/all_to_all | solution.py:172
  86.6 4.9 %collective-permute-start = (bf16[40,256]{1,0:T(8,128)(2,1)S(1)}, bf16[40,256]{1,0:T(8,128)(2,1)S(1)}, u32[]{:S(2)}, u32[]{:S(2)}) collective-permute-start(bf16[40,256]{1,0:T(8,128)(2,1)S(1)} %get-tuple-element.94), channel_id=1, source_target_pairs={{0,64},{4,68},{8,72},{12,76},{16,80},{20,84},{24,88},{28,92},{32,9... | collective-permute-start | bytes 61448 | tf_op jit(solution)/shard_map/ppermute | solution.py:168
  94.8 3.0 %collective-permute-start.4 = (bf16[2304,256]{1,0:T(8,128)(2,1)}, bf16[2304,256]{1,0:T(8,128)(2,1)}, u32[]{:S(2)}, u32[]{:S(2)}) collective-permute-start(bf16[2304,256]{1,0:T(8,128)(2,1)} %bitcast.100), channel_id=1, source_target_pairs={{0,4},{4,0},{8,12},{12,8},{16,20},{20,16},{24,28},{28,24},{32,36},... | collective-permute-start | bytes 3538952 | tf_op jit(solution)/shard_map/ppermute | solution.py:202
  97.8 2.0 fusion.31
  99.9 2.1 broadcast_in_dim.57
  102.0 4.5 %all-to-all-start.5 = ((bf16[4,576,256]{2,1,0:T(8,128)(2,1)}), bf16[4,576,256]{2,1,0:T(8,128)(2,1)}, u32[]{:S(2)}, u32[]{:S(2)}) async-start(bf16[4,576,256]{2,1,0:T(8,128)(2,1)} %broadcast_in_dim.57), calls=%async_computation.5 | async-start | bytes 2359296 | tf_op jit(solution)/shard_map/all_to_all | solution.py:172
  106.4 1.9 fusion.32
  112.6 3.6 %collective-permute-start.5 = (bf16[2304,256]{1,0:T(8,128)(2,1)}, bf16[2304,256]{1,0:T(8,128)(2,1)}, u32[]{:S(2)}, u32[]{:S(2)}) collective-permute-start(bf16[2304,256]{1,0:T(8,128)(2,1)} %bitcast.21.wa), channel_id=1, source_target_pairs={{0,4},{4,0},{8,12},{12,8},{16,20},{20,16},{24,28},{28,24},{32,36},... | collective-permute-start | bytes 3538952 | tf_op jit(solution)/shard_map/ppermute | solution.py:202
  117.1 2.2 pad.19.y1
  120.9 3.1 %collective-permute-start.7 = (bf16[2304,256]{1,0:T(8,128)(2,1)}, bf16[2304,256]{1,0:T(8,128)(2,1)S(1)}, u32[]{:S(2)}, u32[]{:S(2)}) collective-permute-start(bf16[2304,256]{1,0:T(8,128)(2,1)} %bitcast.25.wa), channel_id=1, source_target_pairs={{0,4},{4,0},{8,12},{12,8},{16,20},{20,16},{24,28},{28,24},{32,36},... | collective-permute-start | bytes 3538952 | tf_op jit(solution)/shard_map/ppermute | solution.py:202
  129.6 7.6 %block_p8.1 = (bf16[22,32,256]{2,1,0:T(8,128)(2,1)S(1)}, bf16[20,32,256]{2,1,0:T(8,128)(2,1)S(1)}, bf16[18,32,256]{2,1,0:T(8,128)(2,1)S(1)}, bf16[20,32,256]{2,1...) custom-call(s32[3]{0:T(128)S(1)} %pad_add_fusion.meta, ...), custom_call_target="tpu_custom_call" | custom-call | flops 9965666304 | bytes 6291456 | tf_op jit(solution)/shard_map/block_p8/pallas_call | solution.py:112
  137.2 5.8 %block_p6.1 = (bf16[18,32,256]{2,1,0:T(8,128)(2,1)S(1)}, bf16[16,32,256]{2,1,0:T(8,128)(2,1)S(1)}, bf16[14,32,256]{2,1,0:T(8,128)(2,1)S(1)}, bf16[16,32,256]{2,1...) custom-call(s32[3]{0:T(128)S(1)} %pad_add_fusion.meta, ...), custom_call_target="tpu_custom_call" | custom-call | flops 5435817984 | bytes 6291456 | tf_op jit(solution)/shard_map/block_p6/pallas_call | solution.py:112
  143.0 5.2 %block_p4.1 = (bf16[14,32,256]{2,1,0:T(8,128)(2,1)S(1)}, bf16[12,32,256]{2,1,0:T(8,128)(2,1)S(1)}, bf16[10,32,256]{2,1,0:T(8,128)(2,1)S(1)}, bf16[12,32,256]{2,1...) custom-call(s32[3]{0:T(128)S(1)} %pad_add_fusion.meta, ...), custom_call_target="tpu_custom_call" | custom-call | flops 4227858432 | bytes 6291456 | tf_op jit(solution)/shard_map/block_p4/pallas_call | solution.py:112
  148.2 4.6 %block_p2.1 = (bf16[8,16,256]{2,1,0:T(8,128)(2,1)S(1)}, bf16[8,16,256]{2,1,0:T(8,128)(2,1)S(1)}, bf16[8,16,256]{2,1,0:T(8,128)(2,1)S(1)}, bf16[8,16,256]{2,1,0:T...) custom-call(s32[3]{0:T(128)S(1)} %pad_add_fusion.meta, ...), custom_call_target="tpu_custom_call" | custom-call | flops 3019898880 | bytes 6291456 | tf_op jit(solution)/shard_map/block_p2/pallas_call | solution.py:112
  153.2 25.9 %all_to_all.51 = bf16[4,896,256]{2,1,0:T(8,128)(2,1)S(1)} all-to-all(bf16[4,896,256]{2,1,0:T(8,128)(2,1)S(1)} %pad_maximum_fusion), channel_id=1, replica_groups=mesh['rows'=64,'section'=4] {'section'}, dimensions={0} | all-to-all | bytes 3670016 | tf_op jit(solution)/shard_map/all_to_all | solution.py:210
  179.1 2.0 kernel_grads.1
  182.2 2.5 %collective-permute-done.8 = bf16[2304,256]{1,0:T(8,128)(2,1)S(1)} collective-permute-done((bf16[2304,256]{1,0:T(8,128)(2,1)S(1)}, bf16[2304,256]{1,0:T(8,128)(2,1)S(1)}, u32[]{:S(2)}, u32[]{:S(2)}) %collective-permute-start.8) | collective-permute-done | bytes 1179680 | tf_op jit(solution)/shard_map/ppermute | solution.py:212
  185.1 19.4 %all_to_all.52 = bf16[4,576,256]{2,1,0:T(8,128)(2,1)} all-to-all(bf16[4,576,256]{2,1,0:T(8,128)(2,1)S(1)} %bitcast.132), channel_id=1, replica_groups={{0,8,16,24},{4,12,20,28},{32,40,48,56},{36,44,52,60},{64,72,80,88},{68,..., dimensions={0} | all-to-all | bytes 2359296 | tf_op jit(solution)/shard_map/all_to_all | solution.py:172
  204.5 2.2 reduce_sum.21
  206.7 10.8 %all-to-all-start.9 = ((bf16[8,72,256]{2,1,0:T(8,128)(2,1)}), bf16[8,72,256]{2,1,0:T(8,128)(2,1)S(1)}, u32[]{:S(2)}, u32[]{:S(2)}) async-start(bf16[8,72,256]{2,1,0:T(8,128)(2,1)} %bitcast.53), calls=%async_computation.9 | async-start | bytes 589824 | tf_op jit(solution)/shard_map/all_to_all | solution.py:172
  218.3 9.9 %all-to-all-done.9 = bf16[8,72,256]{2,1,0:T(8,128)(2,1)S(1)} async-done(((bf16[8,72,256]{2,1,0:T(8,128)(2,1)}), bf16[8,72,256]{2,1,0:T(8,128)(2,1)S(1)}, u32[]{:S(2)}, u32[]{:S(2)}) %all-to-all-start.9) | async-done | bytes 294944 | tf_op jit(solution)/shard_map/all_to_all | solution.py:172
  228.2 6.2 %all-to-all-start.6 = ((bf16[8,16,1024]{2,1,0:T(8,128)(2,1)}), bf16[8,16,1024]{2,1,0:T(8,128)(2,1)S(1)}, u32[]{:S(2)}, u32[]{:S(2)}) async-start(bf16[8,16,1024]{2,1,0:T(8,128)(2,1)} %pad_maximum_fusion.2), calls=%async_computation.6 | async-start | bytes 524288 | tf_op jit(solution)/shard_map/all_to_all | solution.py:172
  234.7 6.3 %all-to-all-done.6 = bf16[8,16,1024]{2,1,0:T(8,128)(2,1)S(1)} async-done(((bf16[8,16,1024]{2,1,0:T(8,128)(2,1)}), bf16[8,16,1024]{2,1,0:T(8,128)(2,1)S(1)}, u32[]{:S(2)}, u32[]{:S(2)}) %all-to-all-start.6) | async-done | bytes 262176 | tf_op jit(solution)/shard_map/all_to_all | solution.py:172
  (72 shorter events, 31.4 us)
Async XLA Ops:
  0.6 1.7 copy-start
  3.4 5.0 %copy-start.6 = (bf16[1,1,128,512]{3,2,1,0:T(8,128)(2,1)S(1)}, bf16[1,1,128,512]{3,2,1,0:T(8,128)(2,1)}, u32[]{:S(2)}) copy-start(bf16[1,1,128,512]{3,2,1,0:T(8,128)(2,1)} %param.4) | copy-start | bytes 393220
  3.4 5.0 %copy-start.7 = (bf16[1,1,128,512]{3,2,1,0:T(8,128)(2,1)S(1)}, bf16[1,1,128,512]{3,2,1,0:T(8,128)(2,1)}, u32[]{:S(2)}) copy-start(bf16[1,1,128,512]{3,2,1,0:T(8,128)(2,1)} %param.3) | copy-start | bytes 393220
  3.4 19.0 %all-to-all-start.1 = ((bf16[4,576,256]{2,1,0:T(8,128)(2,1)}), bf16[4,576,256]{2,1,0:T(8,128)(2,1)}, u32[]{:S(2)}, u32[]{:S(2)}) async-start(bf16[4,576,256]{2,1,0:T(8,128)(2,1)} %broadcast_in_dim.49), calls=%async_computation.1 | async-start | bytes 2359296 | tf_op jit(solution)/shard_map/all_to_all | solution.py:184
  22.5 19.2 %all-to-all-start = ((bf16[8,40,1024]{2,1,0:T(8,128)(2,1)}), bf16[8,40,1024]{2,1,0:T(8,128)(2,1)}, u32[]{:S(2)}, u32[]{:S(2)}) async-start(bf16[8,40,1024]{2,1,0:T(8,128)(2,1)} %fusion.11), calls=%async_computation | async-start | bytes 1310720 | tf_op jit(solution)/shard_map/all_to_all | solution.py:172
  61.6 19.0 %all-to-all-start.3 = ((bf16[4,576,256]{2,1,0:T(8,128)(2,1)}), bf16[4,576,256]{2,1,0:T(8,128)(2,1)}, u32[]{:S(2)}, u32[]{:S(2)}) async-start(bf16[4,576,256]{2,1,0:T(8,128)(2,1)} %broadcast_in_dim.53), calls=%async_computation.3 | async-start | bytes 2359296 | tf_op jit(solution)/shard_map/all_to_all | solution.py:172
  65.9 32.0 %collective-permute-start.1 = (bf16[8,40,1024]{2,1,0:T(8,128)(2,1)}, bf16[8,40,1024]{2,1,0:T(8,128)(2,1)}, u32[]{:S(2)}, u32[]{:S(2)}) collective-permute-start(bf16[8,40,1024]{2,1,0:T(8,128)(2,1)} %all-to-all-done), channel_id=1, source_target_pairs={{0,32},{4,36},{8,40},{12,44},{16,48},{20,52},{24,56},{28,60},{32,6... | collective-permute-start | bytes 1966088 | tf_op jit(solution)/shard_map/ppermute | solution.py:168
  81.7 18.2 %all-to-all-start.4 = ((bf16[4,576,256]{2,1,0:T(8,128)(2,1)}), bf16[4,576,256]{2,1,0:T(8,128)(2,1)S(1)}, u32[]{:S(2)}, u32[]{:S(2)}) async-start(bf16[4,576,256]{2,1,0:T(8,128)(2,1)} %broadcast_in_dim.55), calls=%async_computation.4 | async-start | bytes 2359296 | tf_op jit(solution)/shard_map/all_to_all | solution.py:172
  86.6 7.6 %collective-permute-start = (bf16[40,256]{1,0:T(8,128)(2,1)S(1)}, bf16[40,256]{1,0:T(8,128)(2,1)S(1)}, u32[]{:S(2)}, u32[]{:S(2)}) collective-permute-start(bf16[40,256]{1,0:T(8,128)(2,1)S(1)} %get-tuple-element.94), channel_id=1, source_target_pairs={{0,64},{4,68},{8,72},{12,76},{16,80},{20,84},{24,88},{28,92},{32,9... | collective-permute-start | bytes 61448 | tf_op jit(solution)/shard_map/ppermute | solution.py:168
  91.6 19.6 %collective-permute-start.3 = (bf16[40,256]{1,0:T(8,128)(2,1)}, bf16[40,256]{1,0:T(8,128)(2,1)}, u32[]{:S(2)}, u32[]{:S(2)}) collective-permute-start(bf16[40,256]{1,0:T(8,128)(2,1)} %get-tuple-element.93), channel_id=1, source_target_pairs={{64,0},{68,4},{72,8},{76,12},{80,16},{84,20},{88,24},{92,28},{96,3... | collective-permute-start | bytes 61448 | tf_op jit(solution)/shard_map/ppermute | solution.py:168
  92.9 16.4 %collective-permute-start.2 = (bf16[8,40,1024]{2,1,0:T(8,128)(2,1)}, bf16[8,40,1024]{2,1,0:T(8,128)(2,1)}, u32[]{:S(2)}, u32[]{:S(2)}) collective-permute-start(bf16[8,40,1024]{2,1,0:T(8,128)(2,1)} %all-to-all-done), channel_id=1, source_target_pairs={{32,0},{36,4},{40,8},{44,12},{48,16},{52,20},{56,24},{60,28},{64,3... | collective-permute-start | bytes 1966088 | tf_op jit(solution)/shard_map/ppermute | solution.py:168
  94.8 29.2 %collective-permute-start.4 = (bf16[2304,256]{1,0:T(8,128)(2,1)}, bf16[2304,256]{1,0:T(8,128)(2,1)}, u32[]{:S(2)}, u32[]{:S(2)}) collective-permute-start(bf16[2304,256]{1,0:T(8,128)(2,1)} %bitcast.100), channel_id=1, source_target_pairs={{0,4},{4,0},{8,12},{12,8},{16,20},{20,16},{24,28},{28,24},{32,36},... | collective-permute-start | bytes 3538952 | tf_op jit(solution)/shard_map/ppermute | solution.py:202
  102.0 18.9 %all-to-all-start.5 = ((bf16[4,576,256]{2,1,0:T(8,128)(2,1)}), bf16[4,576,256]{2,1,0:T(8,128)(2,1)}, u32[]{:S(2)}, u32[]{:S(2)}) async-start(bf16[4,576,256]{2,1,0:T(8,128)(2,1)} %broadcast_in_dim.57), calls=%async_computation.5 | async-start | bytes 2359296 | tf_op jit(solution)/shard_map/all_to_all | solution.py:172
  106.4 9.7 %copy-start.10 = (bf16[8,40,256]{2,1,0:T(8,128)(2,1)S(1)}, bf16[8,40,256]{2,1,0:T(8,128)(2,1)}, u32[]{:S(2)}) copy-start(bf16[8,40,256]{2,1,0:T(8,128)(2,1)} %get-tuple-element.82) | copy-start | bytes 491524
  111.2 8.1 %copy-start.8 = (bf16[8,40,256]{2,1,0:T(8,128)(2,1)S(1)}, bf16[8,40,256]{2,1,0:T(8,128)(2,1)}, u32[]{:S(2)}) copy-start(bf16[8,40,256]{2,1,0:T(8,128)(2,1)} %get-tuple-element.81) | copy-start | bytes 491524
  111.2 8.1 %copy-start.9 = (bf16[8,40,256]{2,1,0:T(8,128)(2,1)S(1)}, bf16[8,40,256]{2,1,0:T(8,128)(2,1)}, u32[]{:S(2)}) copy-start(bf16[8,40,256]{2,1,0:T(8,128)(2,1)} %get-tuple-element.83) | copy-start | bytes 491524
  112.6 24.6 %collective-permute-start.5 = (bf16[2304,256]{1,0:T(8,128)(2,1)}, bf16[2304,256]{1,0:T(8,128)(2,1)}, u32[]{:S(2)}, u32[]{:S(2)}) collective-permute-start(bf16[2304,256]{1,0:T(8,128)(2,1)} %bitcast.21.wa), channel_id=1, source_target_pairs={{0,4},{4,0},{8,12},{12,8},{16,20},{20,16},{24,28},{28,24},{32,36},... | collective-permute-start | bytes 3538952 | tf_op jit(solution)/shard_map/ppermute | solution.py:202
  120.9 22.1 %collective-permute-start.6 = (bf16[2304,256]{1,0:T(8,128)(2,1)S(1)}, bf16[2304,256]{1,0:T(8,128)(2,1)}, u32[]{:S(2)}, u32[]{:S(2)}) collective-permute-start(bf16[2304,256]{1,0:T(8,128)(2,1)S(1)} %bitcast.98), channel_id=1, source_target_pairs={{0,4},{4,0},{8,12},{12,8},{16,20},{20,16},{24,28},{28,24},{32,36},... | collective-permute-start | bytes 3538952 | tf_op jit(solution)/shard_map/ppermute | solution.py:202
  120.9 27.3 %collective-permute-start.7 = (bf16[2304,256]{1,0:T(8,128)(2,1)}, bf16[2304,256]{1,0:T(8,128)(2,1)S(1)}, u32[]{:S(2)}, u32[]{:S(2)}) collective-permute-start(bf16[2304,256]{1,0:T(8,128)(2,1)} %bitcast.25.wa), channel_id=1, source_target_pairs={{0,4},{4,0},{8,12},{12,8},{16,20},{20,16},{24,28},{28,24},{32,36},... | collective-permute-start | bytes 3538952 | tf_op jit(solution)/shard_map/ppermute | solution.py:202
  124.0 1.3 copy-start.1
  125.3 1.1 copy-start.2
  126.4 1.1 copy-start.3
  127.4 1.1 copy-start.4
  128.5 1.0 copy-start.5
  181.1 3.6 %collective-permute-start.8 = (bf16[2304,256]{1,0:T(8,128)(2,1)S(1)}, bf16[2304,256]{1,0:T(8,128)(2,1)S(1)}, u32[]{:S(2)}, u32[]{:S(2)}) collective-permute-start(bf16[2304,256]{1,0:T(8,128)(2,1)S(1)} %get-tuple-element.70), channel_id=1, source_target_pairs={{0,4},{4,0},{8,12},{12,8},{16,20},{20,16},{24,28},{28,24},{32,36},... | collective-permute-start | bytes 3538952 | tf_op jit(solution)/shard_map/ppermute | solution.py:212
  206.7 21.5 %all-to-all-start.9 = ((bf16[8,72,256]{2,1,0:T(8,128)(2,1)}), bf16[8,72,256]{2,1,0:T(8,128)(2,1)S(1)}, u32[]{:S(2)}, u32[]{:S(2)}) async-start(bf16[8,72,256]{2,1,0:T(8,128)(2,1)} %bitcast.53), calls=%async_computation.9 | async-start | bytes 589824 | tf_op jit(solution)/shard_map/all_to_all | solution.py:172
  228.2 12.7 %all-to-all-start.6 = ((bf16[8,16,1024]{2,1,0:T(8,128)(2,1)}), bf16[8,16,1024]{2,1,0:T(8,128)(2,1)S(1)}, u32[]{:S(2)}, u32[]{:S(2)}) async-start(bf16[8,16,1024]{2,1,0:T(8,128)(2,1)} %pad_maximum_fusion.2), calls=%async_computation.6 | async-start | bytes 524288 | tf_op jit(solution)/shard_map/all_to_all | solution.py:172
  234.5 7.2 %collective-permute-start.9 = (f32[36,256]{1,0:T(8,128)S(1)}, f32[36,256]{1,0:T(8,128)S(1)}, u32[]{:S(2)}, u32[]{:S(2)}) collective-permute-start(f32[36,256]{1,0:T(8,128)S(1)} %get-tuple-element.98), channel_id=1, source_target_pairs={{0,4},{4,0},{8,12},{12,8},{16,20},{20,16},{24,28},{28,24},{32,36},... | collective-permute-start | bytes 110600 | tf_op jit(solution)/shard_map/ppermute | solution.py:218

commit v2 on v0

v2 whole, which is shorter than its diff:
```python
import math

import jax
import jax.numpy as jnp
from jax import lax
from jax.experimental import pallas as pl
from jax.experimental.pallas import tpu as pltpu
from jax.sharding import Mesh
from jax.sharding import PartitionSpec as P

C = 256
W = 32
WIDE = 48
PIECE = WIDE + 3 * W
QUARTER = 576
SPAN = 18
VMEM = pl.BlockSpec(memory_space=pltpu.VMEM)
SMEM = pl.BlockSpec(memory_space=pltpu.SMEM)
HBM = pl.BlockSpec(memory_space=pltpu.HBM)
PARAMS = pltpu.CompilerParams(vmem_limit_bytes=24 * 1024 * 1024)
f32, bf16 = jnp.float32, jnp.bfloat16


def row_chunks(rows, most=8):
    count = -(-rows // most)
    base, extra = divmod(rows, count)
    out, at = [], 0
    for i in range(count):
        size = base + (1 if i < extra else 0)
        out.append((at, size))
        at += size
    return out


def pieces_kernel(field, cotangent, out, padded):
    padded[0:16] = jnp.zeros((16, 4 * C), f32)
    padded[144:160] = jnp.zeros((16, 4 * C), f32)
    padded[16:144, 0:2 * C] = field[...].astype(f32)
    padded[16:144, 2 * C:4 * C] = cotangent[...].astype(f32)
    for j in range(8):
        out[j, 0:WIDE] = padded[16 * j:16 * j + WIDE, 0:C].astype(bf16)
        for i in range(1, 4):
            at = WIDE + (i - 1) * W
            out[j, at:at + W] = padded[16 * j + 8:16 * j + 8 + W, i * C:(i + 1) * C].astype(bf16)


def make_pieces(field, cotangent):
    return pl.pallas_call(
        pieces_kernel,
        out_shape=jax.ShapeDtypeStruct((8, PIECE, C), bf16),
        in_specs=[VMEM, VMEM],
        out_specs=VMEM,
        scratch_shapes=[pltpu.VMEM((160, 4 * C), f32)],
        compiler_params=PARAMS,
        name="pieces",
    )(field, cotangent)


def blocks_kernel(meta, above, tile, below, far_above, far_below, held, one, one2, three, three2, *refs):
    quarters, (done, acts, w, s1a, s1b, s2a, s2b, s3, s4, t1a, t1b, n2a, n2b, packed, sent, sems) = refs[:8], refs[8:]
    core, rowbase, place, section, y = (meta[i] for i in range(5))
    colbase = 16 * place

    def kernel_copy(k, branch, src, at=0):
        size = src.shape[0]
        return pltpu.make_async_copy(src, w.at[k, branch, pl.ds(at, size)], sems.at[2 * k + jnp.where(branch == core, 0, 1)])

    for k in (3, 2, 1, 0):
        ahead = lax.rem(k + 4 - section, 4)

        @pl.when(ahead == 0)
        def _():
            kernel_copy(k, core, held.at[core]).start()
            kernel_copy(k, 1 - core, held.at[1 - core]).start()

        @pl.when(ahead == 1)
        def _():
            kernel_copy(k, core, one).start()
            kernel_copy(k, 1 - core, one2).start()

        @pl.when(ahead == 3)
        def _():
            kernel_copy(k, core, three).start()
            kernel_copy(k, 1 - core, three2).start()

        @pl.when(ahead == 2)
        def _():
            for d in range(4):
                at = pl.multiple_of(lax.rem(y + 4 - d, 4) * QUARTER, QUARTER)
                kernel_copy(k, core, quarters[d], at).start()
                kernel_copy(k, 1 - core, quarters[4 + d], at).start()

    def put(buf, at, mid, left, right):
        n = mid.shape[0]
        rows = slice(at * W, (at + n) * W)
        buf[rows, 0:C] = left.reshape(n * W, C).astype(bf16)
        buf[rows, C:2 * C] = mid.reshape(n * W, C).astype(bf16)
        buf[rows, 2 * C:3 * C] = right.reshape(n * W, C).astype(bf16)

    def spread(buf, at, value):
        n, wide = value.shape[0], value.shape[1]
        flat = value.reshape(n * wide, C)
        left = pltpu.roll(flat, 1, 0).reshape(n, wide, C)
        right = pltpu.roll(flat, n * wide - 1, 0).reshape(n, wide, C)
        cut = (wide - W) // 2
        put(buf, at, *(v[:, cut:cut + W] for v in (value, left, right)))

    def inside(a, n, halo):
        r = lax.broadcasted_iota(jnp.int32, (n, W, 1), 0) + (rowbase - halo + a)
        c = lax.broadcasted_iota(jnp.int32, (n, W, 1), 1) + (colbase - 8)
        return (r >= 0) & (r < 64) & (c >= 0) & (c < 128)

    def conv(buf, a, n, k, branch):
        acc = None
        for dr in range(3):
            d = jnp.dot(buf[(a + dr) * W:(a + dr + n) * W, :], w[k, branch, 768 * dr:768 * (dr + 1), :],
                        preferred_element_type=f32)
            acc = d if acc is None else acc + d
        return acc.reshape(n, W, C)

    def conv_t(buf, a, n, k, branch):
        acc = None
        for dr in range(3):
            for dc in range(3):
                tap = 3 * dr + dc
                d = lax.dot_general(buf[(a + 2 - dr) * W:(a + 2 - dr + n) * W, (2 - dc) * C:(3 - dc) * C],
                                    w[k, branch, 256 * tap:256 * (tap + 1), :],
                                    (((1,), (1,)), ((), ())), preferred_element_type=f32)
                acc = d if acc is None else acc + d
        return acc.reshape(n, W, C)

    def window(lo, hi, a, n, halo):
        parts, at = [], a - halo
        while at < a - halo + n:
            if at < -8:
                part, took = far_above[lo:hi][None], 1
            elif at >= 16:
                part, took = far_below[lo:hi][None], 1
            else:
                ref, base = ((above, -8), (tile, 0), (below, 8))[0 if at < 0 else 1 if at < 8 else 2]
                took = min(a - halo + n, base + 8) - at
                part = ref[at - base:at - base + took, lo:hi]
            parts.append(part.astype(f32))
            at += took
        return parts[0] if len(parts) == 1 else jnp.concatenate(parts, axis=0)

    def lanes(buf, a, n):
        return buf[a * W:(a + n) * W, C:2 * C].astype(f32).reshape(n, W, C)

    def finish(which, value, a, n, halo):
        lo, hi = max(a, halo), min(a + n, halo + 8)
        for i in range(lo, hi):
            at = lax.rem(i - halo + 8 - place, 8)
            done[at, :, which * C:(which + 1) * C] = value[i - a, 8:24].astype(bf16)

    for a, n in row_chunks(26):
        spread(s1a, a, window(0, WIDE, a, n, 9))
    for k, p in ((3, 8), (2, 6), (1, 4), (0, 2)):
        first, last = k == 3, k == 0
        s1, s1n = (s1a, s1b) if k % 2 else (s1b, s1a)
        s2, s2o = (s2a, s2b) if k % 2 else (s2b, s2a)
        t1n, t1o = (t1a, t1b) if k % 2 else (t1b, t1a)
        n2n, n2o = (n2a, n2b) if k % 2 else (n2b, n2a)

        def old_y2(a, n):
            return window(WIDE, WIDE + W, a, n, p) if first else lanes(s2o, a + 2, n)

        def old_g1(a, n):
            return window(WIDE + W, WIDE + 2 * W, a, n, p - 1) if first else t1o[a + 2:a + 2 + n].astype(f32)

        def old_g2(a, n):
            return window(WIDE + 2 * W, WIDE + 3 * W, a, n, p) if first else n2o[a:a + n].astype(f32)

        kernel_copy(k, core, held.at[0]).wait()
        kernel_copy(k, 1 - core, held.at[0]).wait()
        for a, n in row_chunks(8 + 2 * p):
            pre = conv(s1, a, n, k, 1)
            sig = jax.nn.sigmoid(pre)
            x2 = jnp.where(inside(a, n, p), old_y2(a, n) - pre * sig, 0.0)
            x2 = x2.astype(bf16).astype(f32)
            spread(s2, a, x2)
            if last:
                finish(1, x2, a, n, p)
            dg = old_g2(a, n) * (sig * (1.0 + pre * (1.0 - sig)))
            spread(s3, a, dg.astype(bf16).astype(f32))
        for a, n in row_chunks(6 + 2 * p):
            pre = conv(s2, a, n, k, 0)
            sig = jax.nn.sigmoid(pre)
            m = inside(a, n, p - 1)
            x1 = jnp.where(m, lanes(s1, a + 2, n) - pre * sig, 0.0)
            t1 = jnp.where(m, old_g1(a, n) + conv_t(s3, a, n, k, 1), 0.0)
            t1 = t1.astype(bf16).astype(f32)
            df = t1 * (sig * (1.0 + pre * (1.0 - sig)))
            spread(s4, a, df.astype(bf16).astype(f32))
            if last:
                finish(0, x1, a, n, p - 1)
                finish(2, t1, a, n, p - 1)
            else:
                spread(s1n, a, x1.astype(bf16).astype(f32))
                t1n[a:a + n] = t1.astype(bf16)
        for a, n in row_chunks(4 + 2 * p):
            n2 = jnp.where(inside(a, n, p - 2), old_g2(a + 2, n) + conv_t(s4, a, n, k, 0), 0.0)
            if last:
                finish(3, n2, a, n, p - 2)
            else:
                n2n[a:a + n] = n2.astype(bf16)

        for branch, src, h, delta, hd in ((0, s2, p, s4, p - 1), (1, s1, p + 1, s3, p)):
            for i in range(10):
                v = src[(h - 1 + i) * W:(h + i) * W, 0:C].astype(f32)
                packed[SPAN * i:SPAN * i + 24] = v[8:32]
            sent[4 * branch + k, 0:192] = packed[0:192].astype(bf16)
            d = lanes(delta, hd, 8)[:, 8:24]
            sent[4 * branch + k, 192:320] = d.reshape(128, C).astype(bf16)
            pltpu.make_async_copy(sent.at[4 * branch + k], acts.at[4 * branch + k], sems.at[8 + 4 * branch + k]).start()
    for i in range(8):
        pltpu.make_async_copy(sent.at[i], acts.at[i], sems.at[8 + i]).wait()


def blocks(meta, fields, kernels):
    def spread(rows):
        return pltpu.VMEM((rows * W, 3 * C), bf16)

    def plain(rows):
        return pltpu.VMEM((rows, W, C), bf16)

    flops = sum(2 * 2304 * 256 * W * (4 * (8 + 2 * p) - 12) for p in (8, 6, 4, 2))
    return pl.pallas_call(
        blocks_kernel,
        out_shape=[jax.ShapeDtypeStruct((8, 16, 4 * C), bf16), jax.ShapeDtypeStruct((8, 320, C), bf16)],
        in_specs=[SMEM] + [VMEM] * 5 + [HBM] * len(kernels),
        out_specs=[VMEM, HBM],
        scratch_shapes=[pltpu.VMEM((4, 2, 2304, C), bf16), spread(26), spread(22), spread(24), spread(20), spread(24), spread(22),
                        plain(22), plain(18), plain(20), plain(16),
                        pltpu.VMEM((192, C), f32), pltpu.VMEM((8, 320, C), bf16), pltpu.SemaphoreType.DMA((16,))],
        compiler_params=pltpu.CompilerParams(vmem_limit_bytes=56 * 1024 * 1024),
        cost_estimate=pl.CostEstimate(flops=flops, bytes_accessed=16 * 1024 * 1024, transcendentals=0),
        name="blocks",
    )(meta, *fields, *kernels)


def grad_kernel(acts, out, lhs, packed, grad):
    for m in range(8):
        packed[0:192] = acts[m, 0:192].astype(f32)
        for i in range(10):
            for dc in range(3):
                v = packed[SPAN * i + dc:SPAN * i + dc + 16, :].astype(bf16)
                for dr in range(3):
                    if 0 <= i - dr < 8:
                        at, t = m * 128 + (i - dr) * 16, 3 * dr + dc
                        lhs[at:at + 16, t * C:(t + 1) * C] = v
    d = jnp.concatenate([acts[m, 192:320] for m in range(8)], axis=0)
    for t in range(9):
        grad[t * C:(t + 1) * C, :] = lax.dot_general(
            lhs[:, t * C:(t + 1) * C], d, (((0,), (0,)), ((), ())), preferred_element_type=f32)
    for z in range(8):
        for y in range(4):
            at = (4 * z + y) * 72
            out[y, z] = grad[at:at + 72].astype(bf16)


def kernel_grads(acts):
    return pl.pallas_call(
        grad_kernel,
        out_shape=jax.ShapeDtypeStruct((4, 8, 72, C), bf16),
        in_specs=[VMEM],
        out_specs=VMEM,
        scratch_shapes=[pltpu.VMEM((1024, 2304), bf16), pltpu.VMEM((192, C), f32), pltpu.VMEM((2304, C), f32)],
        compiler_params=PARAMS,
        cost_estimate=pl.CostEstimate(flops=2 * 1024 * 2304 * 256, bytes_accessed=8 * 1024 * 1024, transcendentals=0),
        name="kernel_grads",
    )(acts)


def shift(value, axis, by):
    size = lax.axis_size(axis)
    return lax.ppermute(value, axis, [(i, i + by) for i in range(size) if 0 <= i + by < size])


def turn(value, axis, by):
    size = lax.axis_size(axis)
    return lax.ppermute(value, axis, [(i, (i + by) % size) for i in range(size)])


def around(value, by):
    return lax.ppermute(value, ("y", "core"), [(i, (i + by) % 8) for i in range(8)])


def unpack_kernel(meta, *refs):
    place = meta[2]
    for d in range(8):
        at = pl.multiple_of(lax.rem(place + 8 - d, 8) * 16, 16)
        refs[8][pl.ds(at, 16), :] = refs[d][:, 0:2 * C]
        refs[9][pl.ds(at, 16), :] = refs[d][:, 2 * C:4 * C]


def unpack(meta, back):
    return pl.pallas_call(
        unpack_kernel,
        out_shape=[jax.ShapeDtypeStruct((128, 2 * C), bf16)] * 2,
        in_specs=[SMEM] + [VMEM] * 8,
        out_specs=[VMEM] * 2,
        compiler_params=PARAMS,
        name="unpack",
    )(meta, *back)


def local(block_out, out_grad, weights):
    z, y, core, section = (lax.axis_index(a) for a in ("z", "y", "core", "section"))
    meta = jnp.stack([core, 8 * z, 2 * y + core, section, y]).astype(jnp.int32)

    own = lax.dynamic_index_in_dim(weights[0], core, 0, keepdims=False)
    part = turn(lax.dynamic_slice_in_dim(own, QUARTER * y, QUARTER, 0), "section", 2)
    one, three = turn(own, "section", -1), turn(own, "section", 1)

    tile = lax.all_to_all(make_pieces(block_out[0, 0], out_grad[0, 0]), ("y", "core"), 0, 0)
    far = (shift(tile[7, :WIDE], "z", 2), shift(tile[0, :WIDE], "z", -2))
    near = (shift(tile, "z", 1), shift(tile, "z", -1))
    quarters = [part] + [turn(part, "y", d) for d in (1, 2, 3)]

    far, near, one, three, quarters = lax.optimization_barrier((far, near, one, three, quarters))
    others = [turn(v, "core", 1) for v in (one, three, *quarters)]
    fields = (near[0], tile, near[1], *far)
    done, acts = blocks(meta, fields, (weights[0], one, others[0], three, others[1], *quarters, *others[2:]))

    back = [done[0]] + [around(done[d], d) for d in range(1, 8)]
    got = lax.all_to_all(acts, ("core", "section"), 0, 0)
    got, back = lax.optimization_barrier((got, back))
    grad = kernel_grads(got)
    restored, input_grad = unpack(meta, back)
    grad = lax.all_to_all(grad, "y", 0, 0).astype(f32).sum(axis=0).astype(bf16)
    grad = lax.all_to_all(grad, "z", 0, 0).astype(f32).sum(axis=0)
    here = lax.dynamic_slice_in_dim(grad, 36 * core, 36, 0)
    there = turn(lax.dynamic_slice_in_dim(grad, 36 * (1 - core), 36, 0), "core", 1)
    grad = jnp.where(core == 0, jnp.stack([here, there]), jnp.stack([there, here]))
    return restored[None, None], input_grad[None, None], (grad * (1.0 / math.sqrt(32768)))[None]


def solution(mesh):
    fine = Mesh(mesh.devices.reshape(8, 4, 2, 4), ("z", "y", "core", "section"))
    rows = ("z", "y", "core")
    spec = P("section", rows, None, None)
    return jax.shard_map(
        local,
        mesh=fine,
        in_specs=(spec, spec, P("section", None, None, None)),
        out_specs=(spec, spec, P("section", None, rows, None)),
        check_vma=False,
    )
```

time: 668 us -> 147 us (0.22)
  waiting for transfers between devices: 336 us -> 48.6 us
  starting transfers between devices: 217 us -> 47.5 us
  matrix products: 34.9 us -> 0 us
  Pallas kernels: 0 us -> 22.4 us
  local copies, waits for them, and re-layouts: 26.8 us -> 7.37 us
  between operations: 18.6 us -> 0.85 us
  other arithmetic: 8.63 us -> 0.99 us
    unnamed x3 -> x0, waiting for transfers between devices: 200 us -> none
    ppermute x62 -> x24, starting transfers between devices: 217 us -> 34.6 us  [the longest x13 17.4 us: turn(): lax.ppermute(value, axis, [(i, (i + by) % size) for i in range(size)])]
    psum x1 -> x0, waiting for transfers between devices: 83 us -> none  [broadcast(): return lax.psum(block, axis)]
    dot_general x42 -> x0, matrix products: 34.9 us -> none  [the longest x7 17.1 us: block_backward(): lax.dot_general(taps_second, delta_f, (((0,), (0,)), ((), ())), preferred...]
    ppermute x62 -> x24, waiting for transfers between devices: 53 us -> 25.4 us  [the longest x4 13.6 us: shift(): lax.ppermute(value, axis, [(i, i + by) for i in range(size) if 0 <= i + b...]
    all_gather x2 -> x0, blocking collectives: 23.5 us -> none  [the longest x1 12.5 us: local(): lax.all_gather(out_grad, 'section', axis=0, tiled=True)]
    all_to_all x0 -> x3, waiting for transfers between devices: none -> 23.2 us  [the longest x1 9.74 us: local(): grad = lax.all_to_all(grad, 'z', 0, 0).astype(f32).sum(axis=0)]
    pallas_call x0 -> x4, Pallas kernels: none -> 22.4 us  [the longest x1 18.6 us: blocks(): pl.pallas_call(blocks_kernel, out_shape=[jax.ShapeDtypeStruct((8, 16, 4 *...]
  transfers between devices with their start and end apart: 64 -> 27, of which waited for: 23 -> 14; matrix products, arithmetic and copies ran while one was open for 7% -> 1% of each run, Pallas kernels for 0% -> 1%
where the time goes in v2:
time: 147 us; the launch traced here: 146 us
  waiting for transfers between devices  48.6 us (33%)
  starting transfers between devices  47.5 us (32%)
  Pallas kernels  22.4 us (15%)
  blocking collectives  18.7 us (13%)
  local copies, waits for them, and re-layouts  7.37 us (5%)
    all_to_all x1, blocking collectives, local(): grad = lax.all_to_all(grad, 'y', 0, 0).astype(f32).sum(axis=0).astype(bf16)  18.7 us
    pallas_call x1, Pallas kernels, blocks(): pl.pallas_call(blocks_kernel, out_shape=[jax.ShapeDtypeStruct((8, 16, 4 *...  18.6 us
    ppermute x13, starting transfers between devices, turn(): lax.ppermute(value, axis, [(i, (i + by) % size) for i in range(size)])  17.4 us
    ppermute x4, waiting for transfers between devices, shift(): lax.ppermute(value, axis, [(i, i + by) for i in range(size) if 0 <= i + b...  13.6 us
    ppermute x4, starting transfers between devices, shift(): lax.ppermute(value, axis, [(i, i + by) for i in range(size) if 0 <= i + b...  10.1 us
    all_to_all x1, waiting for transfers between devices, local(): grad = lax.all_to_all(grad, 'z', 0, 0).astype(f32).sum(axis=0)  9.74 us
    ppermute x13, waiting for transfers between devices, turn(): lax.ppermute(value, axis, [(i, (i + by) % size) for i in range(size)])  8.66 us
    all_to_all x1, waiting for transfers between devices, local(): got = lax.all_to_all(acts, ('core', 'section'), 0, 0)  7.52 us
  transfers between devices with their start and end apart: 27, of which 14 were waited for; matrix products, arithmetic and copies ran while one was open for 1% of the time, Pallas kernels for 1%

profile of v2, /device:TPU:1, one launch (start us, length us, event | category | flops | bytes accessed | tf_op | source)
XLA Modules:
  0.0 146.5 jit_solution(7973121394911305537)
XLA Ops:
  0.6 1.0 dynamic-slice_bitcast_fusion.1
  1.7 3.7 %collective-permute-start.6 = (bf16[576,256]{1,0:T(8,128)(2,1)S(1)}, bf16[576,256]{1,0:T(8,128)(2,1)S(1)}, u32[]{:S(2)}, u32[]{:S(2)}) collective-permute-start(bf16[576,256]{1,0:T(8,128)(2,1)S(1)} %dynamic-slice_bitcast_fusion.1), channel_id=1, source_target_pairs={{0,2},{1,3},{2,0},{3,1},{4,6},{5,7},{6,4},{7,5},{8,10},{9,11},{10,... | collective-permute-start | bytes 884744 | tf_op jit(solution)/shard_map/ppermute | solution.py:282
  8.0 5.4 %all-to-all-start = ((bf16[8,144,256]{2,1,0:T(8,128)(2,1)}), bf16[8,144,256]{2,1,0:T(8,128)(2,1)S(1)}, u32[]{:S(2)}, u32[]{:S(2)}) async-start(bf16[8,144,256]{2,1,0:T(8,128)(2,1)} %pieces.1), calls=%async_computation | async-start | bytes 1179648 | tf_op jit(solution)/shard_map/all_to_all | solution.py:316
  13.5 1.3 dynamic-slice_bitcast_fusion
  14.8 0.9 collective-permute-start.4
  16.3 1.4 collective-permute-start.7
  17.7 5.9 %all-to-all-done.tile = bf16[8,144,256]{2,1,0:T(8,128)(2,1)S(1)} async-done(((bf16[8,144,256]{2,1,0:T(8,128)(2,1)}), bf16[8,144,256]{2,1,0:T(8,128)(2,1)S(1)}, u32[]{:S(2)}, u32[]{:S(2)}) %all-to-all-start) | async-done | bytes 589856 | tf_op jit(solution)/shard_map/all_to_all | solution.py:316
  23.7 4.9 %collective-permute-start = (bf16[48,256]{1,0:T(8,128)(2,1)S(1)}, bf16[48,256]{1,0:T(8,128)(2,1)S(1)}, u32[]{:S(2)}, u32[]{:S(2)}) collective-permute-start(bf16[48,256]{1,0:T(8,128)(2,1)S(1)} %get-tuple-element.56), channel_id=1, source_target_pairs={{0,64},{32,96},{64,128},{96,160},{128,192},{160,224},{1,65},{33,97... | collective-permute-start | bytes 73736 | tf_op jit(solution)/shard_map/ppermute | solution.py:277
  28.6 1.3 collective-permute-start.1
  30.5 5.8 %collective-permute-done.1.far_below = bf16[48,256]{1,0:T(8,128)(2,1)} collective-permute-done((bf16[48,256]{1,0:T(8,128)(2,1)S(1)}, bf16[48,256]{1,0:T(8,128)(2,1)}, u32[]{:S(2)}, u32[]{:S(2)}) %collective-permute-start.1) | collective-permute-done | bytes 24608 | tf_op jit(solution)/shard_map/ppermute | solution.py:277
  36.3 2.7 %collective-permute-start.2 = (bf16[8,144,256]{2,1,0:T(8,128)(2,1)S(1)}, bf16[8,144,256]{2,1,0:T(8,128)(2,1)S(1)}, u32[]{:S(2)}, u32[]{:S(2)}) collective-permute-start(bf16[8,144,256]{2,1,0:T(8,128)(2,1)S(1)} %all-to-all-done.tile), channel_id=1, source_target_pairs={{0,32},{32,64},{64,96},{96,128},{128,160},{160,192},{192,224},{1,3... | collective-permute-start | bytes 1769480 | tf_op jit(solution)/shard_map/ppermute | solution.py:277
  39.0 1.3 collective-permute-start.3
  41.2 5.3 %collective-permute-done.9.refs_3_ = bf16[576,256]{1,0:T(8,128)(2,1)} collective-permute-done((bf16[576,256]{1,0:T(8,128)(2,1)S(1)}, bf16[576,256]{1,0:T(8,128)(2,1)}, u32[]{:S(2)}, u32[]{:S(2)}) %collective-permute-start.9) | collective-permute-done | bytes 294944 | tf_op jit(solution)/shard_map/ppermute | solution.py:282
  46.5 2.8 %collective-permute-done.2.above = bf16[8,144,256]{2,1,0:T(8,128)(2,1)S(1)} collective-permute-done((bf16[8,144,256]{2,1,0:T(8,128)(2,1)S(1)}, bf16[8,144,256]{2,1,0:T(8,128)(2,1)S(1)}, u32[]{:S(2)}, u32[]{:S(2)}) %collective-permute-start.2) | collective-permute-done | bytes 589856 | tf_op jit(solution)/shard_map/ppermute | solution.py:277
  49.4 4.9 %collective-permute-done.3.below = bf16[8,144,256]{2,1,0:T(8,128)(2,1)S(1)} collective-permute-done((bf16[8,144,256]{2,1,0:T(8,128)(2,1)S(1)}, bf16[8,144,256]{2,1,0:T(8,128)(2,1)S(1)}, u32[]{:S(2)}, u32[]{:S(2)}) %collective-permute-start.3) | collective-permute-done | bytes 589856 | tf_op jit(solution)/shard_map/ppermute | solution.py:277
  54.3 3.8 %collective-permute-start.10 = (bf16[2304,256]{1,0:T(8,128)(2,1)S(1)}, bf16[2304,256]{1,0:T(8,128)(2,1)S(1)}, u32[]{:S(2)}, u32[]{:S(2)}) collective-permute-start(bf16[2304,256]{1,0:T(8,128)(2,1)S(1)} %collective-permute-done.4.one), channel_id=1, source_target_pairs={{0,4},{4,0},{1,5},{5,1},{2,6},{6,2},{3,7},{7,3},{8,12},{12,8},{9,1... | collective-permute-start | bytes 3538952 | tf_op jit(solution)/shard_map/ppermute | solution.py:282
  59.4 2.5 %collective-permute-done.12.refs_4_ = bf16[576,256]{1,0:T(8,128)(2,1)S(1)} collective-permute-done((bf16[576,256]{1,0:T(8,128)(2,1)S(1)}, bf16[576,256]{1,0:T(8,128)(2,1)S(1)}, u32[]{:S(2)}, u32[]{:S(2)}) %collective-permute-start.12) | collective-permute-done | bytes 294944 | tf_op jit(solution)/shard_map/ppermute | solution.py:282
  64.5 1.0 copy-done.6
  65.5 18.6 %blocks.1 = (bf16[8,16,1024]{2,1,0:T(8,128)(2,1)}, bf16[8,320,256]{2,1,0:T(8,128)(2,1)}) custom-call(s32[5]{0:T(128)} %stack.37.meta, bf16[8,144,256]{2,1,0:T(8,128)(2,1)} %copy-done.7, bf16[8,144,256]{2,1,0:T(8,128)(2,1)} %copy-done.3, bf16[8,144,256]{2,1,0:T(8,128)(2,1)} %copy-done.8, bf16[48,256]{1,0:T(8,128)(2,1)} %copy-done.12, ...), custom_call_target="tpu_custom_call" | custom-call | flops 9059696640 | bytes 16777216 | tf_op jit(solution)/shard_map/blocks/pallas_call | solution.py:228
  84.1 4.0 %all-to-all-start.1 = ((bf16[8,320,256]{2,1,0:T(8,128)(2,1)}), bf16[8,320,256]{2,1,0:T(8,128)(2,1)S(1)}, u32[]{:S(2)}, u32[]{:S(2)}) async-start(bf16[8,320,256]{2,1,0:T(8,128)(2,1)} %get-tuple-element.36), calls=%async_computation.1 | async-start | bytes 2621440 | tf_op jit(solution)/shard_map/all_to_all | solution.py:327
  88.6 2.3 %collective-permute-start.18 = (bf16[16,1024]{1,0:T(8,128)(2,1)S(1)}, bf16[16,1024]{1,0:T(8,128)(2,1)S(1)}, u32[]{:S(2)}, u32[]{:S(2)}) collective-permute-start(bf16[16,1024]{1,0:T(8,128)(2,1)S(1)} %get-tuple-element.61), channel_id=1, source_target_pairs={{0,12},{4,16},{8,20},{12,24},{16,28},{20,0},{24,4},{28,8},{1,13},{... | collective-permute-start | bytes 98312 | tf_op jit(solution)/shard_map/ppermute | solution.py:286
  90.9 1.3 collective-permute-start.19
  92.2 2.5 %collective-permute-start.20 = (bf16[16,1024]{1,0:T(8,128)(2,1)S(1)}, bf16[16,1024]{1,0:T(8,128)(2,1)S(1)}, u32[]{:S(2)}, u32[]{:S(2)}) collective-permute-start(bf16[16,1024]{1,0:T(8,128)(2,1)S(1)} %get-tuple-element.59), channel_id=1, source_target_pairs={{0,20},{4,24},{8,28},{12,0},{16,4},{20,8},{24,12},{28,16},{1,21},{... | collective-permute-start | bytes 98312 | tf_op jit(solution)/shard_map/ppermute | solution.py:286
  95.7 1.7 %collective-permute-done.20.refs_5_ = bf16[16,1024]{1,0:T(8,128)(2,1)S(1)} collective-permute-done((bf16[16,1024]{1,0:T(8,128)(2,1)S(1)}, bf16[16,1024]{1,0:T(8,128)(2,1)S(1)}, u32[]{:S(2)}, u32[]{:S(2)}) %collective-permute-start.20) | collective-permute-done | bytes 32800 | tf_op jit(solution)/shard_map/ppermute | solution.py:286
  98.4 7.5 %all-to-all-done.1.acts = bf16[8,320,256]{2,1,0:T(8,128)(2,1)S(1)} async-done(((bf16[8,320,256]{2,1,0:T(8,128)(2,1)}), bf16[8,320,256]{2,1,0:T(8,128)(2,1)S(1)}, u32[]{:S(2)}, u32[]{:S(2)}) %all-to-all-start.1) | async-done | bytes 1310752 | tf_op jit(solution)/shard_map/all_to_all | solution.py:327
  105.9 1.7 %kernel_grads.1 = bf16[4,8,72,256]{3,2,1,0:T(8,128)(2,1)S(1)} custom-call(bf16[8,320,256]{2,1,0:T(8,128)(2,1)S(1)} %all-to-all-done.1.acts), custom_call_target="tpu_custom_call" | custom-call | flops 1207959552 | bytes 8388608 | tf_op jit(solution)/shard_map/kernel_grads/pallas_call | solution.py:263
  107.6 18.7 %all_to_all.20 = bf16[4,8,72,256]{3,2,1,0:T(8,128)(2,1)S(1)} all-to-all(bf16[4,8,72,256]{3,2,1,0:T(8,128)(2,1)S(1)} %kernel_grads.1), channel_id=1, replica_groups=mesh['z'=8,'y'=4,'core'=2,'section'=4] {'y'}, dimensions={0} | all-to-all | bytes 2359296 | tf_op jit(solution)/shard_map/all_to_all | solution.py:331
  126.3 0.9 reduce_sum.21
  127.3 3.6 %all-to-all-start.3 = ((bf16[8,72,256]{2,1,0:T(8,128)(2,1)}), bf16[8,72,256]{2,1,0:T(8,128)(2,1)S(1)}, u32[]{:S(2)}, u32[]{:S(2)}) async-start(bf16[8,72,256]{2,1,0:T(8,128)(2,1)} %reduce_sum.21), calls=%async_computation.3 | async-start | bytes 589824 | tf_op jit(solution)/shard_map/all_to_all | solution.py:332
  130.8 9.7 %all-to-all-done.3 = bf16[8,72,256]{2,1,0:T(8,128)(2,1)S(1)} async-done(((bf16[8,72,256]{2,1,0:T(8,128)(2,1)}), bf16[8,72,256]{2,1,0:T(8,128)(2,1)S(1)}, u32[]{:S(2)}, u32[]{:S(2)}) %all-to-all-start.3) | async-done | bytes 294944 | tf_op jit(solution)/shard_map/all_to_all | solution.py:332
  140.6 3.9 %collective-permute-start.23 = (f32[36,256]{1,0:T(8,128)S(1)}, f32[36,256]{1,0:T(8,128)S(1)}, u32[]{:S(2)}, u32[]{:S(2)}) collective-permute-start(f32[36,256]{1,0:T(8,128)S(1)} %get-tuple-element.66), channel_id=1, source_target_pairs={{0,4},{4,0},{1,5},{5,1},{2,6},{6,2},{3,7},{7,3},{8,12},{12,8},{9,1... | collective-permute-start | bytes 110600 | tf_op jit(solution)/shard_map/ppermute | solution.py:282
  144.5 1.3 unpack.1
  (63 shorter events, 12.1 us)
Async XLA Ops:
  1.7 14.7 %collective-permute-start.6 = (bf16[576,256]{1,0:T(8,128)(2,1)S(1)}, bf16[576,256]{1,0:T(8,128)(2,1)S(1)}, u32[]{:S(2)}, u32[]{:S(2)}) collective-permute-start(bf16[576,256]{1,0:T(8,128)(2,1)S(1)} %dynamic-slice_bitcast_fusion.1), channel_id=1, source_target_pairs={{0,2},{1,3},{2,0},{3,1},{4,6},{5,7},{6,4},{7,5},{8,10},{9,11},{10,... | collective-permute-start | bytes 884744 | tf_op jit(solution)/shard_map/ppermute | solution.py:282
  8.0 15.7 %all-to-all-start = ((bf16[8,144,256]{2,1,0:T(8,128)(2,1)}), bf16[8,144,256]{2,1,0:T(8,128)(2,1)S(1)}, u32[]{:S(2)}, u32[]{:S(2)}) async-start(bf16[8,144,256]{2,1,0:T(8,128)(2,1)} %pieces.1), calls=%async_computation | async-start | bytes 1179648 | tf_op jit(solution)/shard_map/all_to_all | solution.py:316
  14.8 39.5 %collective-permute-start.4 = (bf16[2304,256]{1,0:T(8,128)(2,1)S(1)}, bf16[2304,256]{1,0:T(8,128)(2,1)S(1)}, u32[]{:S(2)}, u32[]{:S(2)}) collective-permute-start(bf16[2304,256]{1,0:T(8,128)(2,1)S(1)} %dynamic-slice_bitcast_fusion), channel_id=1, source_target_pairs={{0,3},{1,0},{2,1},{3,2},{4,7},{5,4},{6,5},{7,6},{8,11},{9,8},{10,9... | collective-permute-start | bytes 3538952 | tf_op jit(solution)/shard_map/ppermute | solution.py:282
  15.7 38.5 %collective-permute-start.5 = (bf16[2304,256]{1,0:T(8,128)(2,1)S(1)}, bf16[2304,256]{1,0:T(8,128)(2,1)}, u32[]{:S(2)}, u32[]{:S(2)}) collective-permute-start(bf16[2304,256]{1,0:T(8,128)(2,1)S(1)} %dynamic-slice_bitcast_fusion), channel_id=1, source_target_pairs={{0,1},{1,2},{2,3},{3,0},{4,5},{5,6},{6,7},{7,4},{8,9},{9,10},{10,1... | collective-permute-start | bytes 3538952 | tf_op jit(solution)/shard_map/ppermute | solution.py:282
  16.3 48.1 %copy-start.9 = (bf16[576,256]{1,0:T(8,128)(2,1)}, bf16[576,256]{1,0:T(8,128)(2,1)S(1)}, u32[]{:S(2)}) copy-start(bf16[576,256]{1,0:T(8,128)(2,1)S(1)} %collective-permute-done.6.refs_0_) | copy-start | bytes 884740
  16.3 22.6 %collective-permute-start.7 = (bf16[576,256]{1,0:T(8,128)(2,1)S(1)}, bf16[576,256]{1,0:T(8,128)(2,1)S(1)}, u32[]{:S(2)}, u32[]{:S(2)}) collective-permute-start(bf16[576,256]{1,0:T(8,128)(2,1)S(1)} %collective-permute-done.6.refs_0_), channel_id=1, source_target_pairs={{0,8},{8,16},{16,24},{24,0},{1,9},{9,17},{17,25},{25,1},{2,10},{10... | collective-permute-start | bytes 884744 | tf_op jit(solution)/shard_map/ppermute | solution.py:282
  23.7 40.8 %copy-start.3 = (bf16[8,144,256]{2,1,0:T(8,128)(2,1)}, bf16[8,144,256]{2,1,0:T(8,128)(2,1)S(1)}, u32[]{:S(2)}) copy-start(bf16[8,144,256]{2,1,0:T(8,128)(2,1)S(1)} %all-to-all-done.tile) | copy-start | bytes 1769476
  23.7 6.2 %collective-permute-start = (bf16[48,256]{1,0:T(8,128)(2,1)S(1)}, bf16[48,256]{1,0:T(8,128)(2,1)S(1)}, u32[]{:S(2)}, u32[]{:S(2)}) collective-permute-start(bf16[48,256]{1,0:T(8,128)(2,1)S(1)} %get-tuple-element.56), channel_id=1, source_target_pairs={{0,64},{32,96},{64,128},{96,160},{128,192},{160,224},{1,65},{33,97... | collective-permute-start | bytes 73736 | tf_op jit(solution)/shard_map/ppermute | solution.py:277
  28.6 7.7 %collective-permute-start.1 = (bf16[48,256]{1,0:T(8,128)(2,1)S(1)}, bf16[48,256]{1,0:T(8,128)(2,1)}, u32[]{:S(2)}, u32[]{:S(2)}) collective-permute-start(bf16[48,256]{1,0:T(8,128)(2,1)S(1)} %get-tuple-element.55), channel_id=1, source_target_pairs={{64,0},{96,32},{128,64},{160,96},{192,128},{224,160},{65,1},{97,33... | collective-permute-start | bytes 73736 | tf_op jit(solution)/shard_map/ppermute | solution.py:277
  29.9 10.4 %collective-permute-start.8 = (bf16[576,256]{1,0:T(8,128)(2,1)S(1)}, bf16[576,256]{1,0:T(8,128)(2,1)}, u32[]{:S(2)}, u32[]{:S(2)}) collective-permute-start(bf16[576,256]{1,0:T(8,128)(2,1)S(1)} %collective-permute-done.6.refs_0_), channel_id=1, source_target_pairs={{0,16},{8,24},{16,0},{24,8},{1,17},{9,25},{17,1},{25,9},{2,18},{10... | collective-permute-start | bytes 884744 | tf_op jit(solution)/shard_map/ppermute | solution.py:282
  36.3 13.0 %collective-permute-start.2 = (bf16[8,144,256]{2,1,0:T(8,128)(2,1)S(1)}, bf16[8,144,256]{2,1,0:T(8,128)(2,1)S(1)}, u32[]{:S(2)}, u32[]{:S(2)}) collective-permute-start(bf16[8,144,256]{2,1,0:T(8,128)(2,1)S(1)} %all-to-all-done.tile), channel_id=1, source_target_pairs={{0,32},{32,64},{64,96},{96,128},{128,160},{160,192},{192,224},{1,3... | collective-permute-start | bytes 1769480 | tf_op jit(solution)/shard_map/ppermute | solution.py:277
  39.0 25.5 %copy-start.10 = (bf16[576,256]{1,0:T(8,128)(2,1)}, bf16[576,256]{1,0:T(8,128)(2,1)S(1)}, u32[]{:S(2)}) copy-start(bf16[576,256]{1,0:T(8,128)(2,1)S(1)} %collective-permute-done.7.refs_1_) | copy-start | bytes 884740
  39.0 15.3 %collective-permute-start.3 = (bf16[8,144,256]{2,1,0:T(8,128)(2,1)S(1)}, bf16[8,144,256]{2,1,0:T(8,128)(2,1)S(1)}, u32[]{:S(2)}, u32[]{:S(2)}) collective-permute-start(bf16[8,144,256]{2,1,0:T(8,128)(2,1)S(1)} %all-to-all-done.tile), channel_id=1, source_target_pairs={{32,0},{64,32},{96,64},{128,96},{160,128},{192,160},{224,192},{33,... | collective-permute-start | bytes 1769480 | tf_op jit(solution)/shard_map/ppermute | solution.py:277
  40.3 6.2 %collective-permute-start.9 = (bf16[576,256]{1,0:T(8,128)(2,1)S(1)}, bf16[576,256]{1,0:T(8,128)(2,1)}, u32[]{:S(2)}, u32[]{:S(2)}) collective-permute-start(bf16[576,256]{1,0:T(8,128)(2,1)S(1)} %collective-permute-done.6.refs_0_), channel_id=1, source_target_pairs={{0,24},{8,0},{16,8},{24,16},{1,25},{9,1},{17,9},{25,17},{2,26},{10... | collective-permute-start | bytes 884744 | tf_op jit(solution)/shard_map/ppermute | solution.py:282
  54.3 10.2 %copy-start.5 = (bf16[2304,256]{1,0:T(8,128)(2,1)}, bf16[2304,256]{1,0:T(8,128)(2,1)S(1)}, u32[]{:S(2)}) copy-start(bf16[2304,256]{1,0:T(8,128)(2,1)S(1)} %collective-permute-done.4.one) | copy-start | bytes 3538948
  54.3 10.2 %collective-permute-start.10 = (bf16[2304,256]{1,0:T(8,128)(2,1)S(1)}, bf16[2304,256]{1,0:T(8,128)(2,1)S(1)}, u32[]{:S(2)}, u32[]{:S(2)}) collective-permute-start(bf16[2304,256]{1,0:T(8,128)(2,1)S(1)} %collective-permute-done.4.one), channel_id=1, source_target_pairs={{0,4},{4,0},{1,5},{5,1},{2,6},{6,2},{3,7},{7,3},{8,12},{12,8},{9,1... | collective-permute-start | bytes 3538952 | tf_op jit(solution)/shard_map/ppermute | solution.py:282
  58.1 6.4 %collective-permute-start.11 = (bf16[2304,256]{1,0:T(8,128)(2,1)}, bf16[2304,256]{1,0:T(8,128)(2,1)}, u32[]{:S(2)}, u32[]{:S(2)}) collective-permute-start(bf16[2304,256]{1,0:T(8,128)(2,1)} %collective-permute-done.5.three), channel_id=1, source_target_pairs={{0,4},{4,0},{1,5},{5,1},{2,6},{6,2},{3,7},{7,3},{8,12},{12,8},{9,1... | collective-permute-start | bytes 3538952 | tf_op jit(solution)/shard_map/ppermute | solution.py:282
  58.8 3.0 %collective-permute-start.12 = (bf16[576,256]{1,0:T(8,128)(2,1)S(1)}, bf16[576,256]{1,0:T(8,128)(2,1)S(1)}, u32[]{:S(2)}, u32[]{:S(2)}) collective-permute-start(bf16[576,256]{1,0:T(8,128)(2,1)S(1)} %collective-permute-done.6.refs_0_), channel_id=1, source_target_pairs={{0,4},{4,0},{1,5},{5,1},{2,6},{6,2},{3,7},{7,3},{8,12},{12,8},{9,1... | collective-permute-start | bytes 884744 | tf_op jit(solution)/shard_map/ppermute | solution.py:282
  58.8 4.7 %collective-permute-start.13 = (bf16[576,256]{1,0:T(8,128)(2,1)S(1)}, bf16[576,256]{1,0:T(8,128)(2,1)}, u32[]{:S(2)}, u32[]{:S(2)}) collective-permute-start(bf16[576,256]{1,0:T(8,128)(2,1)S(1)} %collective-permute-done.7.refs_1_), channel_id=1, source_target_pairs={{0,4},{4,0},{1,5},{5,1},{2,6},{6,2},{3,7},{7,3},{8,12},{12,8},{9,1... | collective-permute-start | bytes 884744 | tf_op jit(solution)/shard_map/ppermute | solution.py:282
  59.3 4.5 %collective-permute-start.14 = (bf16[576,256]{1,0:T(8,128)(2,1)}, bf16[576,256]{1,0:T(8,128)(2,1)}, u32[]{:S(2)}, u32[]{:S(2)}) collective-permute-start(bf16[576,256]{1,0:T(8,128)(2,1)} %collective-permute-done.8.refs_2_), channel_id=1, source_target_pairs={{0,4},{4,0},{1,5},{5,1},{2,6},{6,2},{3,7},{7,3},{8,12},{12,8},{9,1... | collective-permute-start | bytes 884744 | tf_op jit(solution)/shard_map/ppermute | solution.py:282
  62.5 1.9 %collective-permute-start.15 = (bf16[576,256]{1,0:T(8,128)(2,1)}, bf16[576,256]{1,0:T(8,128)(2,1)}, u32[]{:S(2)}, u32[]{:S(2)}) collective-permute-start(bf16[576,256]{1,0:T(8,128)(2,1)} %collective-permute-done.9.refs_3_), channel_id=1, source_target_pairs={{0,4},{4,0},{1,5},{5,1},{2,6},{6,2},{3,7},{7,3},{8,12},{12,8},{9,1... | collective-permute-start | bytes 884744 | tf_op jit(solution)/shard_map/ppermute | solution.py:282
  84.1 21.8 %all-to-all-start.1 = ((bf16[8,320,256]{2,1,0:T(8,128)(2,1)}), bf16[8,320,256]{2,1,0:T(8,128)(2,1)S(1)}, u32[]{:S(2)}, u32[]{:S(2)}) async-start(bf16[8,320,256]{2,1,0:T(8,128)(2,1)} %get-tuple-element.36), calls=%async_computation.1 | async-start | bytes 2621440 | tf_op jit(solution)/shard_map/all_to_all | solution.py:327
  88.2 6.5 %collective-permute-start.16 = (bf16[16,1024]{1,0:T(8,128)(2,1)S(1)}, bf16[16,1024]{1,0:T(8,128)(2,1)S(1)}, u32[]{:S(2)}, u32[]{:S(2)}) collective-permute-start(bf16[16,1024]{1,0:T(8,128)(2,1)S(1)} %get-tuple-element.63), channel_id=1, source_target_pairs={{0,4},{4,8},{8,12},{12,16},{16,20},{20,24},{24,28},{28,0},{1,5},{5... | collective-permute-start | bytes 98312 | tf_op jit(solution)/shard_map/ppermute | solution.py:286
  88.5 6.2 %collective-permute-start.17 = (bf16[16,1024]{1,0:T(8,128)(2,1)S(1)}, bf16[16,1024]{1,0:T(8,128)(2,1)S(1)}, u32[]{:S(2)}, u32[]{:S(2)}) collective-permute-start(bf16[16,1024]{1,0:T(8,128)(2,1)S(1)} %get-tuple-element.62), channel_id=1, source_target_pairs={{0,8},{4,12},{8,16},{12,20},{16,24},{20,28},{24,0},{28,4},{1,9},{5... | collective-permute-start | bytes 98312 | tf_op jit(solution)/shard_map/ppermute | solution.py:286
  88.6 6.6 %collective-permute-start.18 = (bf16[16,1024]{1,0:T(8,128)(2,1)S(1)}, bf16[16,1024]{1,0:T(8,128)(2,1)S(1)}, u32[]{:S(2)}, u32[]{:S(2)}) collective-permute-start(bf16[16,1024]{1,0:T(8,128)(2,1)S(1)} %get-tuple-element.61), channel_id=1, source_target_pairs={{0,12},{4,16},{8,20},{12,24},{16,28},{20,0},{24,4},{28,8},{1,13},{... | collective-permute-start | bytes 98312 | tf_op jit(solution)/shard_map/ppermute | solution.py:286
  90.9 4.8 %collective-permute-start.19 = (bf16[16,1024]{1,0:T(8,128)(2,1)S(1)}, bf16[16,1024]{1,0:T(8,128)(2,1)S(1)}, u32[]{:S(2)}, u32[]{:S(2)}) collective-permute-start(bf16[16,1024]{1,0:T(8,128)(2,1)S(1)} %get-tuple-element.60), channel_id=1, source_target_pairs={{0,16},{4,20},{8,24},{12,28},{16,0},{20,4},{24,8},{28,12},{1,17},{... | collective-permute-start | bytes 98312 | tf_op jit(solution)/shard_map/ppermute | solution.py:286
  92.2 5.1 %collective-permute-start.20 = (bf16[16,1024]{1,0:T(8,128)(2,1)S(1)}, bf16[16,1024]{1,0:T(8,128)(2,1)S(1)}, u32[]{:S(2)}, u32[]{:S(2)}) collective-permute-start(bf16[16,1024]{1,0:T(8,128)(2,1)S(1)} %get-tuple-element.59), channel_id=1, source_target_pairs={{0,20},{4,24},{8,28},{12,0},{16,4},{20,8},{24,12},{28,16},{1,21},{... | collective-permute-start | bytes 98312 | tf_op jit(solution)/shard_map/ppermute | solution.py:286
  94.7 3.3 %collective-permute-start.21 = (bf16[16,1024]{1,0:T(8,128)(2,1)S(1)}, bf16[16,1024]{1,0:T(8,128)(2,1)S(1)}, u32[]{:S(2)}, u32[]{:S(2)}) collective-permute-start(bf16[16,1024]{1,0:T(8,128)(2,1)S(1)} %get-tuple-element.58), channel_id=1, source_target_pairs={{0,24},{4,28},{8,0},{12,4},{16,8},{20,12},{24,16},{28,20},{1,25},{... | collective-permute-start | bytes 98312 | tf_op jit(solution)/shard_map/ppermute | solution.py:286
  94.7 3.8 %collective-permute-start.22 = (bf16[16,1024]{1,0:T(8,128)(2,1)S(1)}, bf16[16,1024]{1,0:T(8,128)(2,1)S(1)}, u32[]{:S(2)}, u32[]{:S(2)}) collective-permute-start(bf16[16,1024]{1,0:T(8,128)(2,1)S(1)} %get-tuple-element.57), channel_id=1, source_target_pairs={{0,28},{4,0},{8,4},{12,8},{16,12},{20,16},{24,20},{28,24},{1,29},{... | collective-permute-start | bytes 98312 | tf_op jit(solution)/shard_map/ppermute | solution.py:286
  126.3 18.2 %copy-start.2 = (s32[5]{0:T(128)S(1)}, s32[5]{0:T(128)}, u32[]{:S(2)}) copy-start(s32[5]{0:T(128)} %stack.37.meta) | copy-start | bytes 64
  127.3 13.3 %all-to-all-start.3 = ((bf16[8,72,256]{2,1,0:T(8,128)(2,1)}), bf16[8,72,256]{2,1,0:T(8,128)(2,1)S(1)}, u32[]{:S(2)}, u32[]{:S(2)}) async-start(bf16[8,72,256]{2,1,0:T(8,128)(2,1)} %reduce_sum.21), calls=%async_computation.3 | async-start | bytes 589824 | tf_op jit(solution)/shard_map/all_to_all | solution.py:332
  140.6 5.2 %collective-permute-start.23 = (f32[36,256]{1,0:T(8,128)S(1)}, f32[36,256]{1,0:T(8,128)S(1)}, u32[]{:S(2)}, u32[]{:S(2)}) collective-permute-start(f32[36,256]{1,0:T(8,128)S(1)} %get-tuple-element.66), channel_id=1, source_target_pairs={{0,4},{4,0},{1,5},{5,1},{2,6},{6,2},{3,7},{7,3},{8,12},{12,8},{9,1... | collective-permute-start | bytes 110600 | tf_op jit(solution)/shard_map/ppermute | solution.py:282
  (8 other events, 17.0 us)

commit v3 on v2

--- a/solution.py
+++ b/solution.py
@@ -11,17 +11,18 @@
 C = 256
 W = 32
 WIDE = 48
-PIECE = WIDE + 3 * W
+BOTH = W + 16
+PIECE = WIDE + 16 + 3 * BOTH
 QUARTER = 576
 SPAN = 18
 VMEM = pl.BlockSpec(memory_space=pltpu.VMEM)
-SMEM = pl.BlockSpec(memory_space=pltpu.SMEM)
 HBM = pl.BlockSpec(memory_space=pltpu.HBM)
+ANY = pl.BlockSpec(memory_space=pl.ANY)
 PARAMS = pltpu.CompilerParams(vmem_limit_bytes=24 * 1024 * 1024)
 f32, bf16 = jnp.float32, jnp.bfloat16
 
 
-def row_chunks(rows, most=8):
+def row_chunks(rows, most=12):
     count = -(-rows // most)
     base, extra = divmod(rows, count)
     out, at = [], 0
@@ -37,11 +38,13 @@
     padded[144:160] = jnp.zeros((16, 4 * C), f32)
     padded[16:144, 0:2 * C] = field[...].astype(f32)
     padded[16:144, 2 * C:4 * C] = cotangent[...].astype(f32)
-    for j in range(8):
-        out[j, 0:WIDE] = padded[16 * j:16 * j + WIDE, 0:C].astype(bf16)
+    for chip in range(4):
+        piece = [padded[32 * chip:32 * chip + WIDE + 16, 0:C].astype(bf16)]
         for i in range(1, 4):
-            at = WIDE + (i - 1) * W
-            out[j, at:at + W] = padded[16 * j + 8:16 * j + 8 + W, i * C:(i + 1) * C].astype(bf16)
+            piece.append(padded[32 * chip + 8:32 * chip + 8 + BOTH, i * C:(i + 1) * C].astype(bf16))
+        piece = jnp.concatenate(piece, axis=0)
+        out[2 * chip] = piece
+        out[2 * chip + 1] = piece
 
 
 def make_pieces(field, cotangent):
@@ -56,39 +59,44 @@
     )(field, cotangent)
 
 
-def blocks_kernel(meta, above, tile, below, far_above, far_below, held, one, one2, three, three2, *refs):
-    quarters, (done, acts, w, s1a, s1b, s2a, s2b, s3, s4, t1a, t1b, n2a, n2b, packed, sent, sems) = refs[:8], refs[8:]
-    core, rowbase, place, section, y = (meta[i] for i in range(5))
+def blocks_kernel(tile, beyond, beyond2, far, far2, held, first, first2, second, second2, quarters, quarters2,
+                  done, acts, w, near, ends, s1a, s1b, s2a, s2b, s3, s4, t1a, t1b, n2a, n2b, packed, sent, sems):
+    z, y, core, section = (lax.axis_index(a) for a in ("z", "y", "core", "section"))
+    rowbase, place = 8 * z, 2 * y + core
     colbase = 16 * place
 
-    def kernel_copy(k, branch, src, at=0):
-        size = src.shape[0]
-        return pltpu.make_async_copy(src, w.at[k, branch, pl.ds(at, size)], sems.at[2 * k + jnp.where(branch == core, 0, 1)])
+    loads = [pltpu.make_async_copy(src, dst, sems.at[12 + i]) for i, (src, dst) in enumerate((
+        (beyond, near.at[core]), (beyond2, near.at[1 - core]), (far, ends.at[core]), (far2, ends.at[1 - core])))]
+    for load in loads:
+        load.start()
+
+    def kernel_copy(k, src, part=()):
+        return pltpu.make_async_copy(src, w.at[(k, *part)], sems.at[k])
 
     for k in (3, 2, 1, 0):
         ahead = lax.rem(k + 4 - section, 4)
+        mine = 1 + 2 * core
 
         @pl.when(ahead == 0)
         def _():
-            kernel_copy(k, core, held.at[core]).start()
-            kernel_copy(k, 1 - core, held.at[1 - core]).start()
-
-        @pl.when(ahead == 1)
+            kernel_copy(k, held).start()
+
+        @pl.when(ahead == mine)
         def _():
-            kernel_copy(k, core, one).start()
-            kernel_copy(k, 1 - core, one2).start()
-
-        @pl.when(ahead == 3)
+            kernel_copy(k, first, (0,)).start()
+            kernel_copy(k, second, (1,)).start()
+
+        @pl.when(ahead == 4 - mine)
         def _():
-            kernel_copy(k, core, three).start()
-            kernel_copy(k, 1 - core, three2).start()
+            kernel_copy(k, first2, (0,)).start()
+            kernel_copy(k, second2, (1,)).start()
 
         @pl.when(ahead == 2)
         def _():
             for d in range(4):
-                at = pl.multiple_of(lax.rem(y + 4 - d, 4) * QUARTER, QUARTER)
-                kernel_copy(k, core, quarters[d], at).start()
-                kernel_copy(k, 1 - core, quarters[4 + d], at).start()
+                rows = pl.ds(QUARTER * d, QUARTER)
+                kernel_copy(k, quarters.at[d], (core, rows)).start()
+                kernel_copy(k, quarters2.at[d], (1 - core, rows)).start()
 
     def put(buf, at, mid, left, right):
         n = mid.shape[0]
@@ -129,17 +137,20 @@
                 acc = d if acc is None else acc + d
         return acc.reshape(n, W, C)
 
-    def window(lo, hi, a, n, halo):
+    def window(which, a, n, halo):
+        lo, size = (0, WIDE) if which == 0 else (WIDE + 16 + (which - 1) * BOTH, W)
+        cols = pl.ds(pl.multiple_of(lo + 16 * core, 16), size)
         parts, at = [], a - halo
         while at < a - halo + n:
-            if at < -8:
-                part, took = far_above[lo:hi][None], 1
-            elif at >= 16:
-                part, took = far_below[lo:hi][None], 1
+            if at < -8 or at >= 16:
+                part, took = ends[0 if at < 0 else 1, cols][None], 1
+            elif 0 <= at < 8:
+                took = min(a - halo + n, 8) - at
+                part = tile[at:at + took, cols]
             else:
-                ref, base = ((above, -8), (tile, 0), (below, 8))[0 if at < 0 else 1 if at < 8 else 2]
+                side, base = (0, -8) if at < 0 else (1, 8)
                 took = min(a - halo + n, base + 8) - at
-                part = ref[at - base:at - base + took, lo:hi]
+                part = near[side, at - base:at - base + took, cols]
             parts.append(part.astype(f32))
             at += took
         return parts[0] if len(parts) == 1 else jnp.concatenate(parts, axis=0)
@@ -153,26 +164,27 @@
             at = lax.rem(i - halo + 8 - place, 8)
             done[at, :, which * C:(which + 1) * C] = value[i - a, 8:24].astype(bf16)
 
+    for load in loads:
+        load.wait()
     for a, n in row_chunks(26):
-        spread(s1a, a, window(0, WIDE, a, n, 9))
+        spread(s1a, a, window(0, a, n, 9))
     for k, p in ((3, 8), (2, 6), (1, 4), (0, 2)):
-        first, last = k == 3, k == 0
+        top, last = k == 3, k == 0
         s1, s1n = (s1a, s1b) if k % 2 else (s1b, s1a)
         s2, s2o = (s2a, s2b) if k % 2 else (s2b, s2a)
         t1n, t1o = (t1a, t1b) if k % 2 else (t1b, t1a)
         n2n, n2o = (n2a, n2b) if k % 2 else (n2b, n2a)
 
         def old_y2(a, n):
-            return window(WIDE, WIDE + W, a, n, p) if first else lanes(s2o, a + 2, n)
+            return window(1, a, n, p) if top else lanes(s2o, a + 2, n)
 
         def old_g1(a, n):
-            return window(WIDE + W, WIDE + 2 * W, a, n, p - 1) if first else t1o[a + 2:a + 2 + n].astype(f32)
+            return window(2, a, n, p - 1) if top else t1o[a + 2:a + 2 + n].astype(f32)
 
         def old_g2(a, n):
-            return window(WIDE + 2 * W, WIDE + 3 * W, a, n, p) if first else n2o[a:a + n].astype(f32)
-
-        kernel_copy(k, core, held.at[0]).wait()
-        kernel_copy(k, 1 - core, held.at[0]).wait()
+            return window(3, a, n, p) if top else n2o[a:a + n].astype(f32)
+
+        kernel_copy(k, held).wait()
         for a, n in row_chunks(8 + 2 * p):
             pre = conv(s1, a, n, k, 1)
             sig = jax.nn.sigmoid(pre)
@@ -212,12 +224,12 @@
             sent[4 * branch + k, 0:192] = packed[0:192].astype(bf16)
             d = lanes(delta, hd, 8)[:, 8:24]
             sent[4 * branch + k, 192:320] = d.reshape(128, C).astype(bf16)
-            pltpu.make_async_copy(sent.at[4 * branch + k], acts.at[4 * branch + k], sems.at[8 + 4 * branch + k]).start()
+            pltpu.make_async_copy(sent.at[4 * branch + k], acts.at[4 * branch + k], sems.at[4 + 4 * branch + k]).start()
     for i in range(8):
-        pltpu.make_async_copy(sent.at[i], acts.at[i], sems.at[8 + i]).wait()
-
-
-def blocks(meta, fields, kernels):
+        pltpu.make_async_copy(sent.at[i], acts.at[i], sems.at[4 + i]).wait()
+
+
+def blocks(fields, kernels):
     def spread(rows):
         return pltpu.VMEM((rows * W, 3 * C), bf16)
 
@@ -228,15 +240,16 @@
     return pl.pallas_call(
         blocks_kernel,
         out_shape=[jax.ShapeDtypeStruct((8, 16, 4 * C), bf16), jax.ShapeDtypeStruct((8, 320, C), bf16)],
-        in_specs=[SMEM] + [VMEM] * 5 + [HBM] * len(kernels),
+        in_specs=[VMEM] + [ANY] * (4 + len(kernels)),
         out_specs=[VMEM, HBM],
-        scratch_shapes=[pltpu.VMEM((4, 2, 2304, C), bf16), spread(26), spread(22), spread(24), spread(20), spread(24), spread(22),
+        scratch_shapes=[pltpu.VMEM((4, 2, 2304, C), bf16), pltpu.VMEM((2, 8, PIECE, C), bf16), pltpu.VMEM((2, WIDE + 16, C), bf16),
+                        spread(26), spread(22), spread(24), spread(20), spread(24), spread(22),
                         plain(22), plain(18), plain(20), plain(16),
                         pltpu.VMEM((192, C), f32), pltpu.VMEM((8, 320, C), bf16), pltpu.SemaphoreType.DMA((16,))],
         compiler_params=pltpu.CompilerParams(vmem_limit_bytes=56 * 1024 * 1024),
         cost_estimate=pl.CostEstimate(flops=flops, bytes_accessed=16 * 1024 * 1024, transcendentals=0),
         name="blocks",
-    )(meta, *fields, *kernels)
+    )(*fields, *kernels)
 
 
 def grad_kernel(acts, out, lhs, packed, grad):
@@ -253,10 +266,11 @@
     for t in range(9):
         grad[t * C:(t + 1) * C, :] = lax.dot_general(
             lhs[:, t * C:(t + 1) * C], d, (((0,), (0,)), ((), ())), preferred_element_type=f32)
+    here = lax.axis_index("y")
     for z in range(8):
         for y in range(4):
             at = (4 * z + y) * 72
-            out[y, z] = grad[at:at + 72].astype(bf16)
+            out[lax.rem(y + 4 - here, 4), z] = grad[at:at + 72].astype(bf16)
 
 
 def kernel_grads(acts):
@@ -272,63 +286,67 @@
     )(acts)
 
 
-def shift(value, axis, by):
-    size = lax.axis_size(axis)
-    return lax.ppermute(value, axis, [(i, i + by) for i in range(size) if 0 <= i + by < size])
-
-
 def turn(value, axis, by):
     size = lax.axis_size(axis)
     return lax.ppermute(value, axis, [(i, (i + by) % size) for i in range(size)])
 
 
+def apart(value, by):
+    pairs = [(2 * i + c, 2 * (i + d) + c) for c, d in ((0, by), (1, -by)) for i in range(8) if 0 <= i + d < 8]
+    return lax.ppermute(value, ("z", "core"), pairs)
+
+
 def around(value, by):
     return lax.ppermute(value, ("y", "core"), [(i, (i + by) % 8) for i in range(8)])
 
 
-def unpack_kernel(meta, *refs):
-    place = meta[2]
+def unpack_kernel(*refs):
+    place = 2 * lax.axis_index("y") + lax.axis_index("core")
     for d in range(8):
         at = pl.multiple_of(lax.rem(place + 8 - d, 8) * 16, 16)
         refs[8][pl.ds(at, 16), :] = refs[d][:, 0:2 * C]
         refs[9][pl.ds(at, 16), :] = refs[d][:, 2 * C:4 * C]
 
 
-def unpack(meta, back):
+def unpack(back):
     return pl.pallas_call(
         unpack_kernel,
         out_shape=[jax.ShapeDtypeStruct((128, 2 * C), bf16)] * 2,
-        in_specs=[SMEM] + [VMEM] * 8,
+        in_specs=[VMEM] * 8,
         out_specs=[VMEM] * 2,
         compiler_params=PARAMS,
         name="unpack",
-    )(meta, *back)
+    )(*back)
 
 
 def local(block_out, out_grad, weights):
-    z, y, core, section = (lax.axis_index(a) for a in ("z", "y", "core", "section"))
-    meta = jnp.stack([core, 8 * z, 2 * y + core, section, y]).astype(jnp.int32)
-
-    own = lax.dynamic_index_in_dim(weights[0], core, 0, keepdims=False)
-    part = turn(lax.dynamic_slice_in_dim(own, QUARTER * y, QUARTER, 0), "section", 2)
-    one, three = turn(own, "section", -1), turn(own, "section", 1)
+    y, core = lax.axis_index("y"), lax.axis_index("core")
+
+    part = lax.dynamic_slice(weights[0], (core, QUARTER * y, 0), (1, QUARTER, C))[0]
+    part = turn(part, "section", 2)
+    beside = [lax.ppermute(weights[0, i], ("core", "section"),
+                           [(4 * c + i, 4 * c + (i + (-1, 1)[c]) % 4) for c in range(2) for i in range(4)])
+              for i in range(2)]
 
     tile = lax.all_to_all(make_pieces(block_out[0, 0], out_grad[0, 0]), ("y", "core"), 0, 0)
-    far = (shift(tile[7, :WIDE], "z", 2), shift(tile[0, :WIDE], "z", -2))
-    near = (shift(tile, "z", 1), shift(tile, "z", -1))
-    quarters = [part] + [turn(part, "y", d) for d in (1, 2, 3)]
-
-    far, near, one, three, quarters = lax.optimization_barrier((far, near, one, three, quarters))
-    others = [turn(v, "core", 1) for v in (one, three, *quarters)]
-    fields = (near[0], tile, near[1], *far)
-    done, acts = blocks(meta, fields, (weights[0], one, others[0], three, others[1], *quarters, *others[2:]))
+    part = jnp.broadcast_to(part[None], (4, QUARTER, C))
+    tile, part = lax.optimization_barrier((tile, part))
+    beyond = apart(tile, 1)
+    far = apart(jnp.where(core == 0, tile[7, :WIDE + 16], tile[0, :WIDE + 16]), 2)
+    quarters = lax.all_to_all(part, "y", 0, 0)
+
+    beyond, far, beside, quarters = lax.optimization_barrier((beyond, far, beside, quarters))
+    moved = [v for m in (*beside, quarters) for v in (m, turn(m, "core", 1))]
+    fields = (tile, beyond, turn(beyond, "core", 1), far, turn(far, "core", 1))
+    done, acts = blocks(fields, (weights[0], *moved))
 
     back = [done[0]] + [around(done[d], d) for d in range(1, 8)]
     got = lax.all_to_all(acts, ("core", "section"), 0, 0)
     got, back = lax.optimization_barrier((got, back))
     grad = kernel_grads(got)
-    restored, input_grad = unpack(meta, back)
-    grad = lax.all_to_all(grad, "y", 0, 0).astype(f32).sum(axis=0).astype(bf16)
+    restored, input_grad = unpack(back)
+    terms = [grad[0]] + [turn(grad[d], "y", d) for d in (1, 2, 3)]
+    grad = sum(t.astype(f32) for t in terms).astype(bf16)
     grad = lax.all_to_all(grad, "z", 0, 0).astype(f32).sum(axis=0)
     here = lax.dynamic_slice_in_dim(grad, 36 * core, 36, 0)
     there = turn(lax.dynamic_slice_in_dim(grad, 36 * (1 - core), 36, 0), "core", 1)

time: 147 us -> 144 us (0.980)
  blocking collectives: 18.7 us -> 0 us
  waiting for transfers between devices: 48.6 us -> 62.6 us
  local copies, waits for them, and re-layouts: 7.37 us -> 9.66 us
    all_to_all x1 -> x0, blocking collectives: 18.7 us -> none  [local(): grad = lax.all_to_all(grad, 'y', 0, 0).astype(f32).sum(axis=0).astype(bf16)]
    ppermute x13 -> x10, waiting for transfers between devices: 8.66 us -> 18.9 us  [turn(): lax.ppermute(value, axis, [(i, (i + by) % size) for i in range(size)])]
    ppermute x4, starting transfers between devices: 10.1 us -> 3.85 us  [the longest x2 2.57 us: apart(): return lax.ppermute(value, ('z', 'core'), pairs)]
    all_to_all x1, starting transfers between devices: 3.55 us -> 9.61 us  [local(): grad = lax.all_to_all(grad, 'z', 0, 0).astype(f32).sum(axis=0)]
    ppermute x13 -> x10, starting transfers between devices: 17.4 us -> 12.6 us  [turn(): lax.ppermute(value, axis, [(i, (i + by) % size) for i in range(size)])]
    all_to_all x1, waiting for transfers between devices: 5.95 us -> 10.6 us  [local(): lax.all_to_all(make_pieces(block_out[0, 0], out_grad[0, 0]), ('y', 'core'...]
    all_to_all x0 -> x1, starting transfers between devices: none -> 3.53 us  [local(): quarters = lax.all_to_all(part, 'y', 0, 0)]
    broadcast_in_dim x0 -> x1, local copies, waits for them, and re-layouts: none -> 2.06 us  [local(): part = jnp.broadcast_to(part[None], (4, QUARTER, C))]
  transfers between devices with their start and end apart: 27 -> 25, of which waited for: 14 -> 12; matrix products, arithmetic and copies ran while one was open for 1% -> 3% of each run, Pallas kernels for 1% -> 1%
where the time goes in v3:
time: 144 us; the launch traced here: 143 us
  waiting for transfers between devices  62.6 us (43%)
  starting transfers between devices  46.9 us (33%)
  Pallas kernels  21.8 us (15%)
  local copies, waits for them, and re-layouts  9.66 us (7%)
  other arithmetic  1.71 us (1%)
    ppermute x10, waiting for transfers between devices, turn(): lax.ppermute(value, axis, [(i, (i + by) % size) for i in range(size)])  18.9 us
    pallas_call x1, Pallas kernels, blocks(): pl.pallas_call(blocks_kernel, out_shape=[jax.ShapeDtypeStruct((8, 16, 4 *...  18.4 us
    ppermute x10, starting transfers between devices, turn(): lax.ppermute(value, axis, [(i, (i + by) % size) for i in range(size)])  12.6 us
    ppermute x2, waiting for transfers between devices, apart(): return lax.ppermute(value, ('z', 'core'), pairs)  12.5 us
    all_to_all x1, waiting for transfers between devices, local(): grad = lax.all_to_all(grad, 'z', 0, 0).astype(f32).sum(axis=0)  10.6 us
    all_to_all x1, waiting for transfers between devices, local(): lax.all_to_all(make_pieces(block_out[0, 0], out_grad[0, 0]), ('y', 'core'...  10.6 us
    all_to_all x1, starting transfers between devices, local(): grad = lax.all_to_all(grad, 'z', 0, 0).astype(f32).sum(axis=0)  9.61 us
    ppermute x7, starting transfers between devices, around(): lax.ppermute(value, ('y', 'core'), [(i, (i + by) % 8) for i in range(8)])  7.77 us
  transfers between devices with their start and end apart: 25, of which 12 were waited for; matrix products, arithmetic and copies ran while one was open for 3% of the time, Pallas kernels for 1%

profile of v3, /device:TPU:1, one launch (start us, length us, event | category | flops | bytes accessed | tf_op | source)
XLA Modules:
  0.0 143.5 jit_solution(9734993948147472508)
XLA Ops:
  0.6 1.7 %dynamic-slice_bitcast_fusion = bf16[576,256]{1,0:T(8,128)(2,1)} fusion(bf16[1,2,2304,256]{3,2,1,0:T(8,128)(2,1)} %param.5, s32[]{:T(128)S(6)} %select_n.38, s32[]{:T(128)S(6)} %select_n.39), kind=kLoop, calls=%fused_computation.11 | loop fusion | bytes 589832 | tf_op jit(solution)/shard_map/squeeze | solution.py:325
  2.3 3.6 %collective-permute-start = (bf16[576,256]{1,0:T(8,128)(2,1)}, bf16[576,256]{1,0:T(8,128)(2,1)}, u32[]{:S(2)}, u32[]{:S(2)}) collective-permute-start(bf16[576,256]{1,0:T(8,128)(2,1)} %dynamic-slice_bitcast_fusion), channel_id=1, source_target_pairs={{0,2},{1,3},{2,0},{3,1},{4,6},{5,7},{6,4},{7,5},{8,10},{9,11},{10,... | collective-permute-start | bytes 884744 | tf_op jit(solution)/shard_map/ppermute | solution.py:291
  5.9 0.9 copy-done
  6.8 0.9 copy-done.1
  7.7 1.0 pieces.1
  8.7 5.6 %all-to-all-start = ((bf16[8,208,256]{2,1,0:T(8,128)(2,1)}), bf16[8,208,256]{2,1,0:T(8,128)(2,1)}, u32[]{:S(2)}, u32[]{:S(2)}) async-start(bf16[8,208,256]{2,1,0:T(8,128)(2,1)} %pieces.1), calls=%async_computation | async-start | bytes 1703936 | tf_op jit(solution)/shard_map/all_to_all | solution.py:331
  14.3 1.2 slice_bitcast_fusion
  15.8 1.0 collective-permute-start.4
  16.7 10.6 %all-to-all-done.tile = bf16[8,208,256]{2,1,0:T(8,128)(2,1)} async-done(((bf16[8,208,256]{2,1,0:T(8,128)(2,1)}), bf16[8,208,256]{2,1,0:T(8,128)(2,1)}, u32[]{:S(2)}, u32[]{:S(2)}) %all-to-all-start) | async-done | bytes 852000 | tf_op jit(solution)/shard_map/all_to_all | solution.py:331
  27.3 2.1 %broadcast_in_dim.6 = bf16[4,576,256]{2,1,0:T(8,128)(2,1)} broadcast(bf16[576,256]{1,0:T(8,128)(2,1)} %collective-permute-done), dimensions={1,2} | broadcast | bytes 1474560 | tf_op jit(solution)/shard_map/broadcast_in_dim | solution.py:332
  29.4 3.5 %all-to-all-start.1 = ((bf16[4,576,256]{2,1,0:T(8,128)(2,1)}), bf16[4,576,256]{2,1,0:T(8,128)(2,1)S(1)}, u32[]{:S(2)}, u32[]{:S(2)}) async-start(bf16[4,576,256]{2,1,0:T(8,128)(2,1)} %broadcast_in_dim.6), calls=%async_computation.1 | async-start | bytes 2359296 | tf_op jit(solution)/shard_map/all_to_all | solution.py:336
  32.9 1.3 collective-permute-start.1
  35.0 1.3 collective-permute-start.2
  36.3 12.5 %collective-permute-done.2.far = bf16[64,256]{1,0:T(8,128)(2,1)S(1)} collective-permute-done((bf16[64,256]{1,0:T(8,128)(2,1)S(1)}, bf16[64,256]{1,0:T(8,128)(2,1)S(1)}, u32[]{:S(2)}, u32[]{:S(2)}) %collective-permute-start.2) | collective-permute-done | bytes 32800 | tf_op jit(solution)/shard_map/ppermute | solution.py:296
  48.8 1.5 %collective-permute-start.7 = (bf16[2304,256]{1,0:T(8,128)(2,1)}, bf16[2304,256]{1,0:T(8,128)(2,1)S(1)}, u32[]{:S(2)}, u32[]{:S(2)}) collective-permute-start(bf16[2304,256]{1,0:T(8,128)(2,1)} %collective-permute-done.3.first), channel_id=1, source_target_pairs={{0,4},{4,0},{1,5},{5,1},{2,6},{6,2},{3,7},{7,3},{8,12},{12,8},{9,1... | collective-permute-start | bytes 3538952 | tf_op jit(solution)/shard_map/ppermute | solution.py:291
  51.4 6.1 %collective-permute-done.6.far2 = bf16[64,256]{1,0:T(8,128)(2,1)S(1)} collective-permute-done((bf16[64,256]{1,0:T(8,128)(2,1)S(1)}, bf16[64,256]{1,0:T(8,128)(2,1)S(1)}, u32[]{:S(2)}, u32[]{:S(2)}) %collective-permute-start.6) | collective-permute-done | bytes 32800 | tf_op jit(solution)/shard_map/ppermute | solution.py:291
  59.7 18.4 %blocks.1 = (bf16[8,16,1024]{2,1,0:T(8,128)(2,1)}, bf16[8,320,256]{2,1,0:T(8,128)(2,1)}) custom-call(bf16[8,208,256]{2,1,0:T(8,128)(2,1)} %all-to-all-done.tile, bf16[8,208,256]{2,1,0:T(8,128)(2,1)} %copy-done.8, bf16[8,208,256]{2,1,0:T(8,128)(2,1)} %copy-done.9, bf16[64,256]{1,0:T(8,128)(2,1)} %copy-done.10, bf16[64,256]{1,0:T(8,128)(2,1)} %copy-done.11, ...), custom_call_target="tpu_custom_call" | custom-call | flops 9059696640 | bytes 16777216 | tf_op jit(solution)/shard_map/blocks/pallas_call | solution.py:240
  78.0 4.0 %all-to-all-start.2 = ((bf16[8,320,256]{2,1,0:T(8,128)(2,1)}), bf16[8,320,256]{2,1,0:T(8,128)(2,1)S(1)}, u32[]{:S(2)}, u32[]{:S(2)}) async-start(bf16[8,320,256]{2,1,0:T(8,128)(2,1)} %get-tuple-element.30), calls=%async_computation.2 | async-start | bytes 2621440 | tf_op jit(solution)/shard_map/all_to_all | solution.py:344
  83.1 1.9 %collective-permute-start.12 = (bf16[16,1024]{1,0:T(8,128)(2,1)S(1)}, bf16[16,1024]{1,0:T(8,128)(2,1)S(1)}, u32[]{:S(2)}, u32[]{:S(2)}) collective-permute-start(bf16[16,1024]{1,0:T(8,128)(2,1)S(1)} %get-tuple-element.55), channel_id=1, source_target_pairs={{0,12},{4,16},{8,20},{12,24},{16,28},{20,0},{24,4},{28,8},{1,13},{... | collective-permute-start | bytes 98312 | tf_op jit(solution)/shard_map/ppermute | solution.py:300
  85.0 1.0 collective-permute-start.13
  86.0 2.5 %collective-permute-start.14 = (bf16[16,1024]{1,0:T(8,128)(2,1)S(1)}, bf16[16,1024]{1,0:T(8,128)(2,1)S(1)}, u32[]{:S(2)}, u32[]{:S(2)}) collective-permute-start(bf16[16,1024]{1,0:T(8,128)(2,1)S(1)} %get-tuple-element.53), channel_id=1, source_target_pairs={{0,20},{4,24},{8,28},{12,0},{16,4},{20,8},{24,12},{28,16},{1,21},{... | collective-permute-start | bytes 98312 | tf_op jit(solution)/shard_map/ppermute | solution.py:300
  88.5 1.3 collective-permute-start.16
  89.8 1.3 collective-permute-done.14.refs_5_
  92.3 7.5 %all-to-all-done.2.acts = bf16[8,320,256]{2,1,0:T(8,128)(2,1)S(1)} async-done(((bf16[8,320,256]{2,1,0:T(8,128)(2,1)}), bf16[8,320,256]{2,1,0:T(8,128)(2,1)S(1)}, u32[]{:S(2)}, u32[]{:S(2)}) %all-to-all-start.2) | async-done | bytes 1310752 | tf_op jit(solution)/shard_map/all_to_all | solution.py:344
  99.8 1.7 %kernel_grads.1 = bf16[4,8,72,256]{3,2,1,0:T(8,128)(2,1)S(1)} custom-call(bf16[8,320,256]{2,1,0:T(8,128)(2,1)S(1)} %all-to-all-done.2.acts), custom_call_target="tpu_custom_call" | custom-call | flops 1207959552 | bytes 8388608 | tf_op jit(solution)/shard_map/kernel_grads/pallas_call | solution.py:277
  102.0 2.0 %collective-permute-start.18 = (bf16[8,72,256]{2,1,0:T(8,128)(2,1)S(1)}, bf16[8,72,256]{2,1,0:T(8,128)(2,1)S(1)}, u32[]{:S(2)}, u32[]{:S(2)}) collective-permute-start(bf16[8,72,256]{2,1,0:T(8,128)(2,1)S(1)} %get-tuple-element.50), channel_id=1, source_target_pairs={{0,16},{8,24},{16,0},{24,8},{1,17},{9,25},{17,1},{25,9},{2,18},{10... | collective-permute-start | bytes 884744 | tf_op jit(solution)/shard_map/ppermute | solution.py:291
  103.9 1.2 collective-permute-start.19
  105.1 6.4 %collective-permute-done.17 = bf16[8,72,256]{2,1,0:T(8,128)(2,1)S(1)} collective-permute-done((bf16[8,72,256]{2,1,0:T(8,128)(2,1)S(1)}, bf16[8,72,256]{2,1,0:T(8,128)(2,1)S(1)}, u32[]{:S(2)}, u32[]{:S(2)}) %collective-permute-start.17) | collective-permute-done | bytes 294944 | tf_op jit(solution)/shard_map/ppermute | solution.py:291
  111.5 5.6 %collective-permute-done.18 = bf16[8,72,256]{2,1,0:T(8,128)(2,1)S(1)} collective-permute-done((bf16[8,72,256]{2,1,0:T(8,128)(2,1)S(1)}, bf16[8,72,256]{2,1,0:T(8,128)(2,1)S(1)}, u32[]{:S(2)}, u32[]{:S(2)}) %collective-permute-start.18) | collective-permute-done | bytes 294944 | tf_op jit(solution)/shard_map/ppermute | solution.py:291
  118.6 9.6 %all-to-all-start.3 = ((bf16[8,72,256]{2,1,0:T(8,128)(2,1)}), bf16[8,72,256]{2,1,0:T(8,128)(2,1)S(1)}, u32[]{:S(2)}, u32[]{:S(2)}) async-start(bf16[8,72,256]{2,1,0:T(8,128)(2,1)} %fusion.2), calls=%async_computation.3 | async-start | bytes 589824 | tf_op jit(solution)/shard_map/all_to_all | solution.py:350
  128.2 10.6 %all-to-all-done.3 = bf16[8,72,256]{2,1,0:T(8,128)(2,1)S(1)} async-done(((bf16[8,72,256]{2,1,0:T(8,128)(2,1)}), bf16[8,72,256]{2,1,0:T(8,128)(2,1)S(1)}, u32[]{:S(2)}, u32[]{:S(2)}) %all-to-all-start.3) | async-done | bytes 294944 | tf_op jit(solution)/shard_map/all_to_all | solution.py:350
  138.9 3.0 %collective-permute-start.20 = (f32[36,256]{1,0:T(8,128)S(1)}, f32[36,256]{1,0:T(8,128)S(1)}, u32[]{:S(2)}, u32[]{:S(2)}) collective-permute-start(f32[36,256]{1,0:T(8,128)S(1)} %get-tuple-element.60), channel_id=1, source_target_pairs={{0,4},{4,0},{1,5},{5,1},{2,6},{6,2},{3,7},{7,3},{8,12},{12,8},{9,1... | collective-permute-start | bytes 110600 | tf_op jit(solution)/shard_map/ppermute | solution.py:291
  (57 shorter events, 10.1 us)
Async XLA Ops:
  2.3 14.4 %collective-permute-start = (bf16[576,256]{1,0:T(8,128)(2,1)}, bf16[576,256]{1,0:T(8,128)(2,1)}, u32[]{:S(2)}, u32[]{:S(2)}) collective-permute-start(bf16[576,256]{1,0:T(8,128)(2,1)} %dynamic-slice_bitcast_fusion), channel_id=1, source_target_pairs={{0,2},{1,3},{2,0},{3,1},{4,6},{5,7},{6,4},{7,5},{8,10},{9,11},{10,... | collective-permute-start | bytes 884744 | tf_op jit(solution)/shard_map/ppermute | solution.py:291
  7.7 6.5 %copy-start.2 = (bf16[1,2,2304,256]{3,2,1,0:T(8,128)(2,1)S(1)}, bf16[1,2,2304,256]{3,2,1,0:T(8,128)(2,1)}, u32[]{:S(2)}) copy-start(bf16[1,2,2304,256]{3,2,1,0:T(8,128)(2,1)} %param.5) | copy-start | bytes 7077892
  8.7 18.7 %all-to-all-start = ((bf16[8,208,256]{2,1,0:T(8,128)(2,1)}), bf16[8,208,256]{2,1,0:T(8,128)(2,1)}, u32[]{:S(2)}, u32[]{:S(2)}) async-start(bf16[8,208,256]{2,1,0:T(8,128)(2,1)} %pieces.1), calls=%async_computation | async-start | bytes 1703936 | tf_op jit(solution)/shard_map/all_to_all | solution.py:331
  15.4 33.3 %collective-permute-start.3 = (bf16[2304,256]{1,0:T(8,128)(2,1)}, bf16[2304,256]{1,0:T(8,128)(2,1)}, u32[]{:S(2)}, u32[]{:S(2)}) collective-permute-start(bf16[2304,256]{1,0:T(8,128)(2,1)} %get-tuple-element.47), channel_id=1, source_target_pairs={{0,3},{1,0},{2,1},{3,2},{4,5},{5,6},{6,7},{7,4},{8,11},{9,8},{10,9... | collective-permute-start | bytes 3538952 | tf_op jit(solution)/shard_map/ppermute | solution.py:327
  15.8 33.0 %collective-permute-start.4 = (bf16[2304,256]{1,0:T(8,128)(2,1)S(1)}, bf16[2304,256]{1,0:T(8,128)(2,1)}, u32[]{:S(2)}, u32[]{:S(2)}) collective-permute-start(bf16[2304,256]{1,0:T(8,128)(2,1)S(1)} %get-tuple-element.46), channel_id=1, source_target_pairs={{0,3},{1,0},{2,1},{3,2},{4,5},{5,6},{6,7},{7,4},{8,11},{9,8},{10,9... | collective-permute-start | bytes 3538952 | tf_op jit(solution)/shard_map/ppermute | solution.py:327
  29.4 19.4 %all-to-all-start.1 = ((bf16[4,576,256]{2,1,0:T(8,128)(2,1)}), bf16[4,576,256]{2,1,0:T(8,128)(2,1)S(1)}, u32[]{:S(2)}, u32[]{:S(2)}) async-start(bf16[4,576,256]{2,1,0:T(8,128)(2,1)} %broadcast_in_dim.6), calls=%async_computation.1 | async-start | bytes 2359296 | tf_op jit(solution)/shard_map/all_to_all | solution.py:336
  32.9 15.8 %collective-permute-start.1 = (bf16[8,208,256]{2,1,0:T(8,128)(2,1)}, bf16[8,208,256]{2,1,0:T(8,128)(2,1)S(1)}, u32[]{:S(2)}, u32[]{:S(2)}) collective-permute-start(bf16[8,208,256]{2,1,0:T(8,128)(2,1)} %all-to-all-done.tile), channel_id=1, source_target_pairs={{0,32},{32,64},{64,96},{96,128},{128,160},{160,192},{192,224},{36,... | collective-permute-start | bytes 2555912 | tf_op jit(solution)/shard_map/ppermute | solution.py:296
  35.0 13.7 %collective-permute-start.2 = (bf16[64,256]{1,0:T(8,128)(2,1)S(1)}, bf16[64,256]{1,0:T(8,128)(2,1)S(1)}, u32[]{:S(2)}, u32[]{:S(2)}) collective-permute-start(bf16[64,256]{1,0:T(8,128)(2,1)S(1)} %select_bitcast_fusion), channel_id=1, source_target_pairs={{0,64},{32,96},{64,128},{96,160},{128,192},{160,224},{68,4},{100,3... | collective-permute-start | bytes 98312 | tf_op jit(solution)/shard_map/ppermute | solution.py:296
  48.8 8.8 %copy-start.10 = (bf16[64,256]{1,0:T(8,128)(2,1)}, bf16[64,256]{1,0:T(8,128)(2,1)S(1)}, u32[]{:S(2)}) copy-start(bf16[64,256]{1,0:T(8,128)(2,1)S(1)} %collective-permute-done.2.far) | copy-start | bytes 98308
  48.8 8.8 %copy-start.8 = (bf16[8,208,256]{2,1,0:T(8,128)(2,1)}, bf16[8,208,256]{2,1,0:T(8,128)(2,1)S(1)}, u32[]{:S(2)}) copy-start(bf16[8,208,256]{2,1,0:T(8,128)(2,1)S(1)} %collective-permute-done.1.beyond) | copy-start | bytes 2555908
  48.8 8.8 %copy-start.3 = (bf16[4,576,256]{2,1,0:T(8,128)(2,1)}, bf16[4,576,256]{2,1,0:T(8,128)(2,1)S(1)}, u32[]{:S(2)}) copy-start(bf16[4,576,256]{2,1,0:T(8,128)(2,1)S(1)} %all-to-all-done.1.quarters) | copy-start | bytes 3538948
  48.8 8.7 %collective-permute-start.7 = (bf16[2304,256]{1,0:T(8,128)(2,1)}, bf16[2304,256]{1,0:T(8,128)(2,1)S(1)}, u32[]{:S(2)}, u32[]{:S(2)}) collective-permute-start(bf16[2304,256]{1,0:T(8,128)(2,1)} %collective-permute-done.3.first), channel_id=1, source_target_pairs={{0,4},{4,0},{1,5},{5,1},{2,6},{6,2},{3,7},{7,3},{8,12},{12,8},{9,1... | collective-permute-start | bytes 3538952 | tf_op jit(solution)/shard_map/ppermute | solution.py:291
  50.4 7.1 %collective-permute-start.8 = (bf16[2304,256]{1,0:T(8,128)(2,1)}, bf16[2304,256]{1,0:T(8,128)(2,1)S(1)}, u32[]{:S(2)}, u32[]{:S(2)}) collective-permute-start(bf16[2304,256]{1,0:T(8,128)(2,1)} %collective-permute-done.4.second), channel_id=1, source_target_pairs={{0,4},{4,0},{1,5},{5,1},{2,6},{6,2},{3,7},{7,3},{8,12},{12,8},{9,1... | collective-permute-start | bytes 3538952 | tf_op jit(solution)/shard_map/ppermute | solution.py:291
  50.4 7.2 %collective-permute-start.9 = (bf16[4,576,256]{2,1,0:T(8,128)(2,1)S(1)}, bf16[4,576,256]{2,1,0:T(8,128)(2,1)S(1)}, u32[]{:S(2)}, u32[]{:S(2)}) collective-permute-start(bf16[4,576,256]{2,1,0:T(8,128)(2,1)S(1)} %all-to-all-done.1.quarters), channel_id=1, source_target_pairs={{0,4},{4,0},{1,5},{5,1},{2,6},{6,2},{3,7},{7,3},{8,12},{12,8},{9,1... | collective-permute-start | bytes 3538952 | tf_op jit(solution)/shard_map/ppermute | solution.py:291
  50.9 6.6 %collective-permute-start.5 = (bf16[8,208,256]{2,1,0:T(8,128)(2,1)S(1)}, bf16[8,208,256]{2,1,0:T(8,128)(2,1)S(1)}, u32[]{:S(2)}, u32[]{:S(2)}) collective-permute-start(bf16[8,208,256]{2,1,0:T(8,128)(2,1)S(1)} %collective-permute-done.1.beyond), channel_id=1, source_target_pairs={{0,4},{4,0},{1,5},{5,1},{2,6},{6,2},{3,7},{7,3},{8,12},{12,8},{9,1... | collective-permute-start | bytes 2555912 | tf_op jit(solution)/shard_map/ppermute | solution.py:291
  50.9 6.6 %collective-permute-start.6 = (bf16[64,256]{1,0:T(8,128)(2,1)S(1)}, bf16[64,256]{1,0:T(8,128)(2,1)S(1)}, u32[]{:S(2)}, u32[]{:S(2)}) collective-permute-start(bf16[64,256]{1,0:T(8,128)(2,1)S(1)} %collective-permute-done.2.far), channel_id=1, source_target_pairs={{0,4},{4,0},{1,5},{5,1},{2,6},{6,2},{3,7},{7,3},{8,12},{12,8},{9,1... | collective-permute-start | bytes 98312 | tf_op jit(solution)/shard_map/ppermute | solution.py:291
  57.5 1.7 %copy-start.6 = (bf16[2304,256]{1,0:T(8,128)(2,1)}, bf16[2304,256]{1,0:T(8,128)(2,1)S(1)}, u32[]{:S(2)}) copy-start(bf16[2304,256]{1,0:T(8,128)(2,1)S(1)} %collective-permute-done.8.second2) | copy-start | bytes 3538948
  57.5 2.1 %copy-start.7 = (bf16[4,576,256]{2,1,0:T(8,128)(2,1)}, bf16[4,576,256]{2,1,0:T(8,128)(2,1)S(1)}, u32[]{:S(2)}) copy-start(bf16[4,576,256]{2,1,0:T(8,128)(2,1)S(1)} %collective-permute-done.9.quarters2) | copy-start | bytes 3538948
  78.0 4.0 %copy-start.4 = (bf16[8,16,1024]{2,1,0:T(8,128)(2,1)S(1)}, bf16[8,16,1024]{2,1,0:T(8,128)(2,1)}, u32[]{:S(2)}) copy-start(bf16[8,16,1024]{2,1,0:T(8,128)(2,1)} %get-tuple-element.31) | copy-start | bytes 786436
  78.0 21.8 %all-to-all-start.2 = ((bf16[8,320,256]{2,1,0:T(8,128)(2,1)}), bf16[8,320,256]{2,1,0:T(8,128)(2,1)S(1)}, u32[]{:S(2)}, u32[]{:S(2)}) async-start(bf16[8,320,256]{2,1,0:T(8,128)(2,1)} %get-tuple-element.30), calls=%async_computation.2 | async-start | bytes 2621440 | tf_op jit(solution)/shard_map/all_to_all | solution.py:344
  82.0 6.5 %collective-permute-start.10 = (bf16[16,1024]{1,0:T(8,128)(2,1)S(1)}, bf16[16,1024]{1,0:T(8,128)(2,1)S(1)}, u32[]{:S(2)}, u32[]{:S(2)}) collective-permute-start(bf16[16,1024]{1,0:T(8,128)(2,1)S(1)} %get-tuple-element.57), channel_id=1, source_target_pairs={{0,4},{4,8},{8,12},{12,16},{16,20},{20,24},{24,28},{28,0},{1,5},{5... | collective-permute-start | bytes 98312 | tf_op jit(solution)/shard_map/ppermute | solution.py:300
  82.3 6.2 %collective-permute-start.11 = (bf16[16,1024]{1,0:T(8,128)(2,1)S(1)}, bf16[16,1024]{1,0:T(8,128)(2,1)S(1)}, u32[]{:S(2)}, u32[]{:S(2)}) collective-permute-start(bf16[16,1024]{1,0:T(8,128)(2,1)S(1)} %get-tuple-element.56), channel_id=1, source_target_pairs={{0,8},{4,12},{8,16},{12,20},{16,24},{20,28},{24,0},{28,4},{1,9},{5... | collective-permute-start | bytes 98312 | tf_op jit(solution)/shard_map/ppermute | solution.py:300
  83.1 6.7 %collective-permute-start.12 = (bf16[16,1024]{1,0:T(8,128)(2,1)S(1)}, bf16[16,1024]{1,0:T(8,128)(2,1)S(1)}, u32[]{:S(2)}, u32[]{:S(2)}) collective-permute-start(bf16[16,1024]{1,0:T(8,128)(2,1)S(1)} %get-tuple-element.55), channel_id=1, source_target_pairs={{0,12},{4,16},{8,20},{12,24},{16,28},{20,0},{24,4},{28,8},{1,13},{... | collective-permute-start | bytes 98312 | tf_op jit(solution)/shard_map/ppermute | solution.py:300
  85.0 4.8 %collective-permute-start.13 = (bf16[16,1024]{1,0:T(8,128)(2,1)S(1)}, bf16[16,1024]{1,0:T(8,128)(2,1)S(1)}, u32[]{:S(2)}, u32[]{:S(2)}) collective-permute-start(bf16[16,1024]{1,0:T(8,128)(2,1)S(1)} %get-tuple-element.54), channel_id=1, source_target_pairs={{0,16},{4,20},{8,24},{12,28},{16,0},{20,4},{24,8},{28,12},{1,17},{... | collective-permute-start | bytes 98312 | tf_op jit(solution)/shard_map/ppermute | solution.py:300
  86.0 5.1 %collective-permute-start.14 = (bf16[16,1024]{1,0:T(8,128)(2,1)S(1)}, bf16[16,1024]{1,0:T(8,128)(2,1)S(1)}, u32[]{:S(2)}, u32[]{:S(2)}) collective-permute-start(bf16[16,1024]{1,0:T(8,128)(2,1)S(1)} %get-tuple-element.53), channel_id=1, source_target_pairs={{0,20},{4,24},{8,28},{12,0},{16,4},{20,8},{24,12},{28,16},{1,21},{... | collective-permute-start | bytes 98312 | tf_op jit(solution)/shard_map/ppermute | solution.py:300
  88.5 3.1 %collective-permute-start.15 = (bf16[16,1024]{1,0:T(8,128)(2,1)S(1)}, bf16[16,1024]{1,0:T(8,128)(2,1)S(1)}, u32[]{:S(2)}, u32[]{:S(2)}) collective-permute-start(bf16[16,1024]{1,0:T(8,128)(2,1)S(1)} %get-tuple-element.52), channel_id=1, source_target_pairs={{0,24},{4,28},{8,0},{12,4},{16,8},{20,12},{24,16},{28,20},{1,25},{... | collective-permute-start | bytes 98312 | tf_op jit(solution)/shard_map/ppermute | solution.py:300
  88.5 3.8 %collective-permute-start.16 = (bf16[16,1024]{1,0:T(8,128)(2,1)S(1)}, bf16[16,1024]{1,0:T(8,128)(2,1)S(1)}, u32[]{:S(2)}, u32[]{:S(2)}) collective-permute-start(bf16[16,1024]{1,0:T(8,128)(2,1)S(1)} %get-tuple-element.51), channel_id=1, source_target_pairs={{0,28},{4,0},{8,4},{12,8},{16,12},{20,16},{24,20},{28,24},{1,29},{... | collective-permute-start | bytes 98312 | tf_op jit(solution)/shard_map/ppermute | solution.py:300
  101.6 9.9 %collective-permute-start.17 = (bf16[8,72,256]{2,1,0:T(8,128)(2,1)S(1)}, bf16[8,72,256]{2,1,0:T(8,128)(2,1)S(1)}, u32[]{:S(2)}, u32[]{:S(2)}) collective-permute-start(bf16[8,72,256]{2,1,0:T(8,128)(2,1)S(1)} %get-tuple-element.48), channel_id=1, source_target_pairs={{0,8},{8,16},{16,24},{24,0},{1,9},{9,17},{17,25},{25,1},{2,10},{10... | collective-permute-start | bytes 884744 | tf_op jit(solution)/shard_map/ppermute | solution.py:291
  102.0 15.1 %collective-permute-start.18 = (bf16[8,72,256]{2,1,0:T(8,128)(2,1)S(1)}, bf16[8,72,256]{2,1,0:T(8,128)(2,1)S(1)}, u32[]{:S(2)}, u32[]{:S(2)}) collective-permute-start(bf16[8,72,256]{2,1,0:T(8,128)(2,1)S(1)} %get-tuple-element.50), channel_id=1, source_target_pairs={{0,16},{8,24},{16,0},{24,8},{1,17},{9,25},{17,1},{25,9},{2,18},{10... | collective-permute-start | bytes 884744 | tf_op jit(solution)/shard_map/ppermute | solution.py:291
  103.9 13.8 %collective-permute-start.19 = (bf16[8,72,256]{2,1,0:T(8,128)(2,1)S(1)}, bf16[8,72,256]{2,1,0:T(8,128)(2,1)S(1)}, u32[]{:S(2)}, u32[]{:S(2)}) collective-permute-start(bf16[8,72,256]{2,1,0:T(8,128)(2,1)S(1)} %get-tuple-element.49), channel_id=1, source_target_pairs={{0,24},{8,0},{16,8},{24,16},{1,25},{9,1},{17,9},{25,17},{2,26},{10... | collective-permute-start | bytes 884744 | tf_op jit(solution)/shard_map/ppermute | solution.py:291
  118.6 20.2 %all-to-all-start.3 = ((bf16[8,72,256]{2,1,0:T(8,128)(2,1)}), bf16[8,72,256]{2,1,0:T(8,128)(2,1)S(1)}, u32[]{:S(2)}, u32[]{:S(2)}) async-start(bf16[8,72,256]{2,1,0:T(8,128)(2,1)} %fusion.2), calls=%async_computation.3 | async-start | bytes 589824 | tf_op jit(solution)/shard_map/all_to_all | solution.py:350
  138.9 3.9 %collective-permute-start.20 = (f32[36,256]{1,0:T(8,128)S(1)}, f32[36,256]{1,0:T(8,128)S(1)}, u32[]{:S(2)}, u32[]{:S(2)}) collective-permute-start(f32[36,256]{1,0:T(8,128)S(1)} %get-tuple-element.60), channel_id=1, source_target_pairs={{0,4},{4,0},{1,5},{5,1},{2,6},{6,2},{3,7},{7,3},{8,12},{12,8},{9,1... | collective-permute-start | bytes 110600 | tf_op jit(solution)/shard_map/ppermute | solution.py:291
  (5 other events, 4.6 us)

commit v4 on v3

--- a/solution.py
+++ b/solution.py
@@ -33,7 +33,10 @@
     return out
 
 
-def pieces_kernel(field, cotangent, out, padded):
+def pieces_kernel(field, cotangent, held, out, part, padded, sem):
+    at = pl.multiple_of(QUARTER * lax.axis_index("y"), QUARTER)
+    quarter = pltpu.make_async_copy(held.at[lax.axis_index("core"), pl.ds(at, QUARTER)], part, sem)
+    quarter.start()
     padded[0:16] = jnp.zeros((16, 4 * C), f32)
     padded[144:160] = jnp.zeros((16, 4 * C), f32)
     padded[16:144, 0:2 * C] = field[...].astype(f32)
@@ -45,18 +48,35 @@
         piece = jnp.concatenate(piece, axis=0)
         out[2 * chip] = piece
         out[2 * chip + 1] = piece
-
-
-def make_pieces(field, cotangent):
+    quarter.wait()
+
+
+def make_pieces(field, cotangent, held):
     return pl.pallas_call(
         pieces_kernel,
-        out_shape=jax.ShapeDtypeStruct((8, PIECE, C), bf16),
-        in_specs=[VMEM, VMEM],
-        out_specs=VMEM,
-        scratch_shapes=[pltpu.VMEM((160, 4 * C), f32)],
+        out_shape=[jax.ShapeDtypeStruct((8, PIECE, C), bf16), jax.ShapeDtypeStruct((QUARTER, C), bf16)],
+        in_specs=[VMEM, VMEM, ANY],
+        out_specs=[VMEM, VMEM],
+        scratch_shapes=[pltpu.VMEM((160, 4 * C), f32), pltpu.SemaphoreType.DMA],
         compiler_params=PARAMS,
         name="pieces",
-    )(field, cotangent)
+    )(field, cotangent, held)
+
+
+def repeat_kernel(part, out):
+    for i in range(4):
+        out[i] = part[...]
+
+
+def repeat(part):
+    return pl.pallas_call(
+        repeat_kernel,
+        out_shape=jax.ShapeDtypeStruct((4, QUARTER, C), bf16),
+        in_specs=[VMEM],
+        out_specs=VMEM,
+        compiler_params=PARAMS,
+        name="repeat",
+    )(part)
 
 
 def blocks_kernel(tile, beyond, beyond2, far, far2, held, first, first2, second, second2, quarters, quarters2,
@@ -320,16 +340,16 @@
 
 
 def local(block_out, out_grad, weights):
-    y, core = lax.axis_index("y"), lax.axis_index("core")
-
-    part = lax.dynamic_slice(weights[0], (core, QUARTER * y, 0), (1, QUARTER, C))[0]
+    core = lax.axis_index("core")
+
+    pieces, part = make_pieces(block_out[0, 0], out_grad[0, 0], weights[0])
     part = turn(part, "section", 2)
     beside = [lax.ppermute(weights[0, i], ("core", "section"),
                            [(4 * c + i, 4 * c + (i + (-1, 1)[c]) % 4) for c in range(2) for i in range(4)])
               for i in range(2)]
 
-    tile = lax.all_to_all(make_pieces(block_out[0, 0], out_grad[0, 0]), ("y", "core"), 0, 0)
-    part = jnp.broadcast_to(part[None], (4, QUARTER, C))
+    tile = lax.all_to_all(pieces, ("y", "core"), 0, 0)
+    part = repeat(part)
     tile, part = lax.optimization_barrier((tile, part))
     beyond = apart(tile, 1)
     far = apart(jnp.where(core == 0, tile[7, :WIDE + 16], tile[0, :WIDE + 16]), 2)

time: 144 us -> 142 us (0.986)
  waiting for transfers between devices: 62.6 us -> 59.9 us
  local copies, waits for them, and re-layouts: 9.66 us -> 7.53 us
    broadcast_in_dim x1 -> x0, local copies, waits for them, and re-layouts: 2.06 us -> none  [local(): part = jnp.broadcast_to(part[None], (4, QUARTER, C))]
    squeeze x1 -> x0, local copies, waits for them, and re-layouts: 1.71 us -> none  [local(): lax.dynamic_slice(weights[0], (core, QUARTER * y, 0), (1, QUARTER, C))[0]]
    all_to_all x1, waiting for transfers between devices: 10.6 us -> 9.14 us  [local(): tile = lax.all_to_all(pieces, ('y', 'core'), 0, 0)]
    unnamed x25 -> x29, local copies, waits for them, and re-layouts: 4.6 us -> 5.89 us
  transfers between devices with their start and end apart: 25 -> 25, of which waited for: 12 -> 14; matrix products, arithmetic and copies ran while one was open for 3% -> 2% of each run, Pallas kernels for 1% -> 1%
where the time goes in v4:
time: 142 us; the launch traced here: 141 us
  waiting for transfers between devices  59.9 us (42%)
  starting transfers between devices  48.1 us (34%)
  Pallas kernels  22.9 us (16%)
  local copies, waits for them, and re-layouts  7.53 us (5%)
  other arithmetic  1.69 us (1%)
    pallas_call x1, Pallas kernels, blocks(): pl.pallas_call(blocks_kernel, out_shape=[jax.ShapeDtypeStruct((8, 16, 4 *...  18.3 us
    ppermute x10, waiting for transfers between devices, turn(): lax.ppermute(value, axis, [(i, (i + by) % size) for i in range(size)])  18.2 us
    ppermute x10, starting transfers between devices, turn(): lax.ppermute(value, axis, [(i, (i + by) % size) for i in range(size)])  12.7 us
    ppermute x2, waiting for transfers between devices, apart(): return lax.ppermute(value, ('z', 'core'), pairs)  12.5 us
    all_to_all x1, waiting for transfers between devices, local(): grad = lax.all_to_all(grad, 'z', 0, 0).astype(f32).sum(axis=0)  10.6 us
    all_to_all x1, starting transfers between devices, local(): grad = lax.all_to_all(grad, 'z', 0, 0).astype(f32).sum(axis=0)  10.2 us
    all_to_all x1, waiting for transfers between devices, local(): tile = lax.all_to_all(pieces, ('y', 'core'), 0, 0)  9.14 us
    ppermute x7, starting transfers between devices, around(): lax.ppermute(value, ('y', 'core'), [(i, (i + by) % 8) for i in range(8)])  8.36 us
  transfers between devices with their start and end apart: 25, of which 14 were waited for; matrix products, arithmetic and copies ran while one was open for 2% of the time, Pallas kernels for 1%

profile of v4, /device:TPU:1, one launch (start us, length us, event | category | flops | bytes accessed | tf_op | source)
XLA Modules:
  0.0 140.9 jit_solution(9150729977328646818)
XLA Ops:
  0.6 1.7 %copy-done = bf16[1,2,2304,256]{3,2,1,0:T(8,128)(2,1)S(1)} copy-done((bf16[1,2,2304,256]{3,2,1,0:T(8,128)(2,1)S(1)}, bf16[1,2,2304,256]{3,2,1,0:T(8,128)(2,1)}, u32[]{:S(2)}) %copy-start) | copy-done | bytes 2359320
  4.1 1.0 pieces.1
  5.2 3.7 %collective-permute-start = (bf16[576,256]{1,0:T(8,128)(2,1)S(1)}, bf16[576,256]{1,0:T(8,128)(2,1)S(1)}, u32[]{:S(2)}, u32[]{:S(2)}) collective-permute-start(bf16[576,256]{1,0:T(8,128)(2,1)S(1)} %get-tuple-element.26), channel_id=1, source_target_pairs={{0,2},{1,3},{2,0},{3,1},{4,6},{5,7},{6,4},{7,5},{8,10},{9,11},{10,... | collective-permute-start | bytes 884744 | tf_op jit(solution)/shard_map/ppermute | solution.py:311
  8.8 5.4 %all-to-all-start = ((bf16[8,208,256]{2,1,0:T(8,128)(2,1)}), bf16[8,208,256]{2,1,0:T(8,128)(2,1)}, u32[]{:S(2)}, u32[]{:S(2)}) async-start(bf16[8,208,256]{2,1,0:T(8,128)(2,1)} %get-tuple-element.25), calls=%async_computation | async-start | bytes 1703936 | tf_op jit(solution)/shard_map/all_to_all | solution.py:351
  14.2 1.5 %slice_bitcast_fusion = (bf16[2304,256]{1,0:T(8,128)(2,1)}, bf16[2304,256]{1,0:T(8,128)(2,1)}) fusion(bf16[1,2,2304,256]{3,2,1,0:T(8,128)(2,1)S(1)} %copy-done.1), kind=kLoop, calls=%fused_computation | loop fusion | bytes 4718592 | tf_op jit(solution)/shard_map/squeeze | solution.py:347
  16.1 1.0 collective-permute-start.4
  17.1 1.1 repeat.1
  18.2 9.1 %all-to-all-done.tile = bf16[8,208,256]{2,1,0:T(8,128)(2,1)} async-done(((bf16[8,208,256]{2,1,0:T(8,128)(2,1)}), bf16[8,208,256]{2,1,0:T(8,128)(2,1)}, u32[]{:S(2)}, u32[]{:S(2)}) %all-to-all-start) | async-done | bytes 852000 | tf_op jit(solution)/shard_map/all_to_all | solution.py:351
  27.3 3.5 %all-to-all-start.1 = ((bf16[4,576,256]{2,1,0:T(8,128)(2,1)}), bf16[4,576,256]{2,1,0:T(8,128)(2,1)S(1)}, u32[]{:S(2)}, u32[]{:S(2)}) async-start(bf16[4,576,256]{2,1,0:T(8,128)(2,1)} %repeat.1), calls=%async_computation.1 | async-start | bytes 2359296 | tf_op jit(solution)/shard_map/all_to_all | solution.py:356
  30.9 1.3 collective-permute-start.1
  33.0 1.3 collective-permute-start.2
  34.2 12.5 %collective-permute-done.2.far = bf16[64,256]{1,0:T(8,128)(2,1)S(1)} collective-permute-done((bf16[64,256]{1,0:T(8,128)(2,1)S(1)}, bf16[64,256]{1,0:T(8,128)(2,1)S(1)}, u32[]{:S(2)}, u32[]{:S(2)}) %collective-permute-start.2) | collective-permute-done | bytes 32800 | tf_op jit(solution)/shard_map/ppermute | solution.py:316
  49.3 4.2 %collective-permute-done.6.far2 = bf16[64,256]{1,0:T(8,128)(2,1)S(1)} collective-permute-done((bf16[64,256]{1,0:T(8,128)(2,1)}, bf16[64,256]{1,0:T(8,128)(2,1)S(1)}, u32[]{:S(2)}, u32[]{:S(2)}) %collective-permute-start.6) | collective-permute-done | bytes 32800 | tf_op jit(solution)/shard_map/ppermute | solution.py:311
  53.7 1.7 %collective-permute-done.9.quarters2 = bf16[4,576,256]{2,1,0:T(8,128)(2,1)S(1)} collective-permute-done((bf16[4,576,256]{2,1,0:T(8,128)(2,1)S(1)}, bf16[4,576,256]{2,1,0:T(8,128)(2,1)S(1)}, u32[]{:S(2)}, u32[]{:S(2)}) %collective-permute-start.9) | collective-permute-done | bytes 1179680 | tf_op jit(solution)/shard_map/ppermute | solution.py:311
  55.5 1.1 copy-done.10
  56.6 18.3 %blocks.1 = (bf16[8,16,1024]{2,1,0:T(8,128)(2,1)}, bf16[8,320,256]{2,1,0:T(8,128)(2,1)}) custom-call(bf16[8,208,256]{2,1,0:T(8,128)(2,1)} %all-to-all-done.tile, bf16[8,208,256]{2,1,0:T(8,128)(2,1)} %collective-permute-done.1.beyond, bf16[8,208,256]{2,1,0:T(8,128)(2,1)} %copy-done.11, bf16[64,256]{1,0:T(8,128)(2,1)} %copy-done.12, ...), custom_call_target="tpu_custom_call" | custom-call | flops 9059696640 | bytes 16777216 | tf_op jit(solution)/shard_map/blocks/pallas_call | solution.py:260
  74.9 4.0 %all-to-all-start.2 = ((bf16[8,320,256]{2,1,0:T(8,128)(2,1)}), bf16[8,320,256]{2,1,0:T(8,128)(2,1)S(1)}, u32[]{:S(2)}, u32[]{:S(2)}) async-start(bf16[8,320,256]{2,1,0:T(8,128)(2,1)} %get-tuple-element.34), calls=%async_computation.2 | async-start | bytes 2621440 | tf_op jit(solution)/shard_map/all_to_all | solution.py:364
  79.6 1.0 collective-permute-start.11
  80.6 1.9 %collective-permute-start.12 = (bf16[16,1024]{1,0:T(8,128)(2,1)S(1)}, bf16[16,1024]{1,0:T(8,128)(2,1)S(1)}, u32[]{:S(2)}, u32[]{:S(2)}) collective-permute-start(bf16[16,1024]{1,0:T(8,128)(2,1)S(1)} %get-tuple-element.59), channel_id=1, source_target_pairs={{0,12},{4,16},{8,20},{12,24},{16,28},{20,0},{24,4},{28,8},{1,13},{... | collective-permute-start | bytes 98312 | tf_op jit(solution)/shard_map/ppermute | solution.py:320
  83.3 2.2 %collective-permute-start.14 = (bf16[16,1024]{1,0:T(8,128)(2,1)S(1)}, bf16[16,1024]{1,0:T(8,128)(2,1)S(1)}, u32[]{:S(2)}, u32[]{:S(2)}) collective-permute-start(bf16[16,1024]{1,0:T(8,128)(2,1)S(1)} %get-tuple-element.57), channel_id=1, source_target_pairs={{0,20},{4,24},{8,28},{12,0},{16,4},{20,8},{24,12},{28,16},{1,21},{... | collective-permute-start | bytes 98312 | tf_op jit(solution)/shard_map/ppermute | solution.py:320
  85.5 1.9 %collective-permute-start.16 = (bf16[16,1024]{1,0:T(8,128)(2,1)S(1)}, bf16[16,1024]{1,0:T(8,128)(2,1)S(1)}, u32[]{:S(2)}, u32[]{:S(2)}) collective-permute-start(bf16[16,1024]{1,0:T(8,128)(2,1)S(1)} %get-tuple-element.55), channel_id=1, source_target_pairs={{0,28},{4,0},{8,4},{12,8},{16,12},{20,16},{24,20},{28,24},{1,29},{... | collective-permute-start | bytes 98312 | tf_op jit(solution)/shard_map/ppermute | solution.py:320
  87.3 1.1 collective-permute-done.14.refs_5_
  88.5 1.2 collective-permute-done.16.refs_7_
  89.7 7.0 %all-to-all-done.2.acts = bf16[8,320,256]{2,1,0:T(8,128)(2,1)S(1)} async-done(((bf16[8,320,256]{2,1,0:T(8,128)(2,1)}), bf16[8,320,256]{2,1,0:T(8,128)(2,1)S(1)}, u32[]{:S(2)}, u32[]{:S(2)}) %all-to-all-start.2) | async-done | bytes 1310752 | tf_op jit(solution)/shard_map/all_to_all | solution.py:364
  96.7 1.7 %kernel_grads.1 = bf16[4,8,72,256]{3,2,1,0:T(8,128)(2,1)S(1)} custom-call(bf16[8,320,256]{2,1,0:T(8,128)(2,1)S(1)} %all-to-all-done.2.acts), custom_call_target="tpu_custom_call" | custom-call | flops 1207959552 | bytes 8388608 | tf_op jit(solution)/shard_map/kernel_grads/pallas_call | solution.py:297
  99.2 2.2 %collective-permute-start.18 = (bf16[8,72,256]{2,1,0:T(8,128)(2,1)S(1)}, bf16[8,72,256]{2,1,0:T(8,128)(2,1)S(1)}, u32[]{:S(2)}, u32[]{:S(2)}) collective-permute-start(bf16[8,72,256]{2,1,0:T(8,128)(2,1)S(1)} %get-tuple-element.54), channel_id=1, source_target_pairs={{0,16},{8,24},{16,0},{24,8},{1,17},{9,25},{17,1},{25,9},{2,18},{10... | collective-permute-start | bytes 884744 | tf_op jit(solution)/shard_map/ppermute | solution.py:311
  101.4 1.2 collective-permute-start.19
  102.6 5.4 %collective-permute-done.17 = bf16[8,72,256]{2,1,0:T(8,128)(2,1)S(1)} collective-permute-done((bf16[8,72,256]{2,1,0:T(8,128)(2,1)S(1)}, bf16[8,72,256]{2,1,0:T(8,128)(2,1)S(1)}, u32[]{:S(2)}, u32[]{:S(2)}) %collective-permute-start.17) | collective-permute-done | bytes 294944 | tf_op jit(solution)/shard_map/ppermute | solution.py:311
  108.0 6.5 %collective-permute-done.18 = bf16[8,72,256]{2,1,0:T(8,128)(2,1)S(1)} collective-permute-done((bf16[8,72,256]{2,1,0:T(8,128)(2,1)S(1)}, bf16[8,72,256]{2,1,0:T(8,128)(2,1)S(1)}, u32[]{:S(2)}, u32[]{:S(2)}) %collective-permute-start.18) | collective-permute-done | bytes 294944 | tf_op jit(solution)/shard_map/ppermute | solution.py:311
  115.5 10.2 %all-to-all-start.3 = ((bf16[8,72,256]{2,1,0:T(8,128)(2,1)}), bf16[8,72,256]{2,1,0:T(8,128)(2,1)S(1)}, u32[]{:S(2)}, u32[]{:S(2)}) async-start(bf16[8,72,256]{2,1,0:T(8,128)(2,1)} %fusion.2), calls=%async_computation.3 | async-start | bytes 589824 | tf_op jit(solution)/shard_map/all_to_all | solution.py:370
  125.7 10.6 %all-to-all-done.3 = bf16[8,72,256]{2,1,0:T(8,128)(2,1)S(1)} async-done(((bf16[8,72,256]{2,1,0:T(8,128)(2,1)}), bf16[8,72,256]{2,1,0:T(8,128)(2,1)S(1)}, u32[]{:S(2)}, u32[]{:S(2)}) %all-to-all-start.3) | async-done | bytes 294944 | tf_op jit(solution)/shard_map/all_to_all | solution.py:370
  136.4 3.0 %collective-permute-start.20 = (f32[36,256]{1,0:T(8,128)S(1)}, f32[36,256]{1,0:T(8,128)S(1)}, u32[]{:S(2)}, u32[]{:S(2)}) collective-permute-start(f32[36,256]{1,0:T(8,128)S(1)} %get-tuple-element.64), channel_id=1, source_target_pairs={{0,4},{4,0},{1,5},{5,1},{2,6},{6,2},{3,7},{7,3},{8,12},{12,8},{9,1... | collective-permute-start | bytes 110600 | tf_op jit(solution)/shard_map/ppermute | solution.py:311
  (60 shorter events, 10.7 us)
Async XLA Ops:
  4.1 10.1 %copy-start.1 = (bf16[1,2,2304,256]{3,2,1,0:T(8,128)(2,1)S(1)}, bf16[1,2,2304,256]{3,2,1,0:T(8,128)(2,1)}, u32[]{:S(2)}) copy-start(bf16[1,2,2304,256]{3,2,1,0:T(8,128)(2,1)} %param.5) | copy-start | bytes 7077892
  5.2 11.9 %collective-permute-start = (bf16[576,256]{1,0:T(8,128)(2,1)S(1)}, bf16[576,256]{1,0:T(8,128)(2,1)S(1)}, u32[]{:S(2)}, u32[]{:S(2)}) collective-permute-start(bf16[576,256]{1,0:T(8,128)(2,1)S(1)} %get-tuple-element.26), channel_id=1, source_target_pairs={{0,2},{1,3},{2,0},{3,1},{4,6},{5,7},{6,4},{7,5},{8,10},{9,11},{10,... | collective-permute-start | bytes 884744 | tf_op jit(solution)/shard_map/ppermute | solution.py:311
  8.8 18.5 %all-to-all-start = ((bf16[8,208,256]{2,1,0:T(8,128)(2,1)}), bf16[8,208,256]{2,1,0:T(8,128)(2,1)}, u32[]{:S(2)}, u32[]{:S(2)}) async-start(bf16[8,208,256]{2,1,0:T(8,128)(2,1)} %get-tuple-element.25), calls=%async_computation | async-start | bytes 1703936 | tf_op jit(solution)/shard_map/all_to_all | solution.py:351
  15.8 30.9 %collective-permute-start.3 = (bf16[2304,256]{1,0:T(8,128)(2,1)}, bf16[2304,256]{1,0:T(8,128)(2,1)S(1)}, u32[]{:S(2)}, u32[]{:S(2)}) collective-permute-start(bf16[2304,256]{1,0:T(8,128)(2,1)} %get-tuple-element.51), channel_id=1, source_target_pairs={{0,3},{1,0},{2,1},{3,2},{4,5},{5,6},{6,7},{7,4},{8,11},{9,8},{10,9... | collective-permute-start | bytes 3538952 | tf_op jit(solution)/shard_map/ppermute | solution.py:347
  16.1 30.6 %collective-permute-start.4 = (bf16[2304,256]{1,0:T(8,128)(2,1)}, bf16[2304,256]{1,0:T(8,128)(2,1)S(1)}, u32[]{:S(2)}, u32[]{:S(2)}) collective-permute-start(bf16[2304,256]{1,0:T(8,128)(2,1)} %get-tuple-element.50), channel_id=1, source_target_pairs={{0,3},{1,0},{2,1},{3,2},{4,5},{5,6},{6,7},{7,4},{8,11},{9,8},{10,9... | collective-permute-start | bytes 3538952 | tf_op jit(solution)/shard_map/ppermute | solution.py:347
  27.3 20.0 %all-to-all-start.1 = ((bf16[4,576,256]{2,1,0:T(8,128)(2,1)}), bf16[4,576,256]{2,1,0:T(8,128)(2,1)S(1)}, u32[]{:S(2)}, u32[]{:S(2)}) async-start(bf16[4,576,256]{2,1,0:T(8,128)(2,1)} %repeat.1), calls=%async_computation.1 | async-start | bytes 2359296 | tf_op jit(solution)/shard_map/all_to_all | solution.py:356
  30.9 16.5 %collective-permute-start.1 = (bf16[8,208,256]{2,1,0:T(8,128)(2,1)}, bf16[8,208,256]{2,1,0:T(8,128)(2,1)}, u32[]{:S(2)}, u32[]{:S(2)}) collective-permute-start(bf16[8,208,256]{2,1,0:T(8,128)(2,1)} %all-to-all-done.tile), channel_id=1, source_target_pairs={{0,32},{32,64},{64,96},{96,128},{128,160},{160,192},{192,224},{36,... | collective-permute-start | bytes 2555912 | tf_op jit(solution)/shard_map/ppermute | solution.py:316
  33.0 13.7 %collective-permute-start.2 = (bf16[64,256]{1,0:T(8,128)(2,1)S(1)}, bf16[64,256]{1,0:T(8,128)(2,1)S(1)}, u32[]{:S(2)}, u32[]{:S(2)}) collective-permute-start(bf16[64,256]{1,0:T(8,128)(2,1)S(1)} %select_bitcast_fusion), channel_id=1, source_target_pairs={{0,64},{32,96},{64,128},{96,160},{128,192},{160,224},{68,4},{100,3... | collective-permute-start | bytes 98312 | tf_op jit(solution)/shard_map/ppermute | solution.py:316
  46.7 8.7 %copy-start.6 = (bf16[2304,256]{1,0:T(8,128)(2,1)}, bf16[2304,256]{1,0:T(8,128)(2,1)S(1)}, u32[]{:S(2)}) copy-start(bf16[2304,256]{1,0:T(8,128)(2,1)S(1)} %collective-permute-done.3.first) | copy-start | bytes 3538948
  47.3 8.1 %copy-start.7 = (bf16[2304,256]{1,0:T(8,128)(2,1)}, bf16[2304,256]{1,0:T(8,128)(2,1)S(1)}, u32[]{:S(2)}) copy-start(bf16[2304,256]{1,0:T(8,128)(2,1)S(1)} %collective-permute-done.4.second) | copy-start | bytes 3538948
  47.3 8.1 %copy-start.4 = (bf16[4,576,256]{2,1,0:T(8,128)(2,1)}, bf16[4,576,256]{2,1,0:T(8,128)(2,1)S(1)}, u32[]{:S(2)}) copy-start(bf16[4,576,256]{2,1,0:T(8,128)(2,1)S(1)} %all-to-all-done.1.quarters) | copy-start | bytes 3538948
  47.3 6.2 %collective-permute-start.7 = (bf16[2304,256]{1,0:T(8,128)(2,1)S(1)}, bf16[2304,256]{1,0:T(8,128)(2,1)S(1)}, u32[]{:S(2)}, u32[]{:S(2)}) collective-permute-start(bf16[2304,256]{1,0:T(8,128)(2,1)S(1)} %collective-permute-done.3.first), channel_id=1, source_target_pairs={{0,4},{4,0},{1,5},{5,1},{2,6},{6,2},{3,7},{7,3},{8,12},{12,8},{9,1... | collective-permute-start | bytes 3538952 | tf_op jit(solution)/shard_map/ppermute | solution.py:311
  48.3 5.4 %collective-permute-start.8 = (bf16[2304,256]{1,0:T(8,128)(2,1)S(1)}, bf16[2304,256]{1,0:T(8,128)(2,1)S(1)}, u32[]{:S(2)}, u32[]{:S(2)}) collective-permute-start(bf16[2304,256]{1,0:T(8,128)(2,1)S(1)} %collective-permute-done.4.second), channel_id=1, source_target_pairs={{0,4},{4,0},{1,5},{5,1},{2,6},{6,2},{3,7},{7,3},{8,12},{12,8},{9,1... | collective-permute-start | bytes 3538952 | tf_op jit(solution)/shard_map/ppermute | solution.py:311
  48.3 7.1 %collective-permute-start.9 = (bf16[4,576,256]{2,1,0:T(8,128)(2,1)S(1)}, bf16[4,576,256]{2,1,0:T(8,128)(2,1)S(1)}, u32[]{:S(2)}, u32[]{:S(2)}) collective-permute-start(bf16[4,576,256]{2,1,0:T(8,128)(2,1)S(1)} %all-to-all-done.1.quarters), channel_id=1, source_target_pairs={{0,4},{4,0},{1,5},{5,1},{2,6},{6,2},{3,7},{7,3},{8,12},{12,8},{9,1... | collective-permute-start | bytes 3538952 | tf_op jit(solution)/shard_map/ppermute | solution.py:311
  48.8 4.7 %collective-permute-start.5 = (bf16[8,208,256]{2,1,0:T(8,128)(2,1)}, bf16[8,208,256]{2,1,0:T(8,128)(2,1)S(1)}, u32[]{:S(2)}, u32[]{:S(2)}) collective-permute-start(bf16[8,208,256]{2,1,0:T(8,128)(2,1)} %collective-permute-done.1.beyond), channel_id=1, source_target_pairs={{0,4},{4,0},{1,5},{5,1},{2,6},{6,2},{3,7},{7,3},{8,12},{12,8},{9,1... | collective-permute-start | bytes 2555912 | tf_op jit(solution)/shard_map/ppermute | solution.py:311
  48.8 4.7 %collective-permute-start.6 = (bf16[64,256]{1,0:T(8,128)(2,1)}, bf16[64,256]{1,0:T(8,128)(2,1)S(1)}, u32[]{:S(2)}, u32[]{:S(2)}) collective-permute-start(bf16[64,256]{1,0:T(8,128)(2,1)} %copy-done.12), channel_id=1, source_target_pairs={{0,4},{4,0},{1,5},{5,1},{2,6},{6,2},{3,7},{7,3},{8,12},{12,8},{9,1... | collective-permute-start | bytes 98312 | tf_op jit(solution)/shard_map/ppermute | solution.py:311
  53.5 1.9 %copy-start.13 = (bf16[64,256]{1,0:T(8,128)(2,1)}, bf16[64,256]{1,0:T(8,128)(2,1)S(1)}, u32[]{:S(2)}) copy-start(bf16[64,256]{1,0:T(8,128)(2,1)S(1)} %collective-permute-done.6.far2) | copy-start | bytes 98308
  53.5 1.9 %copy-start.8 = (bf16[2304,256]{1,0:T(8,128)(2,1)}, bf16[2304,256]{1,0:T(8,128)(2,1)S(1)}, u32[]{:S(2)}) copy-start(bf16[2304,256]{1,0:T(8,128)(2,1)S(1)} %collective-permute-done.7.first2) | copy-start | bytes 3538948
  74.9 4.0 %copy-start.5 = (bf16[8,16,1024]{2,1,0:T(8,128)(2,1)S(1)}, bf16[8,16,1024]{2,1,0:T(8,128)(2,1)}, u32[]{:S(2)}) copy-start(bf16[8,16,1024]{2,1,0:T(8,128)(2,1)} %get-tuple-element.35) | copy-start | bytes 786436
  74.9 21.8 %all-to-all-start.2 = ((bf16[8,320,256]{2,1,0:T(8,128)(2,1)}), bf16[8,320,256]{2,1,0:T(8,128)(2,1)S(1)}, u32[]{:S(2)}, u32[]{:S(2)}) async-start(bf16[8,320,256]{2,1,0:T(8,128)(2,1)} %get-tuple-element.34), calls=%async_computation.2 | async-start | bytes 2621440 | tf_op jit(solution)/shard_map/all_to_all | solution.py:364
  79.0 6.5 %collective-permute-start.10 = (bf16[16,1024]{1,0:T(8,128)(2,1)S(1)}, bf16[16,1024]{1,0:T(8,128)(2,1)S(1)}, u32[]{:S(2)}, u32[]{:S(2)}) collective-permute-start(bf16[16,1024]{1,0:T(8,128)(2,1)S(1)} %get-tuple-element.61), channel_id=1, source_target_pairs={{0,4},{4,8},{8,12},{12,16},{16,20},{20,24},{24,28},{28,0},{1,5},{5... | collective-permute-start | bytes 98312 | tf_op jit(solution)/shard_map/ppermute | solution.py:320
  79.6 5.8 %collective-permute-start.11 = (bf16[16,1024]{1,0:T(8,128)(2,1)S(1)}, bf16[16,1024]{1,0:T(8,128)(2,1)S(1)}, u32[]{:S(2)}, u32[]{:S(2)}) collective-permute-start(bf16[16,1024]{1,0:T(8,128)(2,1)S(1)} %get-tuple-element.60), channel_id=1, source_target_pairs={{0,8},{4,12},{8,16},{12,20},{16,24},{20,28},{24,0},{28,4},{1,9},{5... | collective-permute-start | bytes 98312 | tf_op jit(solution)/shard_map/ppermute | solution.py:320
  80.6 6.7 %collective-permute-start.12 = (bf16[16,1024]{1,0:T(8,128)(2,1)S(1)}, bf16[16,1024]{1,0:T(8,128)(2,1)S(1)}, u32[]{:S(2)}, u32[]{:S(2)}) collective-permute-start(bf16[16,1024]{1,0:T(8,128)(2,1)S(1)} %get-tuple-element.59), channel_id=1, source_target_pairs={{0,12},{4,16},{8,20},{12,24},{16,28},{20,0},{24,4},{28,8},{1,13},{... | collective-permute-start | bytes 98312 | tf_op jit(solution)/shard_map/ppermute | solution.py:320
  82.5 4.8 %collective-permute-start.13 = (bf16[16,1024]{1,0:T(8,128)(2,1)S(1)}, bf16[16,1024]{1,0:T(8,128)(2,1)S(1)}, u32[]{:S(2)}, u32[]{:S(2)}) collective-permute-start(bf16[16,1024]{1,0:T(8,128)(2,1)S(1)} %get-tuple-element.58), channel_id=1, source_target_pairs={{0,16},{4,20},{8,24},{12,28},{16,0},{20,4},{24,8},{28,12},{1,17},{... | collective-permute-start | bytes 98312 | tf_op jit(solution)/shard_map/ppermute | solution.py:320
  83.3 5.1 %collective-permute-start.14 = (bf16[16,1024]{1,0:T(8,128)(2,1)S(1)}, bf16[16,1024]{1,0:T(8,128)(2,1)S(1)}, u32[]{:S(2)}, u32[]{:S(2)}) collective-permute-start(bf16[16,1024]{1,0:T(8,128)(2,1)S(1)} %get-tuple-element.57), channel_id=1, source_target_pairs={{0,20},{4,24},{8,28},{12,0},{16,4},{20,8},{24,12},{28,16},{1,21},{... | collective-permute-start | bytes 98312 | tf_op jit(solution)/shard_map/ppermute | solution.py:320
  85.4 3.1 %collective-permute-start.15 = (bf16[16,1024]{1,0:T(8,128)(2,1)S(1)}, bf16[16,1024]{1,0:T(8,128)(2,1)S(1)}, u32[]{:S(2)}, u32[]{:S(2)}) collective-permute-start(bf16[16,1024]{1,0:T(8,128)(2,1)S(1)} %get-tuple-element.56), channel_id=1, source_target_pairs={{0,24},{4,28},{8,0},{12,4},{16,8},{20,12},{24,16},{28,20},{1,25},{... | collective-permute-start | bytes 98312 | tf_op jit(solution)/shard_map/ppermute | solution.py:320
  85.5 4.3 %collective-permute-start.16 = (bf16[16,1024]{1,0:T(8,128)(2,1)S(1)}, bf16[16,1024]{1,0:T(8,128)(2,1)S(1)}, u32[]{:S(2)}, u32[]{:S(2)}) collective-permute-start(bf16[16,1024]{1,0:T(8,128)(2,1)S(1)} %get-tuple-element.55), channel_id=1, source_target_pairs={{0,28},{4,0},{8,4},{12,8},{16,12},{20,16},{24,20},{28,24},{1,29},{... | collective-permute-start | bytes 98312 | tf_op jit(solution)/shard_map/ppermute | solution.py:320
  98.5 9.5 %collective-permute-start.17 = (bf16[8,72,256]{2,1,0:T(8,128)(2,1)S(1)}, bf16[8,72,256]{2,1,0:T(8,128)(2,1)S(1)}, u32[]{:S(2)}, u32[]{:S(2)}) collective-permute-start(bf16[8,72,256]{2,1,0:T(8,128)(2,1)S(1)} %get-tuple-element.52), channel_id=1, source_target_pairs={{0,8},{8,16},{16,24},{24,0},{1,9},{9,17},{17,25},{25,1},{2,10},{10... | collective-permute-start | bytes 884744 | tf_op jit(solution)/shard_map/ppermute | solution.py:311
  99.2 15.3 %collective-permute-start.18 = (bf16[8,72,256]{2,1,0:T(8,128)(2,1)S(1)}, bf16[8,72,256]{2,1,0:T(8,128)(2,1)S(1)}, u32[]{:S(2)}, u32[]{:S(2)}) collective-permute-start(bf16[8,72,256]{2,1,0:T(8,128)(2,1)S(1)} %get-tuple-element.54), channel_id=1, source_target_pairs={{0,16},{8,24},{16,0},{24,8},{1,17},{9,25},{17,1},{25,9},{2,18},{10... | collective-permute-start | bytes 884744 | tf_op jit(solution)/shard_map/ppermute | solution.py:311
  101.4 13.2 %collective-permute-start.19 = (bf16[8,72,256]{2,1,0:T(8,128)(2,1)S(1)}, bf16[8,72,256]{2,1,0:T(8,128)(2,1)S(1)}, u32[]{:S(2)}, u32[]{:S(2)}) collective-permute-start(bf16[8,72,256]{2,1,0:T(8,128)(2,1)S(1)} %get-tuple-element.53), channel_id=1, source_target_pairs={{0,24},{8,0},{16,8},{24,16},{1,25},{9,1},{17,9},{25,17},{2,26},{10... | collective-permute-start | bytes 884744 | tf_op jit(solution)/shard_map/ppermute | solution.py:311
  115.5 20.8 %all-to-all-start.3 = ((bf16[8,72,256]{2,1,0:T(8,128)(2,1)}), bf16[8,72,256]{2,1,0:T(8,128)(2,1)S(1)}, u32[]{:S(2)}, u32[]{:S(2)}) async-start(bf16[8,72,256]{2,1,0:T(8,128)(2,1)} %fusion.2), calls=%async_computation.3 | async-start | bytes 589824 | tf_op jit(solution)/shard_map/all_to_all | solution.py:370
  136.4 3.9 %collective-permute-start.20 = (f32[36,256]{1,0:T(8,128)S(1)}, f32[36,256]{1,0:T(8,128)S(1)}, u32[]{:S(2)}, u32[]{:S(2)}) collective-permute-start(f32[36,256]{1,0:T(8,128)S(1)} %get-tuple-element.64), channel_id=1, source_target_pairs={{0,4},{4,0},{1,5},{5,1},{2,6},{6,2},{3,7},{7,3},{8,12},{12,8},{9,1... | collective-permute-start | bytes 110600 | tf_op jit(solution)/shard_map/ppermute | solution.py:311
  (7 other events, 8.8 us)

commit v5 on v4

--- a/solution.py
+++ b/solution.py
@@ -266,7 +266,7 @@
                         spread(26), spread(22), spread(24), spread(20), spread(24), spread(22),
                         plain(22), plain(18), plain(20), plain(16),
                         pltpu.VMEM((192, C), f32), pltpu.VMEM((8, 320, C), bf16), pltpu.SemaphoreType.DMA((16,))],
-        compiler_params=pltpu.CompilerParams(vmem_limit_bytes=56 * 1024 * 1024),
+        compiler_params=pltpu.CompilerParams(vmem_limit_bytes=44 * 1024 * 1024),
         cost_estimate=pl.CostEstimate(flops=flops, bytes_accessed=16 * 1024 * 1024, transcendentals=0),
         name="blocks",
     )(*fields, *kernels)

time: 142 us -> 139 us (0.979)
  starting transfers between devices: 48.1 us -> 45.6 us
  Pallas kernels: 22.9 us -> 20.7 us
  waiting for transfers between devices: 59.9 us -> 61.8 us
  local copies, waits for them, and re-layouts: 7.53 us -> 9 us
    pallas_call x1, Pallas kernels: 18.3 us -> 16.3 us  [blocks(): pl.pallas_call(blocks_kernel, out_shape=[jax.ShapeDtypeStruct((8, 16, 4 *...]
    unnamed x29 -> x15, local copies, waits for them, and re-layouts: 5.89 us -> 7.34 us
  transfers between devices with their start and end apart: 25 -> 25, of which waited for: 14 -> 13; matrix products, arithmetic and copies ran while one was open for 2% -> 1% of each run, Pallas kernels for 1% -> 1%
where the time goes in v5:
time: 139 us
  waiting for transfers between devices  61.8 us (44%)
  starting transfers between devices  45.6 us (33%)
  Pallas kernels  20.7 us (15%)
  local copies, waits for them, and re-layouts  9 us (6%)
    ppermute x10, waiting for transfers between devices, turn(): lax.ppermute(value, axis, [(i, (i + by) % size) for i in range(size)])  18.3 us
    pallas_call x1, Pallas kernels, blocks(): pl.pallas_call(blocks_kernel, out_shape=[jax.ShapeDtypeStruct((8, 16, 4 *...  16.3 us
    ppermute x2, waiting for transfers between devices, apart(): return lax.ppermute(value, ('z', 'core'), pairs)  13 us
    ppermute x10, starting transfers between devices, turn(): lax.ppermute(value, axis, [(i, (i + by) % size) for i in range(size)])  12.6 us
    all_to_all x1, waiting for transfers between devices, local(): grad = lax.all_to_all(grad, 'z', 0, 0).astype(f32).sum(axis=0)  10.6 us
    all_to_all x1, waiting for transfers between devices, local(): tile = lax.all_to_all(pieces, ('y', 'core'), 0, 0)  9.66 us
    all_to_all x1, starting transfers between devices, local(): grad = lax.all_to_all(grad, 'z', 0, 0).astype(f32).sum(axis=0)  9.36 us
    ppermute x7, starting transfers between devices, around(): lax.ppermute(value, ('y', 'core'), [(i, (i + by) % 8) for i in range(8)])  7.53 us
  transfers between devices with their start and end apart: 25, of which 13 were waited for; matrix products, arithmetic and copies ran while one was open for 1% of the time, Pallas kernels for 1%

profile of v5, /device:TPU:1, one launch (start us, length us, event | category | flops | bytes accessed | tf_op | source)
XLA Modules:
  0.0 138.7 jit_solution(15149354009150233014)
XLA Ops:
  0.6 1.7 %copy-done = bf16[1,2,2304,256]{3,2,1,0:T(8,128)(2,1)S(1)} copy-done((bf16[1,2,2304,256]{3,2,1,0:T(8,128)(2,1)S(1)}, bf16[1,2,2304,256]{3,2,1,0:T(8,128)(2,1)}, u32[]{:S(2)}) %copy-start) | copy-done | bytes 2359320
  2.3 0.9 copy-done.3
  5.9 3.6 %collective-permute-start = (bf16[576,256]{1,0:T(8,128)(2,1)}, bf16[576,256]{1,0:T(8,128)(2,1)S(1)}, u32[]{:S(2)}, u32[]{:S(2)}) collective-permute-start(bf16[576,256]{1,0:T(8,128)(2,1)} %get-tuple-element.26), channel_id=1, source_target_pairs={{0,2},{1,3},{2,0},{3,1},{4,6},{5,7},{6,4},{7,5},{8,10},{9,11},{10,... | collective-permute-start | bytes 884744 | tf_op jit(solution)/shard_map/ppermute | solution.py:311
  9.4 5.4 %all-to-all-start = ((bf16[8,208,256]{2,1,0:T(8,128)(2,1)}), bf16[8,208,256]{2,1,0:T(8,128)(2,1)S(1)}, u32[]{:S(2)}, u32[]{:S(2)}) async-start(bf16[8,208,256]{2,1,0:T(8,128)(2,1)} %copy-done.2), calls=%async_computation | async-start | bytes 1703936 | tf_op jit(solution)/shard_map/all_to_all | solution.py:351
  14.9 1.6 %slice_bitcast_fusion = (bf16[2304,256]{1,0:T(8,128)(2,1)}, bf16[2304,256]{1,0:T(8,128)(2,1)}) fusion(bf16[1,2,2304,256]{3,2,1,0:T(8,128)(2,1)S(1)} %copy-done.1), kind=kLoop, calls=%fused_computation | loop fusion | bytes 4718592 | tf_op jit(solution)/shard_map/squeeze | solution.py:347
  17.1 1.1 repeat.1
  18.2 9.7 %all-to-all-done.tile = bf16[8,208,256]{2,1,0:T(8,128)(2,1)S(1)} async-done(((bf16[8,208,256]{2,1,0:T(8,128)(2,1)}), bf16[8,208,256]{2,1,0:T(8,128)(2,1)S(1)}, u32[]{:S(2)}, u32[]{:S(2)}) %all-to-all-start) | async-done | bytes 852000 | tf_op jit(solution)/shard_map/all_to_all | solution.py:351
  27.8 3.5 %all-to-all-start.1 = ((bf16[4,576,256]{2,1,0:T(8,128)(2,1)}), bf16[4,576,256]{2,1,0:T(8,128)(2,1)S(1)}, u32[]{:S(2)}, u32[]{:S(2)}) async-start(bf16[4,576,256]{2,1,0:T(8,128)(2,1)} %repeat.1), calls=%async_computation.1 | async-start | bytes 2359296 | tf_op jit(solution)/shard_map/all_to_all | solution.py:356
  31.4 1.3 collective-permute-start.1
  32.7 1.3 collective-permute-start.2
  34.0 13.0 %collective-permute-done.2.far = bf16[64,256]{1,0:T(8,128)(2,1)S(1)} collective-permute-done((bf16[64,256]{1,0:T(8,128)(2,1)S(1)}, bf16[64,256]{1,0:T(8,128)(2,1)S(1)}, u32[]{:S(2)}, u32[]{:S(2)}) %collective-permute-start.2) | collective-permute-done | bytes 32800 | tf_op jit(solution)/shard_map/ppermute | solution.py:316
  47.0 1.8 %collective-permute-start.7 = (bf16[2304,256]{1,0:T(8,128)(2,1)S(1)}, bf16[2304,256]{1,0:T(8,128)(2,1)S(1)}, u32[]{:S(2)}, u32[]{:S(2)}) collective-permute-start(bf16[2304,256]{1,0:T(8,128)(2,1)S(1)} %collective-permute-done.3.first), channel_id=1, source_target_pairs={{0,4},{4,0},{1,5},{5,1},{2,6},{6,2},{3,7},{7,3},{8,12},{12,8},{9,1... | collective-permute-start | bytes 3538952 | tf_op jit(solution)/shard_map/ppermute | solution.py:311
  48.8 1.0 copy-done.5
  50.9 3.9 %collective-permute-done.6.far2 = bf16[64,256]{1,0:T(8,128)(2,1)S(1)} collective-permute-done((bf16[64,256]{1,0:T(8,128)(2,1)S(1)}, bf16[64,256]{1,0:T(8,128)(2,1)S(1)}, u32[]{:S(2)}, u32[]{:S(2)}) %collective-permute-start.6) | collective-permute-done | bytes 32800 | tf_op jit(solution)/shard_map/ppermute | solution.py:311
  54.7 1.4 collective-permute-done.5.beyond2
  56.2 1.3 copy-done.6
  57.4 16.3 %blocks.1 = (bf16[8,16,1024]{2,1,0:T(8,128)(2,1)S(1)}, bf16[8,320,256]{2,1,0:T(8,128)(2,1)}) custom-call(bf16[8,208,256]{2,1,0:T(8,128)(2,1)S(1)} %all-to-all-done.tile, bf16[8,208,256]{2,1,0:T(8,128)(2,1)} %collective-permute-done.1.beyond, bf16[8,208,256]{2,1,0:T(8,128)(2,1)S(1)} %collective-permute-done.5.beyond2, ...), custom_call_target="tpu_custom_call" | custom-call | flops 9059696640 | bytes 16777216 | tf_op jit(solution)/shard_map/blocks/pallas_call | solution.py:260
  73.7 3.9 %all-to-all-start.2 = ((bf16[8,320,256]{2,1,0:T(8,128)(2,1)}), bf16[8,320,256]{2,1,0:T(8,128)(2,1)S(1)}, u32[]{:S(2)}, u32[]{:S(2)}) async-start(bf16[8,320,256]{2,1,0:T(8,128)(2,1)} %get-tuple-element.34), calls=%async_computation.2 | async-start | bytes 2621440 | tf_op jit(solution)/shard_map/all_to_all | solution.py:364
  78.4 1.9 %collective-permute-start.12 = (bf16[16,1024]{1,0:T(8,128)(2,1)S(1)}, bf16[16,1024]{1,0:T(8,128)(2,1)S(1)}, u32[]{:S(2)}, u32[]{:S(2)}) collective-permute-start(bf16[16,1024]{1,0:T(8,128)(2,1)S(1)} %get-tuple-element.59), channel_id=1, source_target_pairs={{0,12},{4,16},{8,20},{12,24},{16,28},{20,0},{24,4},{28,8},{1,13},{... | collective-permute-start | bytes 98312 | tf_op jit(solution)/shard_map/ppermute | solution.py:320
  80.3 1.2 collective-permute-start.13
  81.5 2.5 %collective-permute-start.14 = (bf16[16,1024]{1,0:T(8,128)(2,1)S(1)}, bf16[16,1024]{1,0:T(8,128)(2,1)S(1)}, u32[]{:S(2)}, u32[]{:S(2)}) collective-permute-start(bf16[16,1024]{1,0:T(8,128)(2,1)S(1)} %get-tuple-element.57), channel_id=1, source_target_pairs={{0,20},{4,24},{8,28},{12,0},{16,4},{20,8},{24,12},{28,16},{1,21},{... | collective-permute-start | bytes 98312 | tf_op jit(solution)/shard_map/ppermute | solution.py:320
  84.1 1.0 collective-permute-start.16
  85.1 1.5 %collective-permute-done.14.refs_5_ = bf16[16,1024]{1,0:T(8,128)(2,1)S(1)} collective-permute-done((bf16[16,1024]{1,0:T(8,128)(2,1)S(1)}, bf16[16,1024]{1,0:T(8,128)(2,1)S(1)}, u32[]{:S(2)}, u32[]{:S(2)}) %collective-permute-start.14) | collective-permute-done | bytes 32800 | tf_op jit(solution)/shard_map/ppermute | solution.py:320
  87.8 7.5 %all-to-all-done.2.acts = bf16[8,320,256]{2,1,0:T(8,128)(2,1)S(1)} async-done(((bf16[8,320,256]{2,1,0:T(8,128)(2,1)}), bf16[8,320,256]{2,1,0:T(8,128)(2,1)S(1)}, u32[]{:S(2)}, u32[]{:S(2)}) %all-to-all-start.2) | async-done | bytes 1310752 | tf_op jit(solution)/shard_map/all_to_all | solution.py:364
  95.4 1.7 %kernel_grads.1 = bf16[4,8,72,256]{3,2,1,0:T(8,128)(2,1)S(1)} custom-call(bf16[8,320,256]{2,1,0:T(8,128)(2,1)S(1)} %all-to-all-done.2.acts), custom_call_target="tpu_custom_call" | custom-call | flops 1207959552 | bytes 8388608 | tf_op jit(solution)/shard_map/kernel_grads/pallas_call | solution.py:297
  97.5 1.8 %collective-permute-start.18 = (bf16[8,72,256]{2,1,0:T(8,128)(2,1)S(1)}, bf16[8,72,256]{2,1,0:T(8,128)(2,1)S(1)}, u32[]{:S(2)}, u32[]{:S(2)}) collective-permute-start(bf16[8,72,256]{2,1,0:T(8,128)(2,1)S(1)} %get-tuple-element.54), channel_id=1, source_target_pairs={{0,16},{8,24},{16,0},{24,8},{1,17},{9,25},{17,1},{25,9},{2,18},{10... | collective-permute-start | bytes 884744 | tf_op jit(solution)/shard_map/ppermute | solution.py:311
  99.3 1.1 collective-permute-start.19
  100.4 6.8 %collective-permute-done.17 = bf16[8,72,256]{2,1,0:T(8,128)(2,1)S(1)} collective-permute-done((bf16[8,72,256]{2,1,0:T(8,128)(2,1)S(1)}, bf16[8,72,256]{2,1,0:T(8,128)(2,1)S(1)}, u32[]{:S(2)}, u32[]{:S(2)}) %collective-permute-start.17) | collective-permute-done | bytes 294944 | tf_op jit(solution)/shard_map/ppermute | solution.py:311
  107.3 5.1 %collective-permute-done.18 = bf16[8,72,256]{2,1,0:T(8,128)(2,1)S(1)} collective-permute-done((bf16[8,72,256]{2,1,0:T(8,128)(2,1)S(1)}, bf16[8,72,256]{2,1,0:T(8,128)(2,1)S(1)}, u32[]{:S(2)}, u32[]{:S(2)}) %collective-permute-start.18) | collective-permute-done | bytes 294944 | tf_op jit(solution)/shard_map/ppermute | solution.py:311
  114.1 9.4 %all-to-all-start.3 = ((bf16[8,72,256]{2,1,0:T(8,128)(2,1)}), bf16[8,72,256]{2,1,0:T(8,128)(2,1)S(1)}, u32[]{:S(2)}, u32[]{:S(2)}) async-start(bf16[8,72,256]{2,1,0:T(8,128)(2,1)} %fusion.2), calls=%async_computation.3 | async-start | bytes 589824 | tf_op jit(solution)/shard_map/all_to_all | solution.py:370
  123.5 10.6 %all-to-all-done.3 = bf16[8,72,256]{2,1,0:T(8,128)(2,1)S(1)} async-done(((bf16[8,72,256]{2,1,0:T(8,128)(2,1)}), bf16[8,72,256]{2,1,0:T(8,128)(2,1)S(1)}, u32[]{:S(2)}, u32[]{:S(2)}) %all-to-all-start.3) | async-done | bytes 294944 | tf_op jit(solution)/shard_map/all_to_all | solution.py:370
  134.2 3.0 %collective-permute-start.20 = (f32[36,256]{1,0:T(8,128)S(1)}, f32[36,256]{1,0:T(8,128)S(1)}, u32[]{:S(2)}, u32[]{:S(2)}) collective-permute-start(f32[36,256]{1,0:T(8,128)S(1)} %get-tuple-element.64), channel_id=1, source_target_pairs={{0,4},{4,0},{1,5},{5,1},{2,6},{6,2},{3,7},{7,3},{8,12},{12,8},{9,1... | collective-permute-start | bytes 110600 | tf_op jit(solution)/shard_map/ppermute | solution.py:311
  (46 shorter events, 10.1 us)
Async XLA Ops:
  0.6 1.7 %copy-start = (bf16[1,2,2304,256]{3,2,1,0:T(8,128)(2,1)S(1)}, bf16[1,2,2304,256]{3,2,1,0:T(8,128)(2,1)}, u32[]{:S(2)}) copy-start(bf16[1,2,2304,256]{3,2,1,0:T(8,128)(2,1)} %param.5) | copy-start | bytes 7077892
  2.3 0.9 copy-start.3
  3.2 0.9 copy-start.4
  4.1 10.8 %copy-start.1 = (bf16[1,2,2304,256]{3,2,1,0:T(8,128)(2,1)S(1)}, bf16[1,2,2304,256]{3,2,1,0:T(8,128)(2,1)}, u32[]{:S(2)}) copy-start(bf16[1,2,2304,256]{3,2,1,0:T(8,128)(2,1)} %param.5) | copy-start | bytes 7077892
  5.0 0.9 copy-start.2
  5.9 11.2 %collective-permute-start = (bf16[576,256]{1,0:T(8,128)(2,1)}, bf16[576,256]{1,0:T(8,128)(2,1)S(1)}, u32[]{:S(2)}, u32[]{:S(2)}) collective-permute-start(bf16[576,256]{1,0:T(8,128)(2,1)} %get-tuple-element.26), channel_id=1, source_target_pairs={{0,2},{1,3},{2,0},{3,1},{4,6},{5,7},{6,4},{7,5},{8,10},{9,11},{10,... | collective-permute-start | bytes 884744 | tf_op jit(solution)/shard_map/ppermute | solution.py:311
  9.4 18.4 %all-to-all-start = ((bf16[8,208,256]{2,1,0:T(8,128)(2,1)}), bf16[8,208,256]{2,1,0:T(8,128)(2,1)S(1)}, u32[]{:S(2)}, u32[]{:S(2)}) async-start(bf16[8,208,256]{2,1,0:T(8,128)(2,1)} %copy-done.2), calls=%async_computation | async-start | bytes 1703936 | tf_op jit(solution)/shard_map/all_to_all | solution.py:351
  16.4 30.6 %collective-permute-start.3 = (bf16[2304,256]{1,0:T(8,128)(2,1)}, bf16[2304,256]{1,0:T(8,128)(2,1)S(1)}, u32[]{:S(2)}, u32[]{:S(2)}) collective-permute-start(bf16[2304,256]{1,0:T(8,128)(2,1)} %get-tuple-element.51), channel_id=1, source_target_pairs={{0,3},{1,0},{2,1},{3,2},{4,5},{5,6},{6,7},{7,4},{8,11},{9,8},{10,9... | collective-permute-start | bytes 3538952 | tf_op jit(solution)/shard_map/ppermute | solution.py:347
  16.7 30.3 %collective-permute-start.4 = (bf16[2304,256]{1,0:T(8,128)(2,1)}, bf16[2304,256]{1,0:T(8,128)(2,1)}, u32[]{:S(2)}, u32[]{:S(2)}) collective-permute-start(bf16[2304,256]{1,0:T(8,128)(2,1)} %get-tuple-element.50), channel_id=1, source_target_pairs={{0,3},{1,0},{2,1},{3,2},{4,5},{5,6},{6,7},{7,4},{8,11},{9,8},{10,9... | collective-permute-start | bytes 3538952 | tf_op jit(solution)/shard_map/ppermute | solution.py:347
  27.8 19.2 %all-to-all-start.1 = ((bf16[4,576,256]{2,1,0:T(8,128)(2,1)}), bf16[4,576,256]{2,1,0:T(8,128)(2,1)S(1)}, u32[]{:S(2)}, u32[]{:S(2)}) async-start(bf16[4,576,256]{2,1,0:T(8,128)(2,1)} %repeat.1), calls=%async_computation.1 | async-start | bytes 2359296 | tf_op jit(solution)/shard_map/all_to_all | solution.py:356
  31.4 15.6 %collective-permute-start.1 = (bf16[8,208,256]{2,1,0:T(8,128)(2,1)S(1)}, bf16[8,208,256]{2,1,0:T(8,128)(2,1)}, u32[]{:S(2)}, u32[]{:S(2)}) collective-permute-start(bf16[8,208,256]{2,1,0:T(8,128)(2,1)S(1)} %all-to-all-done.tile), channel_id=1, source_target_pairs={{0,32},{32,64},{64,96},{96,128},{128,160},{160,192},{192,224},{36,... | collective-permute-start | bytes 2555912 | tf_op jit(solution)/shard_map/ppermute | solution.py:316
  32.7 14.3 %collective-permute-start.2 = (bf16[64,256]{1,0:T(8,128)(2,1)S(1)}, bf16[64,256]{1,0:T(8,128)(2,1)S(1)}, u32[]{:S(2)}, u32[]{:S(2)}) collective-permute-start(bf16[64,256]{1,0:T(8,128)(2,1)S(1)} %select_bitcast_fusion), channel_id=1, source_target_pairs={{0,64},{32,96},{64,128},{96,160},{128,192},{160,224},{68,4},{100,3... | collective-permute-start | bytes 98312 | tf_op jit(solution)/shard_map/ppermute | solution.py:316
  47.0 9.1 %collective-permute-start.7 = (bf16[2304,256]{1,0:T(8,128)(2,1)S(1)}, bf16[2304,256]{1,0:T(8,128)(2,1)S(1)}, u32[]{:S(2)}, u32[]{:S(2)}) collective-permute-start(bf16[2304,256]{1,0:T(8,128)(2,1)S(1)} %collective-permute-done.3.first), channel_id=1, source_target_pairs={{0,4},{4,0},{1,5},{5,1},{2,6},{6,2},{3,7},{7,3},{8,12},{12,8},{9,1... | collective-permute-start | bytes 3538952 | tf_op jit(solution)/shard_map/ppermute | solution.py:311
  48.8 1.0 copy-start.5
  49.8 6.3 %collective-permute-start.8 = (bf16[2304,256]{1,0:T(8,128)(2,1)}, bf16[2304,256]{1,0:T(8,128)(2,1)S(1)}, u32[]{:S(2)}, u32[]{:S(2)}) collective-permute-start(bf16[2304,256]{1,0:T(8,128)(2,1)} %collective-permute-done.4.second), channel_id=1, source_target_pairs={{0,4},{4,0},{1,5},{5,1},{2,6},{6,2},{3,7},{7,3},{8,12},{12,8},{9,1... | collective-permute-start | bytes 3538952 | tf_op jit(solution)/shard_map/ppermute | solution.py:311
  49.9 6.3 %collective-permute-start.9 = (bf16[4,576,256]{2,1,0:T(8,128)(2,1)S(1)}, bf16[4,576,256]{2,1,0:T(8,128)(2,1)S(1)}, u32[]{:S(2)}, u32[]{:S(2)}) collective-permute-start(bf16[4,576,256]{2,1,0:T(8,128)(2,1)S(1)} %all-to-all-done.1.quarters), channel_id=1, source_target_pairs={{0,4},{4,0},{1,5},{5,1},{2,6},{6,2},{3,7},{7,3},{8,12},{12,8},{9,1... | collective-permute-start | bytes 3538952 | tf_op jit(solution)/shard_map/ppermute | solution.py:311
  50.4 5.8 %collective-permute-start.5 = (bf16[8,208,256]{2,1,0:T(8,128)(2,1)}, bf16[8,208,256]{2,1,0:T(8,128)(2,1)S(1)}, u32[]{:S(2)}, u32[]{:S(2)}) collective-permute-start(bf16[8,208,256]{2,1,0:T(8,128)(2,1)} %collective-permute-done.1.beyond), channel_id=1, source_target_pairs={{0,4},{4,0},{1,5},{5,1},{2,6},{6,2},{3,7},{7,3},{8,12},{12,8},{9,1... | collective-permute-start | bytes 2555912 | tf_op jit(solution)/shard_map/ppermute | solution.py:311
  50.4 4.4 %collective-permute-start.6 = (bf16[64,256]{1,0:T(8,128)(2,1)S(1)}, bf16[64,256]{1,0:T(8,128)(2,1)S(1)}, u32[]{:S(2)}, u32[]{:S(2)}) collective-permute-start(bf16[64,256]{1,0:T(8,128)(2,1)S(1)} %collective-permute-done.2.far), channel_id=1, source_target_pairs={{0,4},{4,0},{1,5},{5,1},{2,6},{6,2},{3,7},{7,3},{8,12},{12,8},{9,1... | collective-permute-start | bytes 98312 | tf_op jit(solution)/shard_map/ppermute | solution.py:311
  56.1 1.3 copy-start.6
  73.7 21.7 %all-to-all-start.2 = ((bf16[8,320,256]{2,1,0:T(8,128)(2,1)}), bf16[8,320,256]{2,1,0:T(8,128)(2,1)S(1)}, u32[]{:S(2)}, u32[]{:S(2)}) async-start(bf16[8,320,256]{2,1,0:T(8,128)(2,1)} %get-tuple-element.34), calls=%async_computation.2 | async-start | bytes 2621440 | tf_op jit(solution)/shard_map/all_to_all | solution.py:364
  77.6 6.5 %collective-permute-start.10 = (bf16[16,1024]{1,0:T(8,128)(2,1)S(1)}, bf16[16,1024]{1,0:T(8,128)(2,1)S(1)}, u32[]{:S(2)}, u32[]{:S(2)}) collective-permute-start(bf16[16,1024]{1,0:T(8,128)(2,1)S(1)} %get-tuple-element.61), channel_id=1, source_target_pairs={{0,4},{4,8},{8,12},{12,16},{16,20},{20,24},{24,28},{28,0},{1,5},{5... | collective-permute-start | bytes 98312 | tf_op jit(solution)/shard_map/ppermute | solution.py:320
  77.9 6.2 %collective-permute-start.11 = (bf16[16,1024]{1,0:T(8,128)(2,1)S(1)}, bf16[16,1024]{1,0:T(8,128)(2,1)S(1)}, u32[]{:S(2)}, u32[]{:S(2)}) collective-permute-start(bf16[16,1024]{1,0:T(8,128)(2,1)S(1)} %get-tuple-element.60), channel_id=1, source_target_pairs={{0,8},{4,12},{8,16},{12,20},{16,24},{20,28},{24,0},{28,4},{1,9},{5... | collective-permute-start | bytes 98312 | tf_op jit(solution)/shard_map/ppermute | solution.py:320
  78.4 6.7 %collective-permute-start.12 = (bf16[16,1024]{1,0:T(8,128)(2,1)S(1)}, bf16[16,1024]{1,0:T(8,128)(2,1)S(1)}, u32[]{:S(2)}, u32[]{:S(2)}) collective-permute-start(bf16[16,1024]{1,0:T(8,128)(2,1)S(1)} %get-tuple-element.59), channel_id=1, source_target_pairs={{0,12},{4,16},{8,20},{12,24},{16,28},{20,0},{24,4},{28,8},{1,13},{... | collective-permute-start | bytes 98312 | tf_op jit(solution)/shard_map/ppermute | solution.py:320
  80.3 4.8 %collective-permute-start.13 = (bf16[16,1024]{1,0:T(8,128)(2,1)S(1)}, bf16[16,1024]{1,0:T(8,128)(2,1)S(1)}, u32[]{:S(2)}, u32[]{:S(2)}) collective-permute-start(bf16[16,1024]{1,0:T(8,128)(2,1)S(1)} %get-tuple-element.58), channel_id=1, source_target_pairs={{0,16},{4,20},{8,24},{12,28},{16,0},{20,4},{24,8},{28,12},{1,17},{... | collective-permute-start | bytes 98312 | tf_op jit(solution)/shard_map/ppermute | solution.py:320
  81.5 5.1 %collective-permute-start.14 = (bf16[16,1024]{1,0:T(8,128)(2,1)S(1)}, bf16[16,1024]{1,0:T(8,128)(2,1)S(1)}, u32[]{:S(2)}, u32[]{:S(2)}) collective-permute-start(bf16[16,1024]{1,0:T(8,128)(2,1)S(1)} %get-tuple-element.57), channel_id=1, source_target_pairs={{0,20},{4,24},{8,28},{12,0},{16,4},{20,8},{24,12},{28,16},{1,21},{... | collective-permute-start | bytes 98312 | tf_op jit(solution)/shard_map/ppermute | solution.py:320
  84.1 3.3 %collective-permute-start.15 = (bf16[16,1024]{1,0:T(8,128)(2,1)S(1)}, bf16[16,1024]{1,0:T(8,128)(2,1)S(1)}, u32[]{:S(2)}, u32[]{:S(2)}) collective-permute-start(bf16[16,1024]{1,0:T(8,128)(2,1)S(1)} %get-tuple-element.56), channel_id=1, source_target_pairs={{0,24},{4,28},{8,0},{12,4},{16,8},{20,12},{24,16},{28,20},{1,25},{... | collective-permute-start | bytes 98312 | tf_op jit(solution)/shard_map/ppermute | solution.py:320
  84.1 3.8 %collective-permute-start.16 = (bf16[16,1024]{1,0:T(8,128)(2,1)S(1)}, bf16[16,1024]{1,0:T(8,128)(2,1)S(1)}, u32[]{:S(2)}, u32[]{:S(2)}) collective-permute-start(bf16[16,1024]{1,0:T(8,128)(2,1)S(1)} %get-tuple-element.55), channel_id=1, source_target_pairs={{0,28},{4,0},{8,4},{12,8},{16,12},{20,16},{24,20},{28,24},{1,29},{... | collective-permute-start | bytes 98312 | tf_op jit(solution)/shard_map/ppermute | solution.py:320
  97.1 10.1 %collective-permute-start.17 = (bf16[8,72,256]{2,1,0:T(8,128)(2,1)S(1)}, bf16[8,72,256]{2,1,0:T(8,128)(2,1)S(1)}, u32[]{:S(2)}, u32[]{:S(2)}) collective-permute-start(bf16[8,72,256]{2,1,0:T(8,128)(2,1)S(1)} %get-tuple-element.52), channel_id=1, source_target_pairs={{0,8},{8,16},{16,24},{24,0},{1,9},{9,17},{17,25},{25,1},{2,10},{10... | collective-permute-start | bytes 884744 | tf_op jit(solution)/shard_map/ppermute | solution.py:311
  97.5 14.9 %collective-permute-start.18 = (bf16[8,72,256]{2,1,0:T(8,128)(2,1)S(1)}, bf16[8,72,256]{2,1,0:T(8,128)(2,1)S(1)}, u32[]{:S(2)}, u32[]{:S(2)}) collective-permute-start(bf16[8,72,256]{2,1,0:T(8,128)(2,1)S(1)} %get-tuple-element.54), channel_id=1, source_target_pairs={{0,16},{8,24},{16,0},{24,8},{1,17},{9,25},{17,1},{25,9},{2,18},{10... | collective-permute-start | bytes 884744 | tf_op jit(solution)/shard_map/ppermute | solution.py:311
  99.3 14.0 %collective-permute-start.19 = (bf16[8,72,256]{2,1,0:T(8,128)(2,1)S(1)}, bf16[8,72,256]{2,1,0:T(8,128)(2,1)S(1)}, u32[]{:S(2)}, u32[]{:S(2)}) collective-permute-start(bf16[8,72,256]{2,1,0:T(8,128)(2,1)S(1)} %get-tuple-element.53), channel_id=1, source_target_pairs={{0,24},{8,0},{16,8},{24,16},{1,25},{9,1},{17,9},{25,17},{2,26},{10... | collective-permute-start | bytes 884744 | tf_op jit(solution)/shard_map/ppermute | solution.py:311
  114.1 20.0 %all-to-all-start.3 = ((bf16[8,72,256]{2,1,0:T(8,128)(2,1)}), bf16[8,72,256]{2,1,0:T(8,128)(2,1)S(1)}, u32[]{:S(2)}, u32[]{:S(2)}) async-start(bf16[8,72,256]{2,1,0:T(8,128)(2,1)} %fusion.2), calls=%async_computation.3 | async-start | bytes 589824 | tf_op jit(solution)/shard_map/all_to_all | solution.py:370
  134.2 3.9 %collective-permute-start.20 = (f32[36,256]{1,0:T(8,128)S(1)}, f32[36,256]{1,0:T(8,128)S(1)}, u32[]{:S(2)}, u32[]{:S(2)}) collective-permute-start(f32[36,256]{1,0:T(8,128)S(1)} %get-tuple-element.64), channel_id=1, source_target_pairs={{0,4},{4,0},{1,5},{5,1},{2,6},{6,2},{3,7},{7,3},{8,12},{12,8},{9,1... | collective-permute-start | bytes 110600 | tf_op jit(solution)/shard_map/ppermute | solution.py:311
